TPU v7x, 128 devices: a whole 4x4x4 slice. The times are simulated.
128 devices in a mesh: row: 8 (over x, z_hi), col: 16 (over y, z_lo, core).
Axes of the slice: x: 4, y: 4, z: 4 (z_hi: 2, z_lo: 2; z = z_hi * 2 + z_lo), core: 2. Of those that a mesh axis runs over, the one named last changes fastest.
Arguments:
- amplitude: float32 [32, 80, 5, 640], P('col', 'row'), may hold values from -6 to 6
- coupling: float32 [80, 5, 32, 640], P('row', None, 'col'), may hold values from -0.3125 to 0.3125
Outputs:
- cycle_term: float32 [32, 640, 32, 640], P('row', None, 'col')
All inputs are finite; a program needn't handle non-finite values.
Results may differ from a plain program's by a relative error of at most 0.00005.
Values sent between devices are 32-bit elements; how exact they have to be, the bound alone decides.
No kernel may reach another device: no remote copies, remote signals or barrier semaphores. Data moves between devices by JAX's collectives and lax.ppermute only.
A program may use at most 128 MiB of HBM per device.

v0:
```python
import jax
import jax.numpy as jnp
from jax import lax
from jax.sharding import PartitionSpec as P


def shards(amplitude, coupling):
    all_rows = lax.all_gather(amplitude, "row", axis=1, tiled=True)
    whole_pairs = lax.all_gather(amplitude, "col", axis=0, tiled=True)
    panel = lax.all_to_all(whole_pairs, "row", split_axis=0, concat_axis=1, tiled=True)
    coupling_panel = lax.all_gather(coupling, "row", axis=0, tiled=True)
    widened = lax.all_gather(coupling, "col", axis=2, tiled=True)
    complete = lax.all_to_all(widened, "row", split_axis=2, concat_axis=0, tiled=True)
    own_rows = panel.shape[0]
    own_cols = all_rows.shape[0]
    summed = panel.shape[1] * panel.shape[2]
    width = panel.shape[3]
    panel_flat = jnp.transpose(panel.reshape(own_rows, summed, width), (1, 0, 2)).reshape(
        summed, own_rows * width
    )
    complete_flat = complete.reshape(summed, own_rows * width)
    coupling_flat = coupling_panel.reshape(summed, own_cols * width)
    rows_flat = jnp.transpose(all_rows.reshape(own_cols, summed, width), (1, 0, 2)).reshape(
        summed, own_cols * width
    )
    left = jnp.concatenate([panel_flat, complete_flat], axis=0)
    right = jnp.concatenate([coupling_flat, rows_flat], axis=0)
    result = lax.dot_general(
        left,
        right,
        (((0,), (0,)), ((), ())),
        precision=lax.Precision.HIGHEST,
        preferred_element_type=jnp.float32,
    )
    return result.reshape(own_rows, width, own_cols, width)


def solution(mesh):
    placed = (P("col", "row", None, None), P("row", None, "col", None))
    return jax.shard_map(
        shards, mesh=mesh, in_specs=placed, out_specs=P("row", None, "col", None), check_vma=False
    )
```

profile of v0, /device:TPU:1, one launch (start us, length us, event | category | flops | bytes accessed | tf_op | source)
XLA Modules:
  0.0 413.0 jit_solution(7713517459673010701)
XLA Ops:
  6.5 0.0 all-gather.5.cloned.1.call-start
  6.5 1.8 copy.5
  8.3 0.0 all-gather.5.cloned.1.call-update
  8.3 0.0 all-gather.7.cloned.1.call-start
  8.4 1.8 copy.7
  10.1 0.0 all-gather.7.cloned.1.call-update
  10.2 0.0 all-gather.11.cloned.1.call-start
  10.2 0.7 all-gather.11.cloned.1.call-update
  10.9 45.4 %all-gather.5.cloned.1.call-done = f32[32,10,5,640]{3,2,1,0:T(8,128)} async-done(((f32[2,10,5,640]{3,2,1,0:T(8,128)}), f32[32,10,5,640]{3,2,1,0:T(8,128)}) %all-gather.5.cloned.1.call-update) | async-done | bytes 4096016 | tf_op jit(solution)/shard_map/all_gather | solution.py:9
  56.2 6.4 %all-to-all-start = ((f32[32,10,5,640]{3,2,1,0:T(8,128)}), f32[32,10,5,640]{3,2,1,0:T(8,128)}, u32[]{:S(2)}, u32[]{:S(2)}) async-start(f32[32,10,5,640]{3,2,1,0:T(8,128)} %all-gather.5.cloned.1.call-done), calls=%async_computation | async-start | bytes 13107200 | tf_op jit(solution)/shard_map/all_to_all | solution.py:10
  62.7 0.0 all-gather.9.cloned.1.call-start
  62.7 0.5 all-gather.9.cloned.1.call-update
  63.2 104.1 %all-gather.7.cloned.1.call-done = f32[10,5,32,640]{3,1,0,2:T(8,128)} async-done(((f32[10,5,2,640]{3,1,0,2:T(8,128)}), f32[10,5,32,640]{3,1,0,2:T(8,128)}) %all-gather.7.cloned.1.call-update) | async-done | bytes 4096016 | tf_op jit(solution)/shard_map/all_gather | solution.py:12
  167.3 0.0 all-to-all-done
  167.3 7.2 %all-to-all-start.1 = ((f32[10,5,32,640]{3,1,0,2:T(8,128)}), f32[10,5,32,640]{3,1,0,2:T(8,128)}, u32[]{:S(2)}, u32[]{:S(2)}) async-start(f32[10,5,32,640]{3,1,0,2:T(8,128)} %all-gather.7.cloned.1.call-done), calls=%async_computation.1 | async-start | bytes 13107200 | tf_op jit(solution)/shard_map/all_to_all | solution.py:13
  174.6 100.0 %all-gather.11.cloned.1.call-done = f32[2,80,5,640]{3,0,2,1:T(2,128)} async-done(((f32[2,10,5,640]{3,0,2,1:T(2,128)}), f32[2,80,5,640]{3,0,2,1:T(2,128)}) %all-gather.11.cloned.1.call-update) | async-done | bytes 2048016 | tf_op jit(solution)/shard_map/all_gather | solution.py:8
  274.5 1.7 copy.12
  276.3 52.0 %all-gather.9.cloned.1.call-done = f32[80,5,2,640]{3,2,1,0:T(2,128)} async-done(((f32[10,5,2,640]{3,2,1,0:T(2,128)}), f32[80,5,2,640]{3,2,1,0:T(2,128)}) %all-gather.9.cloned.1.call-update) | async-done | bytes 2048016 | tf_op jit(solution)/shard_map/all_gather | solution.py:11
  328.2 3.0 copy.11
  331.3 4.4 %copy.6 = f32[8,4,10,5,640]{4,1,3,2,0:T(4,128)S(1)} copy(f32[8,4,10,5,640]{4,3,2,1,0:T(8,128)} %bitcast) | data formatting | bytes 8192000 | tf_op jit(solution)/shard_map/all_to_all | solution.py:10
  335.7 2.2 copy.9
  338.0 0.0 all-to-all-done.1
  338.0 4.4 %copy.8 = f32[10,5,8,4,640]{4,3,1,0,2:T(4,128)S(1)} copy(f32[10,5,8,4,640]{4,1,0,3,2:T(8,128)} %bitcast.4) | data formatting | bytes 8192000 | tf_op jit(solution)/shard_map/all_to_all | solution.py:13
  342.4 0.0 copy-start
  342.4 0.0 copy-start.1
  342.4 0.3 copy.10
  342.7 1.9 copy-done
  344.6 0.7 copy-done.1
  345.2 45.0 %fusion = f32[2560,1280]{1,0:T(8,128)} fusion(f32[400,2560]{1,0:T(8,128)S(1)} %bitcast.24, f32[400,2560]{1,0:T(8,128)S(1)} %bitcast.23, f32[400,1280]{1,0:T(8,128)S(1)} %bitcast.27, f32[400,1280]{1,0:T(8,128)S(1)} %bitcast.28), kind=kOutput, calls=%fused_computation | convolution fusion | flops 31460352000 | bytes 25395200 | tf_op jit(solution)/shard_map/dot_general | solution.py:28
  390.2 16.3 %reshape.29 = f32[4,640,2,640]{3,2,1,0:T(2,128)} reshape(f32[2560,1280]{1,0:T(8,128)} %fusion) | data formatting | bytes 26214400 | tf_op jit(solution)/shard_map/reshape | solution.py:35
Async XLA Ops:
  6.5 49.7 %all-gather.5.cloned.1.call-start = ((), (), s32[]{:S(2)}) async-start(), calls=%async_computation.2 | async-start | bytes 6963200 | tf_op jit(solution)/shard_map/all_gather | solution.py:9
  8.3 159.0 %all-gather.7.cloned.1.call-start = ((), (), s32[]{:S(2)}) async-start(), calls=%async_computation.3 | async-start | bytes 6963200 | tf_op jit(solution)/shard_map/all_gather | solution.py:12
  10.2 264.4 %all-gather.11.cloned.1.call-start = ((), (), s32[]{:S(2)}) async-start(), calls=%async_computation.5 | async-start | bytes 2304000 | tf_op jit(solution)/shard_map/all_gather | solution.py:8
  56.2 111.1 %all-to-all-start = ((f32[32,10,5,640]{3,2,1,0:T(8,128)}), f32[32,10,5,640]{3,2,1,0:T(8,128)}, u32[]{:S(2)}, u32[]{:S(2)}) async-start(f32[32,10,5,640]{3,2,1,0:T(8,128)} %all-gather.5.cloned.1.call-done), calls=%async_computation | async-start | bytes 13107200 | tf_op jit(solution)/shard_map/all_to_all | solution.py:10
  62.7 265.6 %all-gather.9.cloned.1.call-start = ((), (), s32[]{:S(2)}) async-start(), calls=%async_computation.4 | async-start | bytes 2304000 | tf_op jit(solution)/shard_map/all_gather | solution.py:11
  167.3 170.6 %all-to-all-start.1 = ((f32[10,5,32,640]{3,1,0,2:T(8,128)}), f32[10,5,32,640]{3,1,0,2:T(8,128)}, u32[]{:S(2)}, u32[]{:S(2)}) async-start(f32[10,5,32,640]{3,1,0,2:T(8,128)} %all-gather.7.cloned.1.call-done), calls=%async_computation.1 | async-start | bytes 13107200 | tf_op jit(solution)/shard_map/all_to_all | solution.py:13
  342.4 2.2 copy-start
  342.4 2.8 copy-start.1
Sparse Core Ops, SparseCore 0:
  9.1 47.1 all-gather.4
  57.9 109.3 all-gather.6
  169.6 104.9 all-gather.10
  276.7 51.5 all-gather.8
where the time goes:
time: 414 us; the launch traced here: 413 us
  waiting for transfers between devices  303 us (73%)
  matrix products  45 us (11%)
  local copies, waits for them, and re-layouts  38.5 us (9%)
  starting transfers between devices  13.8 us (3%)
  between operations  13.2 us (3%)
    all_gather x1, waiting for transfers between devices, shards(): widened = lax.all_gather(coupling, 'col', axis=2, tiled=True)  104 us
    all_gather x1, waiting for transfers between devices, shards(): all_rows = lax.all_gather(amplitude, 'row', axis=1, tiled=True)  100 us
    all_gather x1, waiting for transfers between devices, shards(): coupling_panel = lax.all_gather(coupling, 'row', axis=0, tiled=True)  52 us
    all_gather x1, waiting for transfers between devices, shards(): whole_pairs = lax.all_gather(amplitude, 'col', axis=0, tiled=True)  45.4 us
    dot_general x1, matrix products, shards(): lax.dot_general(left, right, (((0,), (0,)), ((), ())), precision=lax.Prec...  45 us
    reshape x1, local copies, waits for them, and re-layouts, shards(): return result.reshape(own_rows, width, own_cols, width)  16.3 us
    unnamed x10, local copies, waits for them, and re-layouts  13.3 us
  transfers between devices with their start and end apart: 6, of which 4 were waited for; matrix products, arithmetic and copies ran while one was open for 3% of the time, Pallas kernels for 0%

commit v1 on v0

v1 whole, which is shorter than its diff:
```python
import functools

import jax
import jax.numpy as jnp
from jax import lax
from jax.experimental import pallas as pl
from jax.experimental.pallas import tpu as pltpu
from jax.sharding import PartitionSpec as P

AXES = ("row", "col")
BLOCK = 100
PARTS = 8
DEPTH = 800
MAIN = 768
REST = DEPTH - MAIN
WIDTH = 640
LANES = 128
CUTS = WIDTH // LANES


def flat(x, z, y, low, core):
    return ((x % 4) * 2 + z % 2) * 16 + ((y % 4) * 2 + low % 2) * 2 + core % 2


def permute(value, move):
    pairs = []
    for x in range(4):
        for z in range(2):
            for y in range(4):
                for low in range(2):
                    for core in range(2):
                        pairs.append((flat(x, z, y, low, core), flat(*move(x, z, y, low, core))))
    return lax.ppermute(value, AXES, pairs)


def split(value):
    high = value.astype(jnp.bfloat16)
    return high, (value - high.astype(jnp.float32)).astype(jnp.bfloat16)


def contract(*refs):
    js, own, other = refs[:8], refs[8:16], refs[16:24]
    out = refs[24]
    right, left, rh, rl, rr, lh, ll, lr, stage, sems, osems = refs[25:]
    row, col = lax.axis_index("row"), lax.axis_index("col")
    x, z = row // 2, row % 2
    y, low, core = col // 4, (col // 2) % 2, col % 2

    def place(a, b):
        return (((a + 8) % 4) * 2 + (b + 2) % 2) * BLOCK

    def slots(a, b):
        return [place(a, b), place(a, b + 1), place(a - 1, b), place(a + 1, b),
                place(a - 1, b + 1), place(a + 1, b + 1), place(a + 2, b), place(a + 2, b + 1)]

    def load(ref, cut, target, sem):
        return pltpu.make_async_copy(ref.at[:, :, pl.ds(cut * LANES, LANES)], target, sem)

    copies = []
    for cut in range(CUTS):
        for n, (ref, at) in enumerate(zip(js, slots(x, z))):
            copies.append(load(ref, cut, right.at[cut, pl.ds(at, BLOCK)], sems.at[cut, n]))
        for n, (ref, at) in enumerate(zip(own, slots(y, low))):
            copies.append(load(ref, cut, left.at[core, cut, pl.ds(at, BLOCK)], sems.at[cut, 8 + n]))
        for n, (ref, at) in enumerate(zip(other, slots(y, low))):
            copies.append(load(ref, cut, left.at[1 - core, cut, pl.ds(at, BLOCK)], sems.at[cut, 16 + n]))
    for copy in copies:
        copy.start()
    for copy in copies:
        copy.wait()

    right = right.reshape(CUTS, 2 * DEPTH, LANES)
    left = left.reshape(2, CUTS, 2 * DEPTH, LANES)
    flat_stage = stage.reshape(2, CUTS, 2 * WIDTH, LANES)

    for cut in range(CUTS):
        for j in range(2):
            cols = pl.ds((cut * 2 + j) * LANES, LANES)
            for k in range(0, MAIN, LANES):
                high, rest = split(right[cut, pl.ds(k * 2 + j, LANES, stride=2), :])
                rh[pl.ds(k, LANES), cols] = high
                rl[pl.ds(k, LANES), cols] = rest
            high, rest = split(right[cut, pl.ds(MAIN * 2 + j, REST, stride=2), :])
            rr[pl.ds(0, REST), cols] = high
            rr[pl.ds(REST, REST), cols] = rest
            rr[pl.ds(2 * REST, REST), cols] = high
            rr[pl.ds(3 * REST, REST), cols] = jnp.zeros_like(high)

    def turn(i, cut):
        half, j = i // 2, i % 2
        rows = pl.ds(pl.multiple_of(cut * LANES, LANES), LANES)
        for k in range(0, MAIN, LANES):
            high, rest = split(left[half, cut, pl.ds(k * 2 + j, LANES, stride=2), :].T)
            lh[rows, pl.ds(k, LANES)] = high
            ll[rows, pl.ds(k, LANES)] = rest
        value = left[half, cut, pl.ds(MAIN * 2 + j, REST, stride=2), :]
        high = value.astype(jnp.bfloat16).astype(jnp.float32)
        stack = jnp.concatenate([high, high, value - high, jnp.zeros_like(value)], axis=0)
        lr[rows, :] = stack.T.astype(jnp.bfloat16)

    def dot(a, b):
        return jnp.dot(a, b, preferred_element_type=jnp.float32)

    def flush(i, slot, cut):
        return pltpu.make_async_copy(
            stage.at[slot, cut], out.at[i, :, :, pl.ds(cut * LANES, LANES)], osems.at[slot, cut]
        )

    def one(i, carry):
        slot = i % 2

        def turn_one(cut, c):
            turn(i, cut)
            return c

        lax.fori_loop(0, CUTS, turn_one, 0)

        @pl.when(i >= 2)
        def _():
            for cut in range(CUTS):
                flush(i - 2, slot, cut).wait()

        def columns(cut, c):
            cols = pl.ds(pl.multiple_of(cut * 256, 256), 256)
            acc = dot(lh[...], rh[:, cols])
            acc += dot(lh[...], rl[:, cols])
            acc += dot(ll[...], rh[:, cols])
            acc += dot(lr[...], rr[:, cols])
            flat_stage[slot, cut, pl.ds(0, WIDTH, stride=2), :] = acc[:, :LANES]
            flat_stage[slot, cut, pl.ds(1, WIDTH, stride=2), :] = acc[:, LANES:]
            return c

        lax.fori_loop(0, CUTS, columns, 0)
        for cut in range(CUTS):
            flush(i, slot, cut).start()
        return carry

    lax.fori_loop(0, 4, one, 0)
    for i in (2, 3):
        for cut in range(CUTS):
            flush(i, i % 2, cut).wait()


def multiply(pieces):
    flops = 2 * 2560 * 1280 * 2400
    return pl.pallas_call(
        contract,
        out_shape=jax.ShapeDtypeStruct((4, WIDTH, 2, WIDTH), jnp.float32),
        in_specs=[pl.BlockSpec(memory_space=pl.ANY)] * 24,
        out_specs=pl.BlockSpec(memory_space=pl.ANY),
        scratch_shapes=[
            pltpu.VMEM((CUTS, DEPTH, 2, LANES), jnp.float32),
            pltpu.VMEM((2, CUTS, DEPTH, 2, LANES), jnp.float32),
            pltpu.VMEM((MAIN, 1280), jnp.bfloat16),
            pltpu.VMEM((MAIN, 1280), jnp.bfloat16),
            pltpu.VMEM((LANES, 1280), jnp.bfloat16),
            pltpu.VMEM((WIDTH, MAIN), jnp.bfloat16),
            pltpu.VMEM((WIDTH, MAIN), jnp.bfloat16),
            pltpu.VMEM((WIDTH, LANES), jnp.bfloat16),
            pltpu.VMEM((2, CUTS, WIDTH, 2, LANES), jnp.float32),
            pltpu.SemaphoreType.DMA((CUTS, 24)),
            pltpu.SemaphoreType.DMA((2, CUTS)),
        ],
        compiler_params=pltpu.CompilerParams(vmem_limit_bytes=56 * 1024 * 1024),
        cost_estimate=pl.CostEstimate(flops=flops, bytes_accessed=26 * 10**6, transcendentals=0),
    )(*pieces)


def shards(amplitude, coupling):
    a = jnp.transpose(amplitude, (1, 2, 0, 3))
    lefts = jnp.concatenate([a, coupling], axis=0).reshape(BLOCK, 2, WIDTH)
    rights = jnp.concatenate([coupling, a], axis=0).reshape(BLOCK, 2, WIDTH)

    def gather(first, second, up, down):
        a = permute(first, up)
        b = permute(first, down)
        c = permute(second, up)
        d = permute(second, down)
        e = permute(a, up)
        f = permute(d, down)
        return [first, second, a, b, c, d, e, f]

    turned = permute(lefts, lambda x, z, y, low, core: (y, low, x, z, core))
    far = permute(rights, lambda x, z, y, low, core: (x, z + 1, y, low, core))
    js = gather(rights, far,
                lambda x, z, y, low, core: (x + 1, z, y, low, core),
                lambda x, z, y, low, core: (x - 1, z, y, low, core))
    near = permute(turned, lambda x, z, y, low, core: (x, z, y, low + 1, core))
    own = gather(turned, near,
                 lambda x, z, y, low, core: (x, z, y + 1, low, core),
                 lambda x, z, y, low, core: (x, z, y - 1, low, core))
    other = [permute(v, lambda x, z, y, low, core: (x, z, y, low, core + 1)) for v in own]
    return multiply(js + own + other)


def solution(mesh):
    placed = (P("col", "row", None, None), P("row", None, "col", None))
    return jax.shard_map(
        shards, mesh=mesh, in_specs=placed, out_specs=P("row", None, "col", None), check_vma=False
    )
```

time: 414 us -> 125 us (0.30)
  waiting for transfers between devices: 303 us -> 35.7 us
  matrix products: 45 us -> 0 us
  starting transfers between devices: 13.8 us -> 53.5 us
  local copies, waits for them, and re-layouts: 38.5 us -> 0.87 us
  Pallas kernels: 0 us -> 32.5 us
  between operations: 13.2 us -> 0.25 us
    all_gather x4 -> x0, waiting for transfers between devices: 301 us -> none  [the longest x1 104 us: shards(): widened = lax.all_gather(coupling, 'col', axis=2, tiled=True)]
    ppermute x0 -> x23, starting transfers between devices: none -> 53.5 us  [permute(): return lax.ppermute(value, AXES, pairs)]
    dot_general x1 -> x0, matrix products: 45 us -> none  [shards(): lax.dot_general(left, right, (((0,), (0,)), ((), ())), precision=lax.Prec...]
    ppermute x0 -> x23, waiting for transfers between devices: none -> 35.7 us  [permute(): return lax.ppermute(value, AXES, pairs)]
    pallas_call x0 -> x1, Pallas kernels: none -> 32.5 us  [multiply(): pl.pallas_call(contract, out_shape=jax.ShapeDtypeStruct((4, WIDTH, 2, WID...]
    reshape x1 -> x0, local copies, waits for them, and re-layouts: 16.3 us -> none  [shards(): return result.reshape(own_rows, width, own_cols, width)]
    all_to_all x2 -> x0, starting transfers between devices: 13.7 us -> none  [the longest x1 7.25 us: shards(): lax.all_to_all(widened, 'row', split_axis=2, concat_axis=0, tiled=True)]
    unnamed x10 -> x46, local copies, waits for them, and re-layouts: 13.3 us -> 0.87 us
  transfers between devices with their start and end apart: 6 -> 23, of which waited for: 4 -> 9; matrix products, arithmetic and copies ran while one was open for 3% -> 0% of each run, Pallas kernels for 0% -> 0%
where the time goes in v1:
time: 125 us
  starting transfers between devices  53.5 us (43%)
  waiting for transfers between devices  35.7 us (29%)
  Pallas kernels  32.5 us (26%)
  other arithmetic  1.77 us (1%)
    ppermute x23, starting transfers between devices, permute(): return lax.ppermute(value, AXES, pairs)  53.5 us
    ppermute x23, waiting for transfers between devices, permute(): return lax.ppermute(value, AXES, pairs)  35.7 us
    pallas_call x1, Pallas kernels, multiply(): pl.pallas_call(contract, out_shape=jax.ShapeDtypeStruct((4, WIDTH, 2, WID...  32.5 us
  transfers between devices with their start and end apart: 23, of which 9 were waited for; matrix products, arithmetic and copies ran while one was open for 0% of the time, Pallas kernels for 0%

profile of v1, /device:TPU:1, one launch (start us, length us, event | category | flops | bytes accessed | tf_op | source)
XLA Modules:
  0.0 124.7 jit_solution(4518505693534214820)
XLA Ops:
  0.0 1.8 %pad_maximum_fusion.1 = (f32[20,5,2,640]{3,2,1,0:T(2,128)S(1)}, f32[20,5,2,640]{3,2,1,0:T(2,128)S(1)}) fusion(f32[10,5,2,640]{3,2,1,0:T(2,128)} %param.3, f32[10,5,2,640]{3,2,1,0:T(2,128)} %bitcast.8), kind=kLoop, calls=%fused_computation.1 | loop fusion | flops 256000 | bytes 1536000 | tf_op jit(solution)/shard_map/concatenate | solution.py:171
  1.8 0.0 copy-start
  1.8 0.7 collective-permute-start.7
  2.5 7.2 %collective-permute-start.2 = (f32[100,2,640]{2,1,0:T(2,128)S(1)}, f32[100,2,640]{2,1,0:T(2,128)S(1)}, u32[]{:S(2)}, u32[]{:S(2)}) collective-permute-start(f32[100,2,640]{2,1,0:T(2,128)S(1)} %bitcast.3), channel_id=1, source_target_pairs={{0,96},{1,97},{2,98},{3,99},{4,100},{5,101},{6,102},{7,103},{8,104... | collective-permute-start | bytes 1536008 | tf_op jit(solution)/shard_map/ppermute | solution.py:33
  9.7 0.0 collective-permute-start.1
  9.7 3.1 %collective-permute-start = (f32[100,2,640]{2,1,0:T(2,128)S(1)}, f32[100,2,640]{2,1,0:T(2,128)S(1)}, u32[]{:S(2)}, u32[]{:S(2)}) collective-permute-start(f32[100,2,640]{2,1,0:T(2,128)S(1)} %bitcast.5), channel_id=1, source_target_pairs={{0,16},{1,17},{2,18},{3,19},{4,20},{5,21},{6,22},{7,23},{8,24},{9,... | collective-permute-start | bytes 1536008 | tf_op jit(solution)/shard_map/ppermute | solution.py:33
  12.9 0.0 collective-permute-done.7.refs_8_
  12.9 1.5 %collective-permute-start.15 = (f32[100,2,640]{2,1,0:T(2,128)S(1)}, f32[100,2,640]{2,1,0:T(2,128)S(1)}, u32[]{:S(2)}, u32[]{:S(2)}) collective-permute-start(f32[100,2,640]{2,1,0:T(2,128)S(1)} %collective-permute-done.7.refs_8_), channel_id=1, source_target_pairs={{0,1},{1,0},{2,3},{3,2},{4,5},{5,4},{6,7},{7,6},{8,9},{9,8},{10,11... | collective-permute-start | bytes 1536008 | tf_op jit(solution)/shard_map/ppermute | solution.py:33
  14.4 21.8 %collective-permute-start.10 = (f32[100,2,640]{2,1,0:T(2,128)S(1)}, f32[100,2,640]{2,1,0:T(2,128)S(1)}, u32[]{:S(2)}, u32[]{:S(2)}) collective-permute-start(f32[100,2,640]{2,1,0:T(2,128)S(1)} %collective-permute-done.7.refs_8_), channel_id=1, source_target_pairs={{0,12},{1,13},{2,14},{3,15},{4,0},{5,1},{6,2},{7,3},{8,4},{9,5},{1... | collective-permute-start | bytes 1536008 | tf_op jit(solution)/shard_map/ppermute | solution.py:33
  36.2 2.4 %collective-permute-done.2.refs_3_ = f32[100,2,640]{2,1,0:T(2,128)S(1)} collective-permute-done((f32[100,2,640]{2,1,0:T(2,128)S(1)}, f32[100,2,640]{2,1,0:T(2,128)S(1)}, u32[]{:S(2)}, u32[]{:S(2)}) %collective-permute-start.2) | collective-permute-done | bytes 512032 | tf_op jit(solution)/shard_map/ppermute | solution.py:33
  38.6 0.0 collective-permute-start.9
  38.6 4.6 %collective-permute-done.1.refs_2_ = f32[100,2,640]{2,1,0:T(2,128)S(1)} collective-permute-done((f32[100,2,640]{2,1,0:T(2,128)S(1)}, f32[100,2,640]{2,1,0:T(2,128)S(1)}, u32[]{:S(2)}, u32[]{:S(2)}) %collective-permute-start.1) | collective-permute-done | bytes 512032 | tf_op jit(solution)/shard_map/ppermute | solution.py:33
  43.2 3.0 %collective-permute-start.8 = (f32[100,2,640]{2,1,0:T(2,128)S(1)}, f32[100,2,640]{2,1,0:T(2,128)S(1)}, u32[]{:S(2)}, u32[]{:S(2)}) collective-permute-start(f32[100,2,640]{2,1,0:T(2,128)S(1)} %collective-permute-done.7.refs_8_), channel_id=1, source_target_pairs={{0,2},{1,3},{2,0},{3,1},{4,6},{5,7},{6,4},{7,5},{8,10},{9,11},{10,... | collective-permute-start | bytes 1536008 | tf_op jit(solution)/shard_map/ppermute | solution.py:33
  46.2 0.0 collective-permute-done.refs_1_
  46.2 0.0 collective-permute-start.5
  46.2 0.0 collective-permute-done.15.refs_16_
  46.3 2.7 %collective-permute-start.4 = (f32[100,2,640]{2,1,0:T(2,128)S(1)}, f32[100,2,640]{2,1,0:T(2,128)S(1)}, u32[]{:S(2)}, u32[]{:S(2)}) collective-permute-start(f32[100,2,640]{2,1,0:T(2,128)S(1)} %collective-permute-done.refs_1_), channel_id=1, source_target_pairs={{0,96},{1,97},{2,98},{3,99},{4,100},{5,101},{6,102},{7,103},{8,104... | collective-permute-start | bytes 1536008 | tf_op jit(solution)/shard_map/ppermute | solution.py:33
  48.9 0.0 collective-permute-done.10.refs_11_
  48.9 0.0 collective-permute-start.3
  48.9 3.1 %collective-permute-done.9.refs_10_ = f32[100,2,640]{2,1,0:T(2,128)S(1)} collective-permute-done((f32[100,2,640]{2,1,0:T(2,128)S(1)}, f32[100,2,640]{2,1,0:T(2,128)S(1)}, u32[]{:S(2)}, u32[]{:S(2)}) %collective-permute-start.9) | collective-permute-done | bytes 512032 | tf_op jit(solution)/shard_map/ppermute | solution.py:33
  52.1 2.2 %collective-permute-start.18 = (f32[100,2,640]{2,1,0:T(2,128)S(1)}, f32[100,2,640]{2,1,0:T(2,128)S(1)}, u32[]{:S(2)}, u32[]{:S(2)}) collective-permute-start(f32[100,2,640]{2,1,0:T(2,128)S(1)} %collective-permute-done.10.refs_11_), channel_id=1, source_target_pairs={{0,1},{1,0},{2,3},{3,2},{4,5},{5,4},{6,7},{7,6},{8,9},{9,8},{10,11... | collective-permute-start | bytes 1536008 | tf_op jit(solution)/shard_map/ppermute | solution.py:33
  54.3 3.0 %collective-permute-done.8.refs_9_ = f32[100,2,640]{2,1,0:T(2,128)S(1)} collective-permute-done((f32[100,2,640]{2,1,0:T(2,128)S(1)}, f32[100,2,640]{2,1,0:T(2,128)S(1)}, u32[]{:S(2)}, u32[]{:S(2)}) %collective-permute-start.8) | collective-permute-done | bytes 512032 | tf_op jit(solution)/shard_map/ppermute | solution.py:33
  57.3 0.0 collective-permute-start.12
  57.3 2.1 %collective-permute-done.5.refs_6_ = f32[100,2,640]{2,1,0:T(2,128)S(1)} collective-permute-done((f32[100,2,640]{2,1,0:T(2,128)S(1)}, f32[100,2,640]{2,1,0:T(2,128)S(1)}, u32[]{:S(2)}, u32[]{:S(2)}) %collective-permute-start.5) | collective-permute-done | bytes 512032 | tf_op jit(solution)/shard_map/ppermute | solution.py:33
  59.3 4.0 %collective-permute-start.17 = (f32[100,2,640]{2,1,0:T(2,128)S(1)}, f32[100,2,640]{2,1,0:T(2,128)S(1)}, u32[]{:S(2)}, u32[]{:S(2)}) collective-permute-start(f32[100,2,640]{2,1,0:T(2,128)S(1)} %collective-permute-done.9.refs_10_), channel_id=1, source_target_pairs={{0,1},{1,0},{2,3},{3,2},{4,5},{5,4},{6,7},{7,6},{8,9},{9,8},{10,11... | collective-permute-start | bytes 1536008 | tf_op jit(solution)/shard_map/ppermute | solution.py:33
  63.3 0.0 collective-permute-done.4.refs_5_
  63.3 0.0 collective-permute-start.13
  63.3 7.0 %collective-permute-done.3.refs_4_ = f32[100,2,640]{2,1,0:T(2,128)S(1)} collective-permute-done((f32[100,2,640]{2,1,0:T(2,128)S(1)}, f32[100,2,640]{2,1,0:T(2,128)S(1)}, u32[]{:S(2)}, u32[]{:S(2)}) %collective-permute-start.3) | collective-permute-done | bytes 512032 | tf_op jit(solution)/shard_map/ppermute | solution.py:33
  70.3 2.2 %collective-permute-start.16 = (f32[100,2,640]{2,1,0:T(2,128)S(1)}, f32[100,2,640]{2,1,0:T(2,128)S(1)}, u32[]{:S(2)}, u32[]{:S(2)}) collective-permute-start(f32[100,2,640]{2,1,0:T(2,128)S(1)} %collective-permute-done.8.refs_9_), channel_id=1, source_target_pairs={{0,1},{1,0},{2,3},{3,2},{4,5},{5,4},{6,7},{7,6},{8,9},{9,8},{10,11... | collective-permute-start | bytes 1536008 | tf_op jit(solution)/shard_map/ppermute | solution.py:33
  72.5 0.0 collective-permute-done.18.refs_19_
  72.5 0.0 collective-permute-start.11
  72.5 0.0 collective-permute-done.12.refs_13_
  72.5 2.7 %collective-permute-start.14 = (f32[100,2,640]{2,1,0:T(2,128)S(1)}, f32[100,2,640]{2,1,0:T(2,128)S(1)}, u32[]{:S(2)}, u32[]{:S(2)}) collective-permute-start(f32[100,2,640]{2,1,0:T(2,128)S(1)} %collective-permute-done.12.refs_13_), channel_id=1, source_target_pairs={{0,12},{1,13},{2,14},{3,15},{4,0},{5,1},{6,2},{7,3},{8,4},{9,5},{1... | collective-permute-start | bytes 1536008 | tf_op jit(solution)/shard_map/ppermute | solution.py:33
  75.2 0.0 collective-permute-done.17.refs_18_
  75.2 0.0 collective-permute-start.6
  75.2 2.5 %collective-permute-done.13.refs_14_ = f32[100,2,640]{2,1,0:T(2,128)S(1)} collective-permute-done((f32[100,2,640]{2,1,0:T(2,128)S(1)}, f32[100,2,640]{2,1,0:T(2,128)S(1)}, u32[]{:S(2)}, u32[]{:S(2)}) %collective-permute-start.13) | collective-permute-done | bytes 512032 | tf_op jit(solution)/shard_map/ppermute | solution.py:33
  77.8 1.3 %collective-permute-start.20 = (f32[100,2,640]{2,1,0:T(2,128)S(1)}, f32[100,2,640]{2,1,0:T(2,128)S(1)}, u32[]{:S(2)}, u32[]{:S(2)}) collective-permute-start(f32[100,2,640]{2,1,0:T(2,128)S(1)} %collective-permute-done.12.refs_13_), channel_id=1, source_target_pairs={{0,1},{1,0},{2,3},{3,2},{4,5},{5,4},{6,7},{7,6},{8,9},{9,8},{10,11... | collective-permute-start | bytes 1536008 | tf_op jit(solution)/shard_map/ppermute | solution.py:33
  79.1 0.0 collective-permute-done.16.refs_17_
  79.1 0.1 collective-permute-start.21
  79.2 9.5 %collective-permute-done.11.refs_12_ = f32[100,2,640]{2,1,0:T(2,128)S(1)} collective-permute-done((f32[100,2,640]{2,1,0:T(2,128)S(1)}, f32[100,2,640]{2,1,0:T(2,128)S(1)}, u32[]{:S(2)}, u32[]{:S(2)}) %collective-permute-start.11) | collective-permute-done | bytes 512032 | tf_op jit(solution)/shard_map/ppermute | solution.py:33
  88.7 0.9 collective-permute-start.19
  89.6 0.0 collective-permute-done.14.refs_15_
  89.6 0.1 collective-permute-start.22
  89.7 0.0 collective-permute-done.6.refs_7_
  89.7 0.0 collective-permute-done.21.refs_22_
  89.7 0.0 collective-permute-done.20.refs_21_
  89.7 1.4 %collective-permute-done.19.refs_20_ = f32[100,2,640]{2,1,0:T(2,128)S(1)} collective-permute-done((f32[100,2,640]{2,1,0:T(2,128)S(1)}, f32[100,2,640]{2,1,0:T(2,128)S(1)}, u32[]{:S(2)}, u32[]{:S(2)}) %collective-permute-start.19) | collective-permute-done | bytes 512032 | tf_op jit(solution)/shard_map/ppermute | solution.py:33
  91.1 0.0 copy-done.19
  91.2 0.8 copy-done.22
  91.9 0.0 collective-permute-done.22.refs_23_
  92.0 0.0 copy-done
  92.0 0.0 copy-done.4
  92.0 0.0 copy-done.5
  92.0 0.0 copy-done.6
  92.0 0.0 copy-done.7
  92.0 0.0 copy-done.8
  92.0 0.0 copy-done.9
  92.1 0.0 copy-done.10
  92.1 0.0 copy-done.11
  92.1 0.0 copy-done.12
  92.1 0.0 copy-done.13
  92.1 0.0 copy-done.14
  92.1 0.0 copy-done.15
  92.1 32.5 %shard_map.28 = f32[4,640,2,640]{3,2,1,0:T(2,128)} custom-call(f32[100,2,640]{2,1,0:T(2,128)} %bitcast.6, f32[100,2,640]{2,1,0:T(2,128)} %copy-done.4, f32[100,2,640]{2,1,0:T(2,128)} %copy-done.3, f32[100,2,640]{2,1,0:T(2,128)} %copy-done.2, f32[100,2,640]{2,1,0:T(2,128)} %copy-done.11, f32[100,2,640]{2,1,0:T(2,128)} %copy-done.10, ...), custom_call_target="tpu_custom_call" | custom-call | flops 15728640000 | bytes 26000000 | tf_op jit(solution)/shard_map/pallas_call | solution.py:146
  (30 shorter events, 0.1 us)
Async XLA Ops:
  1.8 90.2 %copy-start = (f32[20,5,2,640]{3,2,1,0:T(2,128)}, f32[20,5,2,640]{3,2,1,0:T(2,128)S(1)}, u32[]{:S(2)}) copy-start(f32[20,5,2,640]{3,2,1,0:T(2,128)S(1)} %get-tuple-element.6) | copy-start | bytes 1536004
  1.8 11.1 %collective-permute-start.7 = (f32[100,2,640]{2,1,0:T(2,128)S(1)}, f32[100,2,640]{2,1,0:T(2,128)S(1)}, u32[]{:S(2)}, u32[]{:S(2)}) collective-permute-start(f32[100,2,640]{2,1,0:T(2,128)S(1)} %bitcast.7), channel_id=1, source_target_pairs={{0,0},{1,1},{2,16},{3,17},{4,32},{5,33},{6,48},{7,49},{8,64},{9,65... | collective-permute-start | bytes 1536008 | tf_op jit(solution)/shard_map/ppermute | solution.py:33
  2.5 36.1 %collective-permute-start.2 = (f32[100,2,640]{2,1,0:T(2,128)S(1)}, f32[100,2,640]{2,1,0:T(2,128)S(1)}, u32[]{:S(2)}, u32[]{:S(2)}) collective-permute-start(f32[100,2,640]{2,1,0:T(2,128)S(1)} %bitcast.3), channel_id=1, source_target_pairs={{0,96},{1,97},{2,98},{3,99},{4,100},{5,101},{6,102},{7,103},{8,104... | collective-permute-start | bytes 1536008 | tf_op jit(solution)/shard_map/ppermute | solution.py:33
  9.7 33.5 %collective-permute-start.1 = (f32[100,2,640]{2,1,0:T(2,128)S(1)}, f32[100,2,640]{2,1,0:T(2,128)S(1)}, u32[]{:S(2)}, u32[]{:S(2)}) collective-permute-start(f32[100,2,640]{2,1,0:T(2,128)S(1)} %bitcast.4), channel_id=1, source_target_pairs={{0,32},{1,33},{2,34},{3,35},{4,36},{5,37},{6,38},{7,39},{8,40},{9,... | collective-permute-start | bytes 1536008 | tf_op jit(solution)/shard_map/ppermute | solution.py:33
  9.7 36.5 %collective-permute-start = (f32[100,2,640]{2,1,0:T(2,128)S(1)}, f32[100,2,640]{2,1,0:T(2,128)S(1)}, u32[]{:S(2)}, u32[]{:S(2)}) collective-permute-start(f32[100,2,640]{2,1,0:T(2,128)S(1)} %bitcast.5), channel_id=1, source_target_pairs={{0,16},{1,17},{2,18},{3,19},{4,20},{5,21},{6,22},{7,23},{8,24},{9,... | collective-permute-start | bytes 1536008 | tf_op jit(solution)/shard_map/ppermute | solution.py:33
  12.9 79.1 %copy-start.1 = (f32[100,2,640]{2,1,0:T(2,128)}, f32[100,2,640]{2,1,0:T(2,128)S(1)}, u32[]{:S(2)}) copy-start(f32[100,2,640]{2,1,0:T(2,128)S(1)} %collective-permute-done.7.refs_8_) | copy-start | bytes 1536004
  12.9 33.4 %collective-permute-start.15 = (f32[100,2,640]{2,1,0:T(2,128)S(1)}, f32[100,2,640]{2,1,0:T(2,128)S(1)}, u32[]{:S(2)}, u32[]{:S(2)}) collective-permute-start(f32[100,2,640]{2,1,0:T(2,128)S(1)} %collective-permute-done.7.refs_8_), channel_id=1, source_target_pairs={{0,1},{1,0},{2,3},{3,2},{4,5},{5,4},{6,7},{7,6},{8,9},{9,8},{10,11... | collective-permute-start | bytes 1536008 | tf_op jit(solution)/shard_map/ppermute | solution.py:33
  14.4 34.5 %collective-permute-start.10 = (f32[100,2,640]{2,1,0:T(2,128)S(1)}, f32[100,2,640]{2,1,0:T(2,128)S(1)}, u32[]{:S(2)}, u32[]{:S(2)}) collective-permute-start(f32[100,2,640]{2,1,0:T(2,128)S(1)} %collective-permute-done.7.refs_8_), channel_id=1, source_target_pairs={{0,12},{1,13},{2,14},{3,15},{4,0},{5,1},{6,2},{7,3},{8,4},{9,5},{1... | collective-permute-start | bytes 1536008 | tf_op jit(solution)/shard_map/ppermute | solution.py:33
  38.6 53.4 %copy-start.2 = (f32[100,2,640]{2,1,0:T(2,128)}, f32[100,2,640]{2,1,0:T(2,128)S(1)}, u32[]{:S(2)}) copy-start(f32[100,2,640]{2,1,0:T(2,128)S(1)} %collective-permute-done.2.refs_3_) | copy-start | bytes 1536004
  38.6 13.4 %collective-permute-start.9 = (f32[100,2,640]{2,1,0:T(2,128)S(1)}, f32[100,2,640]{2,1,0:T(2,128)S(1)}, u32[]{:S(2)}, u32[]{:S(2)}) collective-permute-start(f32[100,2,640]{2,1,0:T(2,128)S(1)} %collective-permute-done.7.refs_8_), channel_id=1, source_target_pairs={{0,4},{1,5},{2,6},{3,7},{4,8},{5,9},{6,10},{7,11},{8,12},{9,13},{1... | collective-permute-start | bytes 1536008 | tf_op jit(solution)/shard_map/ppermute | solution.py:33
  43.2 48.8 %copy-start.3 = (f32[100,2,640]{2,1,0:T(2,128)}, f32[100,2,640]{2,1,0:T(2,128)S(1)}, u32[]{:S(2)}) copy-start(f32[100,2,640]{2,1,0:T(2,128)S(1)} %collective-permute-done.1.refs_2_) | copy-start | bytes 1536004
  43.2 14.1 %collective-permute-start.8 = (f32[100,2,640]{2,1,0:T(2,128)S(1)}, f32[100,2,640]{2,1,0:T(2,128)S(1)}, u32[]{:S(2)}, u32[]{:S(2)}) collective-permute-start(f32[100,2,640]{2,1,0:T(2,128)S(1)} %collective-permute-done.7.refs_8_), channel_id=1, source_target_pairs={{0,2},{1,3},{2,0},{3,1},{4,6},{5,7},{6,4},{7,5},{8,10},{9,11},{10,... | collective-permute-start | bytes 1536008 | tf_op jit(solution)/shard_map/ppermute | solution.py:33
  46.2 45.8 %copy-start.4 = (f32[100,2,640]{2,1,0:T(2,128)}, f32[100,2,640]{2,1,0:T(2,128)S(1)}, u32[]{:S(2)}) copy-start(f32[100,2,640]{2,1,0:T(2,128)S(1)} %collective-permute-done.refs_1_) | copy-start | bytes 1536004
  46.2 13.1 %collective-permute-start.5 = (f32[100,2,640]{2,1,0:T(2,128)S(1)}, f32[100,2,640]{2,1,0:T(2,128)S(1)}, u32[]{:S(2)}, u32[]{:S(2)}) collective-permute-start(f32[100,2,640]{2,1,0:T(2,128)S(1)} %collective-permute-done.1.refs_2_), channel_id=1, source_target_pairs={{0,32},{1,33},{2,34},{3,35},{4,36},{5,37},{6,38},{7,39},{8,40},{9,... | collective-permute-start | bytes 1536008 | tf_op jit(solution)/shard_map/ppermute | solution.py:33
  46.3 45.8 %copy-start.5 = (f32[100,2,640]{2,1,0:T(2,128)}, f32[100,2,640]{2,1,0:T(2,128)S(1)}, u32[]{:S(2)}) copy-start(f32[100,2,640]{2,1,0:T(2,128)S(1)} %collective-permute-done.15.refs_16_) | copy-start | bytes 1536004
  46.3 17.1 %collective-permute-start.4 = (f32[100,2,640]{2,1,0:T(2,128)S(1)}, f32[100,2,640]{2,1,0:T(2,128)S(1)}, u32[]{:S(2)}, u32[]{:S(2)}) collective-permute-start(f32[100,2,640]{2,1,0:T(2,128)S(1)} %collective-permute-done.refs_1_), channel_id=1, source_target_pairs={{0,96},{1,97},{2,98},{3,99},{4,100},{5,101},{6,102},{7,103},{8,104... | collective-permute-start | bytes 1536008 | tf_op jit(solution)/shard_map/ppermute | solution.py:33
  48.9 43.1 %copy-start.6 = (f32[100,2,640]{2,1,0:T(2,128)}, f32[100,2,640]{2,1,0:T(2,128)S(1)}, u32[]{:S(2)}) copy-start(f32[100,2,640]{2,1,0:T(2,128)S(1)} %collective-permute-done.10.refs_11_) | copy-start | bytes 1536004
  48.9 21.4 %collective-permute-start.3 = (f32[100,2,640]{2,1,0:T(2,128)S(1)}, f32[100,2,640]{2,1,0:T(2,128)S(1)}, u32[]{:S(2)}, u32[]{:S(2)}) collective-permute-start(f32[100,2,640]{2,1,0:T(2,128)S(1)} %collective-permute-done.refs_1_), channel_id=1, source_target_pairs={{0,32},{1,33},{2,34},{3,35},{4,36},{5,37},{6,38},{7,39},{8,40},{9,... | collective-permute-start | bytes 1536008 | tf_op jit(solution)/shard_map/ppermute | solution.py:33
  52.1 40.0 %copy-start.7 = (f32[100,2,640]{2,1,0:T(2,128)}, f32[100,2,640]{2,1,0:T(2,128)S(1)}, u32[]{:S(2)}) copy-start(f32[100,2,640]{2,1,0:T(2,128)S(1)} %collective-permute-done.9.refs_10_) | copy-start | bytes 1536004
  52.1 20.4 %collective-permute-start.18 = (f32[100,2,640]{2,1,0:T(2,128)S(1)}, f32[100,2,640]{2,1,0:T(2,128)S(1)}, u32[]{:S(2)}, u32[]{:S(2)}) collective-permute-start(f32[100,2,640]{2,1,0:T(2,128)S(1)} %collective-permute-done.10.refs_11_), channel_id=1, source_target_pairs={{0,1},{1,0},{2,3},{3,2},{4,5},{5,4},{6,7},{7,6},{8,9},{9,8},{10,11... | collective-permute-start | bytes 1536008 | tf_op jit(solution)/shard_map/ppermute | solution.py:33
  57.3 34.8 %copy-start.8 = (f32[100,2,640]{2,1,0:T(2,128)}, f32[100,2,640]{2,1,0:T(2,128)S(1)}, u32[]{:S(2)}) copy-start(f32[100,2,640]{2,1,0:T(2,128)S(1)} %collective-permute-done.8.refs_9_) | copy-start | bytes 1536004
  57.3 15.3 %collective-permute-start.12 = (f32[100,2,640]{2,1,0:T(2,128)S(1)}, f32[100,2,640]{2,1,0:T(2,128)S(1)}, u32[]{:S(2)}, u32[]{:S(2)}) collective-permute-start(f32[100,2,640]{2,1,0:T(2,128)S(1)} %collective-permute-done.8.refs_9_), channel_id=1, source_target_pairs={{0,12},{1,13},{2,14},{3,15},{4,0},{5,1},{6,2},{7,3},{8,4},{9,5},{1... | collective-permute-start | bytes 1536008 | tf_op jit(solution)/shard_map/ppermute | solution.py:33
  59.3 32.7 %copy-start.9 = (f32[100,2,640]{2,1,0:T(2,128)}, f32[100,2,640]{2,1,0:T(2,128)S(1)}, u32[]{:S(2)}) copy-start(f32[100,2,640]{2,1,0:T(2,128)S(1)} %collective-permute-done.5.refs_6_) | copy-start | bytes 1536004
  59.3 15.9 %collective-permute-start.17 = (f32[100,2,640]{2,1,0:T(2,128)S(1)}, f32[100,2,640]{2,1,0:T(2,128)S(1)}, u32[]{:S(2)}, u32[]{:S(2)}) collective-permute-start(f32[100,2,640]{2,1,0:T(2,128)S(1)} %collective-permute-done.9.refs_10_), channel_id=1, source_target_pairs={{0,1},{1,0},{2,3},{3,2},{4,5},{5,4},{6,7},{7,6},{8,9},{9,8},{10,11... | collective-permute-start | bytes 1536008 | tf_op jit(solution)/shard_map/ppermute | solution.py:33
  63.3 28.7 %copy-start.10 = (f32[100,2,640]{2,1,0:T(2,128)}, f32[100,2,640]{2,1,0:T(2,128)S(1)}, u32[]{:S(2)}) copy-start(f32[100,2,640]{2,1,0:T(2,128)S(1)} %collective-permute-done.4.refs_5_) | copy-start | bytes 1536004
  63.3 14.4 %collective-permute-start.13 = (f32[100,2,640]{2,1,0:T(2,128)S(1)}, f32[100,2,640]{2,1,0:T(2,128)S(1)}, u32[]{:S(2)}, u32[]{:S(2)}) collective-permute-start(f32[100,2,640]{2,1,0:T(2,128)S(1)} %collective-permute-done.9.refs_10_), channel_id=1, source_target_pairs={{0,4},{1,5},{2,6},{3,7},{4,8},{5,9},{6,10},{7,11},{8,12},{9,13},{1... | collective-permute-start | bytes 1536008 | tf_op jit(solution)/shard_map/ppermute | solution.py:33
  70.3 21.8 %copy-start.11 = (f32[100,2,640]{2,1,0:T(2,128)}, f32[100,2,640]{2,1,0:T(2,128)S(1)}, u32[]{:S(2)}) copy-start(f32[100,2,640]{2,1,0:T(2,128)S(1)} %collective-permute-done.3.refs_4_) | copy-start | bytes 1536004
  70.3 8.8 %collective-permute-start.16 = (f32[100,2,640]{2,1,0:T(2,128)S(1)}, f32[100,2,640]{2,1,0:T(2,128)S(1)}, u32[]{:S(2)}, u32[]{:S(2)}) collective-permute-start(f32[100,2,640]{2,1,0:T(2,128)S(1)} %collective-permute-done.8.refs_9_), channel_id=1, source_target_pairs={{0,1},{1,0},{2,3},{3,2},{4,5},{5,4},{6,7},{7,6},{8,9},{9,8},{10,11... | collective-permute-start | bytes 1536008 | tf_op jit(solution)/shard_map/ppermute | solution.py:33
  72.5 19.6 %copy-start.12 = (f32[100,2,640]{2,1,0:T(2,128)}, f32[100,2,640]{2,1,0:T(2,128)S(1)}, u32[]{:S(2)}) copy-start(f32[100,2,640]{2,1,0:T(2,128)S(1)} %collective-permute-done.18.refs_19_) | copy-start | bytes 1536004
  72.5 16.2 %collective-permute-start.11 = (f32[100,2,640]{2,1,0:T(2,128)S(1)}, f32[100,2,640]{2,1,0:T(2,128)S(1)}, u32[]{:S(2)}, u32[]{:S(2)}) collective-permute-start(f32[100,2,640]{2,1,0:T(2,128)S(1)} %collective-permute-done.8.refs_9_), channel_id=1, source_target_pairs={{0,4},{1,5},{2,6},{3,7},{4,8},{5,9},{6,10},{7,11},{8,12},{9,13},{1... | collective-permute-start | bytes 1536008 | tf_op jit(solution)/shard_map/ppermute | solution.py:33
  72.5 19.6 %copy-start.13 = (f32[100,2,640]{2,1,0:T(2,128)}, f32[100,2,640]{2,1,0:T(2,128)S(1)}, u32[]{:S(2)}) copy-start(f32[100,2,640]{2,1,0:T(2,128)S(1)} %collective-permute-done.12.refs_13_) | copy-start | bytes 1536004
  72.5 17.1 %collective-permute-start.14 = (f32[100,2,640]{2,1,0:T(2,128)S(1)}, f32[100,2,640]{2,1,0:T(2,128)S(1)}, u32[]{:S(2)}, u32[]{:S(2)}) collective-permute-start(f32[100,2,640]{2,1,0:T(2,128)S(1)} %collective-permute-done.12.refs_13_), channel_id=1, source_target_pairs={{0,12},{1,13},{2,14},{3,15},{4,0},{5,1},{6,2},{7,3},{8,4},{9,5},{1... | collective-permute-start | bytes 1536008 | tf_op jit(solution)/shard_map/ppermute | solution.py:33
  75.2 16.9 %copy-start.14 = (f32[100,2,640]{2,1,0:T(2,128)}, f32[100,2,640]{2,1,0:T(2,128)S(1)}, u32[]{:S(2)}) copy-start(f32[100,2,640]{2,1,0:T(2,128)S(1)} %collective-permute-done.17.refs_18_) | copy-start | bytes 1536004
  75.2 14.5 %collective-permute-start.6 = (f32[100,2,640]{2,1,0:T(2,128)S(1)}, f32[100,2,640]{2,1,0:T(2,128)S(1)}, u32[]{:S(2)}, u32[]{:S(2)}) collective-permute-start(f32[100,2,640]{2,1,0:T(2,128)S(1)} %collective-permute-done.4.refs_5_), channel_id=1, source_target_pairs={{0,96},{1,97},{2,98},{3,99},{4,100},{5,101},{6,102},{7,103},{8,104... | collective-permute-start | bytes 1536008 | tf_op jit(solution)/shard_map/ppermute | solution.py:33
  77.8 14.3 %copy-start.15 = (f32[100,2,640]{2,1,0:T(2,128)}, f32[100,2,640]{2,1,0:T(2,128)S(1)}, u32[]{:S(2)}) copy-start(f32[100,2,640]{2,1,0:T(2,128)S(1)} %collective-permute-done.13.refs_14_) | copy-start | bytes 1536004
  77.8 12.0 %collective-permute-start.20 = (f32[100,2,640]{2,1,0:T(2,128)S(1)}, f32[100,2,640]{2,1,0:T(2,128)S(1)}, u32[]{:S(2)}, u32[]{:S(2)}) collective-permute-start(f32[100,2,640]{2,1,0:T(2,128)S(1)} %collective-permute-done.12.refs_13_), channel_id=1, source_target_pairs={{0,1},{1,0},{2,3},{3,2},{4,5},{5,4},{6,7},{7,6},{8,9},{9,8},{10,11... | collective-permute-start | bytes 1536008 | tf_op jit(solution)/shard_map/ppermute | solution.py:33
  79.1 10.6 %copy-start.16 = (f32[100,2,640]{2,1,0:T(2,128)}, f32[100,2,640]{2,1,0:T(2,128)S(1)}, u32[]{:S(2)}) copy-start(f32[100,2,640]{2,1,0:T(2,128)S(1)} %collective-permute-done.16.refs_17_) | copy-start | bytes 1536004
  79.1 10.6 %collective-permute-start.21 = (f32[100,2,640]{2,1,0:T(2,128)S(1)}, f32[100,2,640]{2,1,0:T(2,128)S(1)}, u32[]{:S(2)}, u32[]{:S(2)}) collective-permute-start(f32[100,2,640]{2,1,0:T(2,128)S(1)} %collective-permute-done.13.refs_14_), channel_id=1, source_target_pairs={{0,1},{1,0},{2,3},{3,2},{4,5},{5,4},{6,7},{7,6},{8,9},{9,8},{10,11... | collective-permute-start | bytes 1536008 | tf_op jit(solution)/shard_map/ppermute | solution.py:33
  88.7 2.4 %copy-start.17 = (f32[100,2,640]{2,1,0:T(2,128)}, f32[100,2,640]{2,1,0:T(2,128)S(1)}, u32[]{:S(2)}) copy-start(f32[100,2,640]{2,1,0:T(2,128)S(1)} %collective-permute-done.11.refs_12_) | copy-start | bytes 1536004
  88.7 2.4 %collective-permute-start.19 = (f32[100,2,640]{2,1,0:T(2,128)S(1)}, f32[100,2,640]{2,1,0:T(2,128)S(1)}, u32[]{:S(2)}, u32[]{:S(2)}) collective-permute-start(f32[100,2,640]{2,1,0:T(2,128)S(1)} %collective-permute-done.11.refs_12_), channel_id=1, source_target_pairs={{0,1},{1,0},{2,3},{3,2},{4,5},{5,4},{6,7},{7,6},{8,9},{9,8},{10,11... | collective-permute-start | bytes 1536008 | tf_op jit(solution)/shard_map/ppermute | solution.py:33
  89.6 1.5 %copy-start.18 = (f32[100,2,640]{2,1,0:T(2,128)}, f32[100,2,640]{2,1,0:T(2,128)S(1)}, u32[]{:S(2)}) copy-start(f32[100,2,640]{2,1,0:T(2,128)S(1)} %collective-permute-done.14.refs_15_) | copy-start | bytes 1536004
  89.6 2.4 %collective-permute-start.22 = (f32[100,2,640]{2,1,0:T(2,128)S(1)}, f32[100,2,640]{2,1,0:T(2,128)}, u32[]{:S(2)}, u32[]{:S(2)}) collective-permute-start(f32[100,2,640]{2,1,0:T(2,128)S(1)} %collective-permute-done.14.refs_15_), channel_id=1, source_target_pairs={{0,1},{1,0},{2,3},{3,2},{4,5},{5,4},{6,7},{7,6},{8,9},{9,8},{10,11... | collective-permute-start | bytes 1536008 | tf_op jit(solution)/shard_map/ppermute | solution.py:33
  89.7 1.4 %copy-start.19 = (f32[100,2,640]{2,1,0:T(2,128)}, f32[100,2,640]{2,1,0:T(2,128)S(1)}, u32[]{:S(2)}) copy-start(f32[100,2,640]{2,1,0:T(2,128)S(1)} %collective-permute-done.6.refs_7_) | copy-start | bytes 1536004
  89.7 1.4 %copy-start.21 = (f32[100,2,640]{2,1,0:T(2,128)}, f32[100,2,640]{2,1,0:T(2,128)S(1)}, u32[]{:S(2)}) copy-start(f32[100,2,640]{2,1,0:T(2,128)S(1)} %collective-permute-done.21.refs_22_) | copy-start | bytes 1536004
  89.7 1.4 %copy-start.20 = (f32[100,2,640]{2,1,0:T(2,128)}, f32[100,2,640]{2,1,0:T(2,128)S(1)}, u32[]{:S(2)}) copy-start(f32[100,2,640]{2,1,0:T(2,128)S(1)} %collective-permute-done.20.refs_21_) | copy-start | bytes 1536004
  91.1 0.8 copy-start.22

commit v2 on v0

v2 whole, which is shorter than its diff:
```python
import functools

import jax
import jax.numpy as jnp
from jax import lax
from jax.experimental import pallas as pl
from jax.experimental.pallas import tpu as pltpu
from jax.sharding import PartitionSpec as P

AXES = ("row", "col")
HALF = 50
GROUP = 4
PARTIAL = 2 * GROUP * HALF
MAIN = PARTIAL // 128 * 128
REST = PARTIAL - MAIN
DEPTH = 3 * MAIN + 128
WIDTH = 640
LANES = 128
CUTS = WIDTH // LANES
LIMIT = 40 * 1024 * 1024


def flat(x, z, y, low, core):
    return ((x % 4) * 2 + z % 2) * 16 + ((y % 4) * 2 + low % 2) * 2 + core % 2


def permute(value, move):
    pairs = []
    for x in range(4):
        for z in range(2):
            for y in range(4):
                for low in range(2):
                    for core in range(2):
                        pairs.append((flat(x, z, y, low, core), flat(*move(x, z, y, low, core))))
    return lax.ppermute(value, AXES, pairs)


def together(*values):
    return lax.optimization_barrier(values)


def split(value):
    high = value.astype(jnp.bfloat16)
    return high, (value - high.astype(jnp.float32)).astype(jnp.bfloat16)


def dot(a, b):
    return jnp.dot(a, b, preferred_element_type=jnp.float32)


def fetch(ref, half, target, at, cut, sem):
    return pltpu.make_async_copy(
        ref.at[pl.ds(half * HALF, HALF), :, pl.ds(cut * LANES, LANES)],
        target.at[cut, pl.ds(at, HALF)],
        sem,
    )


def fetch_lefts(refs, target, sems):
    copies = []
    for cut in range(CUTS):
        for half in range(2):
            for n, ref in enumerate(refs):
                at = half * GROUP * HALF + n * HALF
                copies.append(fetch(ref, half, target, at, cut, sems.at[cut, half, n]))
    return copies


def fill_right(source, first, target):
    for cut in range(CUTS):
        for j in range(2):
            cols = pl.ds((cut * 2 + j) * LANES, LANES)
            for k in range(0, MAIN, LANES):
                high, rest = split(source[cut, pl.ds((first + k) * 2 + j, LANES, stride=2), :])
                target[pl.ds(k, LANES), cols] = high
                target[pl.ds(MAIN + k, LANES), cols] = rest
                target[pl.ds(2 * MAIN + k, LANES), cols] = high
            high, rest = split(source[cut, pl.ds((first + MAIN) * 2 + j, REST, stride=2), :])
            target[pl.ds(3 * MAIN, REST), cols] = high
            target[pl.ds(3 * MAIN + REST, REST), cols] = rest
            target[pl.ds(3 * MAIN + 2 * REST, REST), cols] = high
            target[pl.ds(3 * MAIN + 3 * REST, 128 - 3 * REST), cols] = jnp.zeros((128 - 3 * REST, LANES), jnp.bfloat16)


def fill_left(source, j, cut, target):
    rows = pl.ds(cut * LANES, LANES)
    for k in range(0, MAIN, LANES):
        high, rest = split(source[cut, pl.ds(k * 2 + j, LANES, stride=2), :].T)
        target[rows, pl.ds(k, LANES)] = high
        target[rows, pl.ds(MAIN + k, LANES)] = high
        target[rows, pl.ds(2 * MAIN + k, LANES)] = rest
    value = source[cut, pl.ds(MAIN * 2 + j, REST, stride=2), :]
    high = value.astype(jnp.bfloat16).astype(jnp.float32)
    pad = jnp.zeros((128 - 3 * REST, LANES), jnp.float32)
    stack = jnp.concatenate([high, high, value - high, pad], axis=0)
    target[rows, pl.ds(3 * MAIN, LANES)] = stack.T.astype(jnp.bfloat16)


def fill_all(source, j, target):
    for cut in range(CUTS):
        fill_left(source, j, cut, target)


def begin(*refs):
    js, mine, theirs = refs[:8], refs[8:12], refs[12:14]
    total, later = refs[14:16]
    right, left, now, even, odd, jsems, isems = refs[16:]
    held = (even, odd)
    row, col = lax.axis_index("row"), lax.axis_index("col")
    x, z = row // 2, row % 2
    y, low, core = col // 4, (col // 2) % 2, col % 2
    way = 1 - 2 * core

    places = [(x, z), (x, z + 1), (x - way, z), (x + way, z),
              (x - way, z + 1), (x + way, z + 1), (x + 2, z), (x + 2, z + 1)]

    def position(a, b, half):
        delta = (a - (y - x + 2 * half) + 16) % 4
        other = (b + low + half) % 2
        side = jnp.where(delta == (4 - way) % 4, 2, 3) + 2 * other
        n = jnp.where(delta == 0, other, jnp.where(delta == 2, 6 + other, side))
        return (n // GROUP) * PARTIAL + half * GROUP * HALF + (n % GROUP) * HALF

    rights = []
    for half in range(2):
        for n, (ref, (a, b)) in enumerate(zip(js, places)):
            at = position(a, b, half)
            for cut in range(CUTS):
                rights.append(fetch(ref, half, right, at, cut, jsems.at[cut, half, n]))
    pieces = [theirs[n // 2].at[pl.ds(n % 2 * 2 * HALF, 2 * HALF)] for n in (0, 1, 3, 2)]
    lefts = [fetch_lefts(mine, left.at[0], isems.at[0]), fetch_lefts(pieces, left.at[1], isems.at[1])]
    for copy in rights + lefts[0] + lefts[1]:
        copy.start()
    for copy in rights:
        copy.wait()
    right = right.reshape(CUTS, 4 * PARTIAL, LANES)
    sources = [left.at[h].reshape(CUTS, 2 * PARTIAL, LANES) for h in range(2)]
    fill_right(right, 0, now)
    fill_right(right, PARTIAL, later)
    for half in range(2):
        for copy in lefts[half]:
            copy.wait()
    fill_all(sources[0], 0, held[0])
    for i in range(4):
        total[i] = dot(held[i % 2][...], now[...])
        if i < 3:
            fill_all(sources[(i + 1) // 2], (i + 1) % 2, held[(i + 1) % 2])


def finish(*refs):
    mine, theirs, total, now = refs[:4], refs[4:8], refs[8], refs[9]
    out, left, even, odd, before, stage, isems, osems = refs[10:]
    held = (even, odd)
    core = lax.axis_index("col") % 2
    lefts = [fetch_lefts(mine, left.at[0], isems.at[0]), fetch_lefts(theirs, left.at[1], isems.at[1])]

    def flush(i, cut):
        return pltpu.make_async_copy(
            stage.at[i % 2, cut],
            out.at[2 * ((core + i // 2) % 2) + i % 2, :, :, pl.ds(cut * LANES, LANES)],
            osems.at[i % 2, cut],
        )

    for copy in lefts[0]:
        copy.start()
    for copy in lefts[1]:
        copy.start()
    sources = [left.at[h].reshape(CUTS, 2 * PARTIAL, LANES) for h in range(2)]
    flat_stage = stage.reshape(2, CUTS, 2 * WIDTH, LANES)
    def store(i):
        for cut in range(CUTS):
            for j in range(2):
                at = (cut * 2 + j) * LANES
                flat_stage[i % 2, cut, pl.ds(j, WIDTH, stride=2), :] = before[:, pl.ds(at, LANES)]

    for half in range(2):
        for copy in lefts[half]:
            copy.wait()
    fill_all(sources[0], 0, held[0])
    for i in range(4):
        before[...] = total[i] + dot(held[i % 2][...], now[...])
        if i < 3:
            fill_all(sources[(i + 1) // 2], (i + 1) % 2, held[(i + 1) % 2])
        if i >= 2:
            for cut in range(CUTS):
                flush(i - 2, cut).wait()
        store(i)
        for cut in range(CUTS):
            flush(i, cut).start()
    for i in (2, 3):
        for cut in range(CUTS):
            flush(i, cut).wait()


ANY = pl.BlockSpec(memory_space=pl.ANY)
NEAR = pl.BlockSpec(memory_space=pltpu.VMEM)
WIDE = 10 * LANES


def start_products(js, mine, theirs):
    return pl.pallas_call(
        begin,
        out_shape=(
            pltpu.VMEM((4, WIDTH, WIDE), jnp.float32),
            pltpu.VMEM((DEPTH, WIDE), jnp.bfloat16),
        ),
        in_specs=[ANY] * 14,
        out_specs=(NEAR, NEAR),
        scratch_shapes=[
            pltpu.VMEM((CUTS, 2 * PARTIAL, 2, LANES), jnp.float32),
            pltpu.VMEM((2, CUTS, PARTIAL, 2, LANES), jnp.float32),
            pltpu.VMEM((DEPTH, WIDE), jnp.bfloat16),
            pltpu.VMEM((WIDTH, DEPTH), jnp.bfloat16),
            pltpu.VMEM((WIDTH, DEPTH), jnp.bfloat16),
            pltpu.SemaphoreType.DMA((CUTS, 2, 8)),
            pltpu.SemaphoreType.DMA((2, CUTS, 2, GROUP)),
        ],
        compiler_params=pltpu.CompilerParams(vmem_limit_bytes=LIMIT),
        cost_estimate=pl.CostEstimate(flops=10**6, bytes_accessed=10**5, transcendentals=0),
    )(*js, *mine, *theirs)


def end_products(mine, theirs, total, kept):
    return pl.pallas_call(
        finish,
        out_shape=jax.ShapeDtypeStruct((4, WIDTH, 2, WIDTH), jnp.float32),
        in_specs=[ANY] * 8 + [NEAR] * 2,
        out_specs=ANY,
        scratch_shapes=[
            pltpu.VMEM((2, CUTS, PARTIAL, 2, LANES), jnp.float32),
            pltpu.VMEM((WIDTH, DEPTH), jnp.bfloat16),
            pltpu.VMEM((WIDTH, DEPTH), jnp.bfloat16),
            pltpu.VMEM((WIDTH, WIDE), jnp.float32),
            pltpu.VMEM((2, CUTS, WIDTH, 2, LANES), jnp.float32),
            pltpu.SemaphoreType.DMA((2, CUTS, 2, GROUP)),
            pltpu.SemaphoreType.DMA((2, CUTS)),
        ],
        compiler_params=pltpu.CompilerParams(vmem_limit_bytes=LIMIT),
        cost_estimate=pl.CostEstimate(flops=2 * 2560 * 1280 * DEPTH, bytes_accessed=34 * 10**6, transcendentals=0),
    )(
        *mine,
        *theirs,
        pltpu.with_memory_space_constraint(total, pltpu.VMEM),
        pltpu.with_memory_space_constraint(kept, pltpu.VMEM),
    )


def shards(amplitude, coupling):
    amps = jnp.transpose(amplitude, (1, 2, 0, 3)).reshape(HALF, 2, WIDTH)
    ints = coupling.reshape(HALF, 2, WIDTH)
    block = jnp.concatenate([ints, amps], axis=0)

    def way(core):
        return 1 - 2 * core

    def right(x, z, y, low, core):
        return x + way(core), z, y, low, core

    def left(x, z, y, low, core):
        return x - way(core), z, y, low, core

    def up(x, z, y, low, core):
        return x, z, y + way(core), low, core

    def down(x, z, y, low, core):
        return x, z, y - way(core), low, core

    def near(x, z, y, low, core):
        return x, z, y, low + 1, core

    def tilt(value, shift):
        return permute(value, lambda x, z, y, low, core: (x, z, y + x + shift, low, core))

    def mirror(value, shift):
        return permute(
            value, lambda x, z, y, low, core: (y - x - shift, low, y, z + shift // 2, core)
        )

    def swap(value):
        return permute(value, lambda x, z, y, low, core: (x, z, y, low, core + 1))

    ta = tilt(amps, 0)
    tw = tilt(ints, 2)
    ja = permute(block, right)
    jb = permute(block, left)
    far = permute(block, lambda x, z, y, low, core: (x, z + 1, y, low, core))
    ta, tw = together(ta, tw)
    ma = mirror(ta, 0)
    mw = mirror(tw, 2)

    ma, mw, far, ja, jb = together(ma, mw, far, ja, jb)
    held = jnp.concatenate([ma, mw], axis=0)
    a = permute(held, up)
    b = permute(held, down)
    beside = permute(held, near)
    jc = permute(far, right)
    jd = permute(far, left)

    held, beside, a, b, ja, jc, jd = together(held, beside, a, b, ja, jc, jd)
    e = permute(a, up)
    je = permute(ja, right)
    jf = permute(jd, left)
    early = [swap(jnp.concatenate([held, beside], axis=0)), swap(jnp.concatenate([a, b], axis=0))]
    e, beside, *early = together(e, beside, *early)
    f = permute(e, near)
    c = permute(beside, up)
    d = permute(beside, down)
    js = [block, far, ja, jb, jc, jd, je, jf]
    total, kept = start_products(js, [held, beside, a, b], early)
    c, d, e, f, total = together(c, d, e, f, total)
    c2, d2, e2, f2 = swap(c), swap(d), swap(e), swap(f)
    return end_products([c, d, e, f], [d2, c2, e2, f2], total, kept)


def solution(mesh):
    placed = (P("col", "row", None, None), P("row", None, "col", None))
    return jax.shard_map(
        shards, mesh=mesh, in_specs=placed, out_specs=P("row", None, "col", None), check_vma=False
    )
```

time: 414 us -> 104 us (0.25)
  waiting for transfers between devices: 303 us -> 34.2 us
  matrix products: 45 us -> 0 us
  local copies, waits for them, and re-layouts: 38.5 us -> 2.56 us
  Pallas kernels: 0 us -> 29.5 us
  starting transfers between devices: 13.8 us -> 35.2 us
  between operations: 13.2 us -> 0.49 us
    all_gather x4 -> x0, waiting for transfers between devices: 301 us -> none  [the longest x1 104 us: shards(): widened = lax.all_gather(coupling, 'col', axis=2, tiled=True)]
    dot_general x1 -> x0, matrix products: 45 us -> none  [shards(): lax.dot_general(left, right, (((0,), (0,)), ((), ())), precision=lax.Prec...]
    ppermute x0 -> x24, starting transfers between devices: none -> 35.2 us  [permute(): return lax.ppermute(value, AXES, pairs)]
    ppermute x0 -> x24, waiting for transfers between devices: none -> 34.2 us  [permute(): return lax.ppermute(value, AXES, pairs)]
    pallas_call x0 -> x2, Pallas kernels: none -> 29.5 us  [the longest x1 15 us: end_products(): pl.pallas_call(finish, out_shape=jax.ShapeDtypeStruct((4, WIDTH, 2, WIDTH...]
    reshape x1 -> x0, local copies, waits for them, and re-layouts: 16.3 us -> none  [shards(): return result.reshape(own_rows, width, own_cols, width)]
    all_to_all x2 -> x0, starting transfers between devices: 13.7 us -> none  [the longest x1 7.25 us: shards(): lax.all_to_all(widened, 'row', split_axis=2, concat_axis=0, tiled=True)]
    unnamed x10 -> x43, local copies, waits for them, and re-layouts: 13.3 us -> 2.5 us
  transfers between devices with their start and end apart: 6 -> 24, of which waited for: 4 -> 13; matrix products, arithmetic and copies ran while one was open for 3% -> 2% of each run, Pallas kernels for 0% -> 14%
where the time goes in v2:
time: 104 us
  starting transfers between devices  35.2 us (34%)
  waiting for transfers between devices  34.2 us (33%)
  Pallas kernels  29.5 us (28%)
  local copies, waits for them, and re-layouts  2.56 us (2%)
  other arithmetic  2.17 us (2%)
    ppermute x24, starting transfers between devices, permute(): return lax.ppermute(value, AXES, pairs)  35.2 us
    ppermute x24, waiting for transfers between devices, permute(): return lax.ppermute(value, AXES, pairs)  34.2 us
    pallas_call x1, Pallas kernels, end_products(): pl.pallas_call(finish, out_shape=jax.ShapeDtypeStruct((4, WIDTH, 2, WIDTH...  15 us
    pallas_call x1, Pallas kernels, start_products(): pl.pallas_call(begin, out_shape=(pltpu.VMEM((4, WIDTH, WIDE), jnp.float32...  14.5 us
    unnamed x43, local copies, waits for them, and re-layouts  2.5 us
  transfers between devices with their start and end apart: 24, of which 13 were waited for; matrix products, arithmetic and copies ran while one was open for 2% of the time, Pallas kernels for 14%

profile of v2, /device:TPU:1, one launch (start us, length us, event | category | flops | bytes accessed | tf_op | source)
XLA Modules:
  0.0 104.0 jit_solution(4631264307669452162)
XLA Ops:
  0.0 1.6 %collective-permute-start = (f32[50,2,640]{2,1,0:T(2,128)}, f32[50,2,640]{2,1,0:T(2,128)S(1)}, u32[]{:S(2)}, u32[]{:S(2)}) collective-permute-start(f32[50,2,640]{2,1,0:T(2,128)} %bitcast.4), channel_id=1, source_target_pairs={{0,0},{1,1},{2,2},{3,3},{4,4},{5,5},{6,6},{7,7},{8,8},{9,9},{10,10... | collective-permute-start | bytes 768008 | tf_op jit(solution)/shard_map/ppermute | solution.py:35
  1.6 5.6 %collective-permute-start.1 = (f32[50,2,640]{2,1,0:T(2,128)}, f32[50,2,640]{2,1,0:T(2,128)S(1)}, u32[]{:S(2)}, u32[]{:S(2)}) collective-permute-start(f32[50,2,640]{2,1,0:T(2,128)} %bitcast.6), channel_id=1, source_target_pairs={{0,8},{1,9},{2,10},{3,11},{4,12},{5,13},{6,14},{7,15},{8,0},{9,1},... | collective-permute-start | bytes 768008 | tf_op jit(solution)/shard_map/ppermute | solution.py:35
  7.2 1.3 %pad_maximum_fusion.2.refs_0_ = f32[100,2,640]{2,1,0:T(2,128)S(1)} fusion(f32[50,2,640]{2,1,0:T(2,128)} %bitcast.5, f32[50,2,640]{2,1,0:T(2,128)} %bitcast.7), kind=kLoop, calls=%fused_computation.2 | loop fusion | flops 128000 | bytes 1024000 | tf_op jit(solution)/shard_map/concatenate | solution.py:251
  8.5 0.0 copy-start.1
  8.5 1.4 %collective-permute-start.6 = (f32[100,2,640]{2,1,0:T(2,128)S(1)}, f32[100,2,640]{2,1,0:T(2,128)S(1)}, u32[]{:S(2)}, u32[]{:S(2)}) collective-permute-start(f32[100,2,640]{2,1,0:T(2,128)S(1)} %pad_maximum_fusion.2.refs_0_), channel_id=1, source_target_pairs={{0,96},{1,33},{2,98},{3,35},{4,100},{5,37},{6,102},{7,39},{8,104},... | collective-permute-start | bytes 1536008 | tf_op jit(solution)/shard_map/ppermute | solution.py:35
  10.0 1.3 %collective-permute-start.5 = (f32[100,2,640]{2,1,0:T(2,128)S(1)}, f32[100,2,640]{2,1,0:T(2,128)S(1)}, u32[]{:S(2)}, u32[]{:S(2)}) collective-permute-start(f32[100,2,640]{2,1,0:T(2,128)S(1)} %pad_maximum_fusion.2.refs_0_), channel_id=1, source_target_pairs={{0,32},{1,97},{2,34},{3,99},{4,36},{5,101},{6,38},{7,103},{8,40},{... | collective-permute-start | bytes 1536008 | tf_op jit(solution)/shard_map/ppermute | solution.py:35
  11.3 3.6 %collective-permute-start.4 = (f32[100,2,640]{2,1,0:T(2,128)S(1)}, f32[100,2,640]{2,1,0:T(2,128)S(1)}, u32[]{:S(2)}, u32[]{:S(2)}) collective-permute-start(f32[100,2,640]{2,1,0:T(2,128)S(1)} %pad_maximum_fusion.2.refs_0_), channel_id=1, source_target_pairs={{0,16},{1,17},{2,18},{3,19},{4,20},{5,21},{6,22},{7,23},{8,24},{9,... | collective-permute-start | bytes 1536008 | tf_op jit(solution)/shard_map/ppermute | solution.py:35
  14.9 0.0 collective-permute-done
  14.9 0.0 collective-permute-done.1
  14.9 0.7 collective-permute-start.2
  15.6 3.6 %collective-permute-start.3 = (f32[50,2,640]{2,1,0:T(2,128)S(1)}, f32[50,2,640]{2,1,0:T(2,128)S(1)}, u32[]{:S(2)}, u32[]{:S(2)}) collective-permute-start(f32[50,2,640]{2,1,0:T(2,128)S(1)} %collective-permute-done.1), channel_id=1, source_target_pairs={{0,66},{1,67},{2,82},{3,83},{4,102},{5,103},{6,118},{7,119},{8,10}... | collective-permute-start | bytes 768008 | tf_op jit(solution)/shard_map/ppermute | solution.py:35
  19.2 0.0 collective-permute-done.2
  19.2 12.1 %collective-permute-done.3 = f32[50,2,640]{2,1,0:T(2,128)S(1)} collective-permute-done((f32[50,2,640]{2,1,0:T(2,128)S(1)}, f32[50,2,640]{2,1,0:T(2,128)S(1)}, u32[]{:S(2)}, u32[]{:S(2)}) %collective-permute-start.3) | collective-permute-done | bytes 256032 | tf_op jit(solution)/shard_map/ppermute | solution.py:35
  31.3 0.0 collective-permute-done.6.refs_3_
  31.3 0.0 collective-permute-done.5.refs_2_
  31.3 0.0 collective-permute-done.4.refs_1_
  31.4 0.1 constant_dynamic-update-slice_fusion.refs_8_
  31.4 0.0 copy-start
  31.4 0.1 collective-permute-start.9
  31.5 2.9 %collective-permute-start.8 = (f32[100,2,640]{2,1,0:T(2,128)S(1)}, f32[100,2,640]{2,1,0:T(2,128)S(1)}, u32[]{:S(2)}, u32[]{:S(2)}) collective-permute-start(f32[100,2,640]{2,1,0:T(2,128)S(1)} %constant_dynamic-update-slice_fusion.refs_8_), channel_id=1, source_target_pairs={{0,4},{1,13},{2,6},{3,15},{4,8},{5,1},{6,10},{7,3},{8,12},{9,5},{1... | collective-permute-start | bytes 1536008 | tf_op jit(solution)/shard_map/ppermute | solution.py:35
  34.4 2.1 %collective-permute-start.7 = (f32[100,2,640]{2,1,0:T(2,128)S(1)}, f32[100,2,640]{2,1,0:T(2,128)S(1)}, u32[]{:S(2)}, u32[]{:S(2)}) collective-permute-start(f32[100,2,640]{2,1,0:T(2,128)S(1)} %constant_dynamic-update-slice_fusion.refs_8_), channel_id=1, source_target_pairs={{0,2},{1,3},{2,0},{3,1},{4,6},{5,7},{6,4},{7,5},{8,10},{9,11},{10,... | collective-permute-start | bytes 1536008 | tf_op jit(solution)/shard_map/ppermute | solution.py:35
  36.5 0.9 collective-permute-start.11
  37.3 1.8 %collective-permute-start.10 = (f32[100,2,640]{2,1,0:T(2,128)S(1)}, f32[100,2,640]{2,1,0:T(2,128)S(1)}, u32[]{:S(2)}, u32[]{:S(2)}) collective-permute-start(f32[100,2,640]{2,1,0:T(2,128)S(1)} %collective-permute-done.4.refs_1_), channel_id=1, source_target_pairs={{0,32},{1,97},{2,34},{3,99},{4,36},{5,101},{6,38},{7,103},{8,40},{... | collective-permute-start | bytes 1536008 | tf_op jit(solution)/shard_map/ppermute | solution.py:35
  39.1 1.6 %collective-permute-done.9.refs_11_ = f32[100,2,640]{2,1,0:T(2,128)S(1)} collective-permute-done((f32[100,2,640]{2,1,0:T(2,128)S(1)}, f32[100,2,640]{2,1,0:T(2,128)S(1)}, u32[]{:S(2)}, u32[]{:S(2)}) %collective-permute-start.9) | collective-permute-done | bytes 512032 | tf_op jit(solution)/shard_map/ppermute | solution.py:35
  40.8 2.3 %collective-permute-done.8.refs_10_ = f32[100,2,640]{2,1,0:T(2,128)S(1)} collective-permute-done((f32[100,2,640]{2,1,0:T(2,128)S(1)}, f32[100,2,640]{2,1,0:T(2,128)S(1)}, u32[]{:S(2)}, u32[]{:S(2)}) %collective-permute-start.8) | collective-permute-done | bytes 512032 | tf_op jit(solution)/shard_map/ppermute | solution.py:35
  43.1 3.1 %collective-permute-done.7.refs_9_ = f32[100,2,640]{2,1,0:T(2,128)S(1)} collective-permute-done((f32[100,2,640]{2,1,0:T(2,128)S(1)}, f32[100,2,640]{2,1,0:T(2,128)S(1)}, u32[]{:S(2)}, u32[]{:S(2)}) %collective-permute-start.7) | collective-permute-done | bytes 512032 | tf_op jit(solution)/shard_map/ppermute | solution.py:35
  46.2 1.4 %collective-permute-done.11.refs_5_ = f32[100,2,640]{2,1,0:T(2,128)S(1)} collective-permute-done((f32[100,2,640]{2,1,0:T(2,128)S(1)}, f32[100,2,640]{2,1,0:T(2,128)S(1)}, u32[]{:S(2)}, u32[]{:S(2)}) %collective-permute-start.11) | collective-permute-done | bytes 512032 | tf_op jit(solution)/shard_map/ppermute | solution.py:35
  47.6 2.3 %collective-permute-done.10.refs_4_ = f32[100,2,640]{2,1,0:T(2,128)S(1)} collective-permute-done((f32[100,2,640]{2,1,0:T(2,128)S(1)}, f32[100,2,640]{2,1,0:T(2,128)S(1)}, u32[]{:S(2)}, u32[]{:S(2)}) %collective-permute-start.10) | collective-permute-done | bytes 512032 | tf_op jit(solution)/shard_map/ppermute | solution.py:35
  49.9 0.8 copy-done.19
  50.7 0.4 pad_maximum_fusion.1
  51.1 1.9 %collective-permute-start.14 = (f32[200,2,640]{2,1,0:T(2,128)S(1)}, f32[200,2,640]{2,1,0:T(2,128)S(1)}, u32[]{:S(2)}, u32[]{:S(2)}) collective-permute-start(f32[200,2,640]{2,1,0:T(2,128)S(1)} %pad_maximum_fusion.1), channel_id=1, source_target_pairs={{0,1},{1,0},{2,3},{3,2},{4,5},{5,4},{6,7},{7,6},{8,9},{9,8},{10,11... | collective-permute-start | bytes 3072008 | tf_op jit(solution)/shard_map/ppermute | solution.py:35
  53.1 0.4 pad_maximum_fusion
  53.5 0.1 collective-permute-start.13
  53.6 0.9 collective-permute-start.12
  54.5 2.5 %collective-permute-start.18 = (f32[100,2,640]{2,1,0:T(2,128)S(1)}, f32[100,2,640]{2,1,0:T(2,128)S(1)}, u32[]{:S(2)}, u32[]{:S(2)}) collective-permute-start(f32[100,2,640]{2,1,0:T(2,128)S(1)} %collective-permute-done.5.refs_2_), channel_id=1, source_target_pairs={{0,32},{1,97},{2,34},{3,99},{4,36},{5,101},{6,38},{7,103},{8,40},{... | collective-permute-start | bytes 1536008 | tf_op jit(solution)/shard_map/ppermute | solution.py:35
  57.1 0.0 collective-permute-start.19
  57.1 4.9 %collective-permute-done.12.refs_2_ = f32[100,2,640]{2,1,0:T(2,128)S(1)} collective-permute-done((f32[100,2,640]{2,1,0:T(2,128)S(1)}, f32[100,2,640]{2,1,0:T(2,128)S(1)}, u32[]{:S(2)}, u32[]{:S(2)}) %collective-permute-start.12) | collective-permute-done | bytes 512032 | tf_op jit(solution)/shard_map/ppermute | solution.py:35
  62.0 0.0 collective-permute-done.14.refs_13_
  62.0 0.0 collective-permute-done.13.refs_12_
  62.0 0.0 copy-start.6
  62.0 0.1 collective-permute-start.17
  62.1 0.1 collective-permute-start.16
  62.2 2.9 %collective-permute-start.15 = (f32[100,2,640]{2,1,0:T(2,128)S(1)}, f32[100,2,640]{2,1,0:T(2,128)S(1)}, u32[]{:S(2)}, u32[]{:S(2)}) collective-permute-start(f32[100,2,640]{2,1,0:T(2,128)S(1)} %collective-permute-done.7.refs_9_), channel_id=1, source_target_pairs={{0,4},{1,13},{2,6},{3,15},{4,8},{5,1},{6,10},{7,3},{8,12},{9,5},{1... | collective-permute-start | bytes 1536008 | tf_op jit(solution)/shard_map/ppermute | solution.py:35
  65.1 3.1 %collective-permute-done.18.refs_6_ = f32[100,2,640]{2,1,0:T(2,128)S(1)} collective-permute-done((f32[100,2,640]{2,1,0:T(2,128)S(1)}, f32[100,2,640]{2,1,0:T(2,128)S(1)}, u32[]{:S(2)}, u32[]{:S(2)}) %collective-permute-start.18) | collective-permute-done | bytes 512032 | tf_op jit(solution)/shard_map/ppermute | solution.py:35
  68.2 0.8 copy-done.20
  69.0 0.3 collective-permute-done.19.refs_7_
  69.3 0.0 copy-done.1
  69.3 0.0 copy-done.16
  69.4 14.5 %shard_map.28 = (f32[4,640,1280]{2,1,0:T(8,128)S(1)}, bf16[1280,1280]{1,0:T(8,128)(2,1)S(1)}) custom-call(f32[100,2,640]{2,1,0:T(2,128)} %copy-done.1, f32[100,2,640]{2,1,0:T(2,128)} %copy-done.17, f32[100,2,640]{2,1,0:T(2,128)} %copy-done.16, f32[100,2,640]{2,1,0:T(2,128)} %copy-done.15, f32[100,2,640]{2,1,0:T(2,128)} %copy-done.19, ...), custom_call_target="tpu_custom_call" | custom-call | flops 1000000 | bytes 100000 | tf_op jit(solution)/shard_map/pallas_call | solution.py:201
  83.9 0.0 collective-permute-done.17.refs_3_
  83.9 0.0 copy-start.8
  83.9 0.0 collective-permute-done.16.refs_1_
  83.9 0.0 collective-permute-done.15.refs_0_
  83.9 0.1 collective-permute-start.21
  84.0 0.5 collective-permute-start.20
  84.5 0.1 collective-permute-start.22
  84.6 0.4 collective-permute-start.23
  85.0 0.9 collective-permute-done.21.refs_5_
  85.9 0.7 collective-permute-done.20.refs_4_
  86.6 0.7 collective-permute-done.22.refs_6_
  87.4 0.7 collective-permute-done.23.refs_7_
  88.2 0.0 copy-done.13
  88.2 0.7 copy-done.14
  88.9 15.0 %shard_map.29 = f32[4,640,2,640]{3,2,1,0:T(2,128)} custom-call(f32[100,2,640]{2,1,0:T(2,128)} %copy-done.10, f32[100,2,640]{2,1,0:T(2,128)} %copy-done.9, f32[100,2,640]{2,1,0:T(2,128)} %copy-done.7, f32[100,2,640]{2,1,0:T(2,128)} %copy-done.8, f32[100,2,640]{2,1,0:T(2,128)} %copy-done.12, f32[100,2,640]{2,1,0:T(2,128)} %copy-done.11, ...), custom_call_target="tpu_custom_call" | custom-call | flops 8388608000 | bytes 34000000 | tf_op jit(solution)/shard_map/pallas_call | solution.py:224
  (33 shorter events, 0.1 us)
Async XLA Ops:
  0.0 14.9 %collective-permute-start = (f32[50,2,640]{2,1,0:T(2,128)}, f32[50,2,640]{2,1,0:T(2,128)S(1)}, u32[]{:S(2)}, u32[]{:S(2)}) collective-permute-start(f32[50,2,640]{2,1,0:T(2,128)} %bitcast.4), channel_id=1, source_target_pairs={{0,0},{1,1},{2,2},{3,3},{4,4},{5,5},{6,6},{7,7},{8,8},{9,9},{10,10... | collective-permute-start | bytes 768008 | tf_op jit(solution)/shard_map/ppermute | solution.py:35
  1.6 13.3 %collective-permute-start.1 = (f32[50,2,640]{2,1,0:T(2,128)}, f32[50,2,640]{2,1,0:T(2,128)S(1)}, u32[]{:S(2)}, u32[]{:S(2)}) collective-permute-start(f32[50,2,640]{2,1,0:T(2,128)} %bitcast.6), channel_id=1, source_target_pairs={{0,8},{1,9},{2,10},{3,11},{4,12},{5,13},{6,14},{7,15},{8,0},{9,1},... | collective-permute-start | bytes 768008 | tf_op jit(solution)/shard_map/ppermute | solution.py:35
  8.5 60.7 %copy-start.1 = (f32[100,2,640]{2,1,0:T(2,128)}, f32[100,2,640]{2,1,0:T(2,128)S(1)}, u32[]{:S(2)}) copy-start(f32[100,2,640]{2,1,0:T(2,128)S(1)} %pad_maximum_fusion.2.refs_0_) | copy-start | bytes 1536004
  8.5 22.7 %collective-permute-start.6 = (f32[100,2,640]{2,1,0:T(2,128)S(1)}, f32[100,2,640]{2,1,0:T(2,128)S(1)}, u32[]{:S(2)}, u32[]{:S(2)}) collective-permute-start(f32[100,2,640]{2,1,0:T(2,128)S(1)} %pad_maximum_fusion.2.refs_0_), channel_id=1, source_target_pairs={{0,96},{1,33},{2,98},{3,35},{4,100},{5,37},{6,102},{7,39},{8,104},... | collective-permute-start | bytes 1536008 | tf_op jit(solution)/shard_map/ppermute | solution.py:35
  10.0 21.3 %collective-permute-start.5 = (f32[100,2,640]{2,1,0:T(2,128)S(1)}, f32[100,2,640]{2,1,0:T(2,128)S(1)}, u32[]{:S(2)}, u32[]{:S(2)}) collective-permute-start(f32[100,2,640]{2,1,0:T(2,128)S(1)} %pad_maximum_fusion.2.refs_0_), channel_id=1, source_target_pairs={{0,32},{1,97},{2,34},{3,99},{4,36},{5,101},{6,38},{7,103},{8,40},{... | collective-permute-start | bytes 1536008 | tf_op jit(solution)/shard_map/ppermute | solution.py:35
  11.3 20.0 %collective-permute-start.4 = (f32[100,2,640]{2,1,0:T(2,128)S(1)}, f32[100,2,640]{2,1,0:T(2,128)S(1)}, u32[]{:S(2)}, u32[]{:S(2)}) collective-permute-start(f32[100,2,640]{2,1,0:T(2,128)S(1)} %pad_maximum_fusion.2.refs_0_), channel_id=1, source_target_pairs={{0,16},{1,17},{2,18},{3,19},{4,20},{5,21},{6,22},{7,23},{8,24},{9,... | collective-permute-start | bytes 1536008 | tf_op jit(solution)/shard_map/ppermute | solution.py:35
  14.9 4.2 %collective-permute-start.2 = (f32[50,2,640]{2,1,0:T(2,128)S(1)}, f32[50,2,640]{2,1,0:T(2,128)S(1)}, u32[]{:S(2)}, u32[]{:S(2)}) collective-permute-start(f32[50,2,640]{2,1,0:T(2,128)S(1)} %collective-permute-done), channel_id=1, source_target_pairs={{0,0},{1,1},{2,16},{3,17},{4,36},{5,37},{6,52},{7,53},{8,72},{9,73... | collective-permute-start | bytes 768008 | tf_op jit(solution)/shard_map/ppermute | solution.py:35
  15.6 15.7 %collective-permute-start.3 = (f32[50,2,640]{2,1,0:T(2,128)S(1)}, f32[50,2,640]{2,1,0:T(2,128)S(1)}, u32[]{:S(2)}, u32[]{:S(2)}) collective-permute-start(f32[50,2,640]{2,1,0:T(2,128)S(1)} %collective-permute-done.1), channel_id=1, source_target_pairs={{0,66},{1,67},{2,82},{3,83},{4,102},{5,103},{6,118},{7,119},{8,10}... | collective-permute-start | bytes 768008 | tf_op jit(solution)/shard_map/ppermute | solution.py:35
  31.3 38.0 %copy-start.15 = (f32[100,2,640]{2,1,0:T(2,128)}, f32[100,2,640]{2,1,0:T(2,128)S(1)}, u32[]{:S(2)}) copy-start(f32[100,2,640]{2,1,0:T(2,128)S(1)} %collective-permute-done.6.refs_3_) | copy-start | bytes 1536004
  31.3 38.0 %copy-start.16 = (f32[100,2,640]{2,1,0:T(2,128)}, f32[100,2,640]{2,1,0:T(2,128)S(1)}, u32[]{:S(2)}) copy-start(f32[100,2,640]{2,1,0:T(2,128)S(1)} %collective-permute-done.5.refs_2_) | copy-start | bytes 1536004
  31.3 38.0 %copy-start.17 = (f32[100,2,640]{2,1,0:T(2,128)}, f32[100,2,640]{2,1,0:T(2,128)S(1)}, u32[]{:S(2)}) copy-start(f32[100,2,640]{2,1,0:T(2,128)S(1)} %collective-permute-done.4.refs_1_) | copy-start | bytes 1536004
  31.4 37.9 %copy-start = (f32[100,2,640]{2,1,0:T(2,128)}, f32[100,2,640]{2,1,0:T(2,128)S(1)}, u32[]{:S(2)}) copy-start(f32[100,2,640]{2,1,0:T(2,128)S(1)} %constant_dynamic-update-slice_fusion.refs_8_) | copy-start | bytes 1536004
  31.4 9.3 %collective-permute-start.9 = (f32[100,2,640]{2,1,0:T(2,128)S(1)}, f32[100,2,640]{2,1,0:T(2,128)S(1)}, u32[]{:S(2)}, u32[]{:S(2)}) collective-permute-start(f32[100,2,640]{2,1,0:T(2,128)S(1)} %constant_dynamic-update-slice_fusion.refs_8_), channel_id=1, source_target_pairs={{0,12},{1,5},{2,14},{3,7},{4,0},{5,9},{6,2},{7,11},{8,4},{9,13},{1... | collective-permute-start | bytes 1536008 | tf_op jit(solution)/shard_map/ppermute | solution.py:35
  31.5 11.6 %collective-permute-start.8 = (f32[100,2,640]{2,1,0:T(2,128)S(1)}, f32[100,2,640]{2,1,0:T(2,128)S(1)}, u32[]{:S(2)}, u32[]{:S(2)}) collective-permute-start(f32[100,2,640]{2,1,0:T(2,128)S(1)} %constant_dynamic-update-slice_fusion.refs_8_), channel_id=1, source_target_pairs={{0,4},{1,13},{2,6},{3,15},{4,8},{5,1},{6,10},{7,3},{8,12},{9,5},{1... | collective-permute-start | bytes 1536008 | tf_op jit(solution)/shard_map/ppermute | solution.py:35
  34.4 11.8 %collective-permute-start.7 = (f32[100,2,640]{2,1,0:T(2,128)S(1)}, f32[100,2,640]{2,1,0:T(2,128)S(1)}, u32[]{:S(2)}, u32[]{:S(2)}) collective-permute-start(f32[100,2,640]{2,1,0:T(2,128)S(1)} %constant_dynamic-update-slice_fusion.refs_8_), channel_id=1, source_target_pairs={{0,2},{1,3},{2,0},{3,1},{4,6},{5,7},{6,4},{7,5},{8,10},{9,11},{10,... | collective-permute-start | bytes 1536008 | tf_op jit(solution)/shard_map/ppermute | solution.py:35
  36.5 11.1 %collective-permute-start.11 = (f32[100,2,640]{2,1,0:T(2,128)S(1)}, f32[100,2,640]{2,1,0:T(2,128)S(1)}, u32[]{:S(2)}, u32[]{:S(2)}) collective-permute-start(f32[100,2,640]{2,1,0:T(2,128)S(1)} %collective-permute-done.4.refs_1_), channel_id=1, source_target_pairs={{0,96},{1,33},{2,98},{3,35},{4,100},{5,37},{6,102},{7,39},{8,104},... | collective-permute-start | bytes 1536008 | tf_op jit(solution)/shard_map/ppermute | solution.py:35
  37.3 12.6 %collective-permute-start.10 = (f32[100,2,640]{2,1,0:T(2,128)S(1)}, f32[100,2,640]{2,1,0:T(2,128)S(1)}, u32[]{:S(2)}, u32[]{:S(2)}) collective-permute-start(f32[100,2,640]{2,1,0:T(2,128)S(1)} %collective-permute-done.4.refs_1_), channel_id=1, source_target_pairs={{0,32},{1,97},{2,34},{3,99},{4,36},{5,101},{6,38},{7,103},{8,40},{... | collective-permute-start | bytes 1536008 | tf_op jit(solution)/shard_map/ppermute | solution.py:35
  40.8 28.5 %copy-start.3 = (f32[100,2,640]{2,1,0:T(2,128)}, f32[100,2,640]{2,1,0:T(2,128)S(1)}, u32[]{:S(2)}) copy-start(f32[100,2,640]{2,1,0:T(2,128)S(1)} %collective-permute-done.9.refs_11_) | copy-start | bytes 1536004
  43.1 26.2 %copy-start.4 = (f32[100,2,640]{2,1,0:T(2,128)}, f32[100,2,640]{2,1,0:T(2,128)S(1)}, u32[]{:S(2)}) copy-start(f32[100,2,640]{2,1,0:T(2,128)S(1)} %collective-permute-done.8.refs_10_) | copy-start | bytes 1536004
  46.2 23.1 %copy-start.2 = (f32[100,2,640]{2,1,0:T(2,128)}, f32[100,2,640]{2,1,0:T(2,128)S(1)}, u32[]{:S(2)}) copy-start(f32[100,2,640]{2,1,0:T(2,128)S(1)} %collective-permute-done.7.refs_9_) | copy-start | bytes 1536004
  47.6 21.8 %copy-start.18 = (f32[100,2,640]{2,1,0:T(2,128)}, f32[100,2,640]{2,1,0:T(2,128)S(1)}, u32[]{:S(2)}) copy-start(f32[100,2,640]{2,1,0:T(2,128)S(1)} %collective-permute-done.11.refs_5_) | copy-start | bytes 1536004
  49.9 0.8 copy-start.19
  51.1 10.8 %collective-permute-start.14 = (f32[200,2,640]{2,1,0:T(2,128)S(1)}, f32[200,2,640]{2,1,0:T(2,128)S(1)}, u32[]{:S(2)}, u32[]{:S(2)}) collective-permute-start(f32[200,2,640]{2,1,0:T(2,128)S(1)} %pad_maximum_fusion.1), channel_id=1, source_target_pairs={{0,1},{1,0},{2,3},{3,2},{4,5},{5,4},{6,7},{7,6},{8,9},{9,8},{10,11... | collective-permute-start | bytes 3072008 | tf_op jit(solution)/shard_map/ppermute | solution.py:35
  53.5 8.5 %collective-permute-start.13 = (f32[200,2,640]{2,1,0:T(2,128)S(1)}, f32[200,2,640]{2,1,0:T(2,128)S(1)}, u32[]{:S(2)}, u32[]{:S(2)}) collective-permute-start(f32[200,2,640]{2,1,0:T(2,128)S(1)} %pad_maximum_fusion), channel_id=1, source_target_pairs={{0,1},{1,0},{2,3},{3,2},{4,5},{5,4},{6,7},{7,6},{8,9},{9,8},{10,11... | collective-permute-start | bytes 3072008 | tf_op jit(solution)/shard_map/ppermute | solution.py:35
  53.6 8.4 %collective-permute-start.12 = (f32[100,2,640]{2,1,0:T(2,128)S(1)}, f32[100,2,640]{2,1,0:T(2,128)S(1)}, u32[]{:S(2)}, u32[]{:S(2)}) collective-permute-start(f32[100,2,640]{2,1,0:T(2,128)S(1)} %collective-permute-done.8.refs_10_), channel_id=1, source_target_pairs={{0,4},{1,13},{2,6},{3,15},{4,8},{5,1},{6,10},{7,3},{8,12},{9,5},{1... | collective-permute-start | bytes 1536008 | tf_op jit(solution)/shard_map/ppermute | solution.py:35
  54.5 13.6 %collective-permute-start.18 = (f32[100,2,640]{2,1,0:T(2,128)S(1)}, f32[100,2,640]{2,1,0:T(2,128)S(1)}, u32[]{:S(2)}, u32[]{:S(2)}) collective-permute-start(f32[100,2,640]{2,1,0:T(2,128)S(1)} %collective-permute-done.5.refs_2_), channel_id=1, source_target_pairs={{0,32},{1,97},{2,34},{3,99},{4,36},{5,101},{6,38},{7,103},{8,40},{... | collective-permute-start | bytes 1536008 | tf_op jit(solution)/shard_map/ppermute | solution.py:35
  57.1 12.2 %collective-permute-start.19 = (f32[100,2,640]{2,1,0:T(2,128)S(1)}, f32[100,2,640]{2,1,0:T(2,128)}, u32[]{:S(2)}, u32[]{:S(2)}) collective-permute-start(f32[100,2,640]{2,1,0:T(2,128)S(1)} %collective-permute-done.11.refs_5_), channel_id=1, source_target_pairs={{0,96},{1,33},{2,98},{3,35},{4,100},{5,37},{6,102},{7,39},{8,104},... | collective-permute-start | bytes 1536008 | tf_op jit(solution)/shard_map/ppermute | solution.py:35
  62.0 26.1 %copy-start.7 = (f32[100,2,640]{2,1,0:T(2,128)}, f32[100,2,640]{2,1,0:T(2,128)S(1)}, u32[]{:S(2)}) copy-start(f32[100,2,640]{2,1,0:T(2,128)S(1)} %collective-permute-done.12.refs_2_) | copy-start | bytes 1536004
  62.0 7.4 %copy-start.5 = (f32[200,2,640]{2,1,0:T(2,128)}, f32[200,2,640]{2,1,0:T(2,128)S(1)}, u32[]{:S(2)}) copy-start(f32[200,2,640]{2,1,0:T(2,128)S(1)} %collective-permute-done.14.refs_13_) | copy-start | bytes 3072004
  62.0 7.4 %copy-start.6 = (f32[200,2,640]{2,1,0:T(2,128)}, f32[200,2,640]{2,1,0:T(2,128)S(1)}, u32[]{:S(2)}) copy-start(f32[200,2,640]{2,1,0:T(2,128)S(1)} %collective-permute-done.13.refs_12_) | copy-start | bytes 3072004
  62.0 21.9 %collective-permute-start.17 = (f32[100,2,640]{2,1,0:T(2,128)S(1)}, f32[100,2,640]{2,1,0:T(2,128)S(1)}, u32[]{:S(2)}, u32[]{:S(2)}) collective-permute-start(f32[100,2,640]{2,1,0:T(2,128)S(1)} %collective-permute-done.12.refs_2_), channel_id=1, source_target_pairs={{0,2},{1,3},{2,0},{3,1},{4,6},{5,7},{6,4},{7,5},{8,10},{9,11},{10,... | collective-permute-start | bytes 1536008 | tf_op jit(solution)/shard_map/ppermute | solution.py:35
  62.1 21.8 %collective-permute-start.16 = (f32[100,2,640]{2,1,0:T(2,128)S(1)}, f32[100,2,640]{2,1,0:T(2,128)S(1)}, u32[]{:S(2)}, u32[]{:S(2)}) collective-permute-start(f32[100,2,640]{2,1,0:T(2,128)S(1)} %collective-permute-done.7.refs_9_), channel_id=1, source_target_pairs={{0,12},{1,5},{2,14},{3,7},{4,0},{5,9},{6,2},{7,11},{8,4},{9,13},{1... | collective-permute-start | bytes 1536008 | tf_op jit(solution)/shard_map/ppermute | solution.py:35
  62.2 21.7 %collective-permute-start.15 = (f32[100,2,640]{2,1,0:T(2,128)S(1)}, f32[100,2,640]{2,1,0:T(2,128)S(1)}, u32[]{:S(2)}, u32[]{:S(2)}) collective-permute-start(f32[100,2,640]{2,1,0:T(2,128)S(1)} %collective-permute-done.7.refs_9_), channel_id=1, source_target_pairs={{0,4},{1,13},{2,6},{3,15},{4,8},{5,1},{6,10},{7,3},{8,12},{9,5},{1... | collective-permute-start | bytes 1536008 | tf_op jit(solution)/shard_map/ppermute | solution.py:35
  68.2 0.8 copy-start.20
  83.9 4.2 %copy-start.8 = (f32[100,2,640]{2,1,0:T(2,128)}, f32[100,2,640]{2,1,0:T(2,128)S(1)}, u32[]{:S(2)}) copy-start(f32[100,2,640]{2,1,0:T(2,128)S(1)} %collective-permute-done.17.refs_3_) | copy-start | bytes 1536004
  83.9 4.2 %copy-start.9 = (f32[100,2,640]{2,1,0:T(2,128)}, f32[100,2,640]{2,1,0:T(2,128)S(1)}, u32[]{:S(2)}) copy-start(f32[100,2,640]{2,1,0:T(2,128)S(1)} %collective-permute-done.16.refs_1_) | copy-start | bytes 1536004
  83.9 4.2 %copy-start.10 = (f32[100,2,640]{2,1,0:T(2,128)}, f32[100,2,640]{2,1,0:T(2,128)S(1)}, u32[]{:S(2)}) copy-start(f32[100,2,640]{2,1,0:T(2,128)S(1)} %collective-permute-done.15.refs_0_) | copy-start | bytes 1536004
  83.9 2.0 %collective-permute-start.21 = (f32[100,2,640]{2,1,0:T(2,128)S(1)}, f32[100,2,640]{2,1,0:T(2,128)S(1)}, u32[]{:S(2)}, u32[]{:S(2)}) collective-permute-start(f32[100,2,640]{2,1,0:T(2,128)S(1)} %collective-permute-done.15.refs_0_), channel_id=1, source_target_pairs={{0,1},{1,0},{2,3},{3,2},{4,5},{5,4},{6,7},{7,6},{8,9},{9,8},{10,11... | collective-permute-start | bytes 1536008 | tf_op jit(solution)/shard_map/ppermute | solution.py:35
  84.0 2.6 %collective-permute-start.20 = (f32[100,2,640]{2,1,0:T(2,128)S(1)}, f32[100,2,640]{2,1,0:T(2,128)S(1)}, u32[]{:S(2)}, u32[]{:S(2)}) collective-permute-start(f32[100,2,640]{2,1,0:T(2,128)S(1)} %collective-permute-done.16.refs_1_), channel_id=1, source_target_pairs={{0,1},{1,0},{2,3},{3,2},{4,5},{5,4},{6,7},{7,6},{8,9},{9,8},{10,11... | collective-permute-start | bytes 1536008 | tf_op jit(solution)/shard_map/ppermute | solution.py:35
  84.5 2.8 %collective-permute-start.22 = (f32[100,2,640]{2,1,0:T(2,128)S(1)}, f32[100,2,640]{2,1,0:T(2,128)S(1)}, u32[]{:S(2)}, u32[]{:S(2)}) collective-permute-start(f32[100,2,640]{2,1,0:T(2,128)S(1)} %collective-permute-done.12.refs_2_), channel_id=1, source_target_pairs={{0,1},{1,0},{2,3},{3,2},{4,5},{5,4},{6,7},{7,6},{8,9},{9,8},{10,11... | collective-permute-start | bytes 1536008 | tf_op jit(solution)/shard_map/ppermute | solution.py:35
  84.6 3.5 %collective-permute-start.23 = (f32[100,2,640]{2,1,0:T(2,128)S(1)}, f32[100,2,640]{2,1,0:T(2,128)S(1)}, u32[]{:S(2)}, u32[]{:S(2)}) collective-permute-start(f32[100,2,640]{2,1,0:T(2,128)S(1)} %collective-permute-done.17.refs_3_), channel_id=1, source_target_pairs={{0,1},{1,0},{2,3},{3,2},{4,5},{5,4},{6,7},{7,6},{8,9},{9,8},{10,11... | collective-permute-start | bytes 1536008 | tf_op jit(solution)/shard_map/ppermute | solution.py:35
  85.9 2.2 %copy-start.11 = (f32[100,2,640]{2,1,0:T(2,128)}, f32[100,2,640]{2,1,0:T(2,128)S(1)}, u32[]{:S(2)}) copy-start(f32[100,2,640]{2,1,0:T(2,128)S(1)} %collective-permute-done.21.refs_5_) | copy-start | bytes 1536004
  86.6 1.5 %copy-start.12 = (f32[100,2,640]{2,1,0:T(2,128)}, f32[100,2,640]{2,1,0:T(2,128)S(1)}, u32[]{:S(2)}) copy-start(f32[100,2,640]{2,1,0:T(2,128)S(1)} %collective-permute-done.20.refs_4_) | copy-start | bytes 1536004
  87.4 0.8 copy-start.13
  88.1 0.8 copy-start.14

commit v3 on v2

v3 whole, which is shorter than its diff:
```python
import jax
import jax.numpy as jnp
from jax import lax
from jax.experimental import pallas as pl
from jax.experimental.pallas import tpu as pltpu
from jax.sharding import PartitionSpec as P

AXES = ("row", "col")
HALF = 50
GROUP = 4
PARTIAL = 2 * GROUP * HALF
MAIN = PARTIAL // 128 * 128
REST = PARTIAL - MAIN
DEPTH = 3 * MAIN + 128
WIDTH = 640
LANES = 128
CUTS = WIDTH // LANES


def flat(x, z, y, low, core):
    return ((x % 4) * 2 + z % 2) * 16 + ((y % 4) * 2 + low % 2) * 2 + core % 2


def permute(value, move):
    pairs = []
    for x in range(4):
        for z in range(2):
            for y in range(4):
                for low in range(2):
                    for core in range(2):
                        pairs.append((flat(x, z, y, low, core), flat(*move(x, z, y, low, core))))
    return lax.ppermute(value, AXES, pairs)


def together(*values):
    return lax.optimization_barrier(values)


def split(value):
    high = value.astype(jnp.bfloat16)
    return high, (value - high.astype(jnp.float32)).astype(jnp.bfloat16)


def dot(a, b):
    return jnp.dot(a, b, preferred_element_type=jnp.float32)


def fetch(ref, half, target, at, cut, sem):
    return pltpu.make_async_copy(
        ref.at[pl.ds(half * HALF, HALF), :, pl.ds(cut * LANES, LANES)],
        target.at[cut, pl.ds(at, HALF)],
        sem,
    )


def fetch_lefts(refs, target, sems):
    copies = []
    for cut in range(CUTS):
        for half in range(2):
            for n, ref in enumerate(refs):
                at = half * GROUP * HALF + n * HALF
                copies.append(fetch(ref, half, target, at, cut, sems.at[cut, half, n]))
    return copies


def fill_right(source, first, target):
    for cut in range(CUTS):
        for j in range(2):
            cols = pl.ds((cut * 2 + j) * LANES, LANES)
            for k in range(0, MAIN, LANES):
                high, rest = split(source[cut, pl.ds((first + k) * 2 + j, LANES, stride=2), :])
                target[pl.ds(k, LANES), cols] = high
                target[pl.ds(MAIN + k, LANES), cols] = rest
                target[pl.ds(2 * MAIN + k, LANES), cols] = high
            high, rest = split(source[cut, pl.ds((first + MAIN) * 2 + j, REST, stride=2), :])
            target[pl.ds(3 * MAIN, REST), cols] = high
            target[pl.ds(3 * MAIN + REST, REST), cols] = rest
            target[pl.ds(3 * MAIN + 2 * REST, REST), cols] = high
            target[pl.ds(3 * MAIN + 3 * REST, 128 - 3 * REST), cols] = jnp.zeros((128 - 3 * REST, LANES), jnp.bfloat16)


def fill_left(source, j, cut, target):
    rows = pl.ds(cut * LANES, LANES)
    for k in range(0, MAIN, LANES):
        high, rest = split(source[cut, pl.ds(k * 2 + j, LANES, stride=2), :].T)
        target[rows, pl.ds(k, LANES)] = high
        target[rows, pl.ds(MAIN + k, LANES)] = high
        target[rows, pl.ds(2 * MAIN + k, LANES)] = rest
    value = source[cut, pl.ds(MAIN * 2 + j, REST, stride=2), :]
    high = value.astype(jnp.bfloat16).astype(jnp.float32)
    pad = jnp.zeros((128 - 3 * REST, LANES), jnp.float32)
    stack = jnp.concatenate([high, high, value - high, pad], axis=0)
    target[rows, pl.ds(3 * MAIN, LANES)] = stack.T.astype(jnp.bfloat16)


def fill_all(source, j, target):
    for cut in range(CUTS):
        fill_left(source, j, cut, target)


def places(z, x, way):
    return [(x, z), (x, z + 1), (x - way, z), (x + way, z),
            (x - way, z + 1), (x + way, z + 1), (x + 2, z), (x + 2, z + 1)]


def fetch_rights(refs, chosen, target, sems):
    row, col = lax.axis_index("row"), lax.axis_index("col")
    x, z = row // 2, row % 2
    y, low, core = col // 4, (col // 2) % 2, col % 2
    way = 1 - 2 * core
    copies = []
    for half in range(2):
        for m, (ref, n) in enumerate(zip(refs, chosen)):
            a, b = places(z, x, way)[n]
            delta = (a - (y - x + 2 * half) + 16) % 4
            other = (b + low + half) % 2
            side = jnp.where(delta == (4 - way) % 4, 2, 3) + 2 * other
            n = jnp.where(delta == 0, other, jnp.where(delta == 2, 6 + other, side))
            at = (n // GROUP) * PARTIAL + half * GROUP * HALF + (n % GROUP) * HALF
            for cut in range(CUTS):
                copies.append(fetch(ref, half, target, at, cut, sems.at[cut, half, m]))
    return copies


def prepare(*refs):
    js, mine = refs[:6], refs[6:10]
    right, held = refs[10:12]
    left, jsems, isems = refs[12:]
    lefts = fetch_lefts(mine, left, isems)
    rights = fetch_rights(js, range(6), right, jsems)
    for copy in lefts + rights:
        copy.start()
    for copy in lefts:
        copy.wait()
    for i in range(2):
        fill_all(left.reshape(CUTS, 2 * PARTIAL, LANES), i, held.at[i])
    for copy in rights:
        copy.wait()


def begin(je, jf, _, held, total, now, later, right, jsems):
    rights = fetch_rights([je, jf], (6, 7), right, jsems)
    for copy in rights:
        copy.start()
    for copy in rights:
        copy.wait()
    source = right.reshape(CUTS, 4 * PARTIAL, LANES)
    fill_right(source, 0, now)
    for i in range(2):
        total[i] = dot(held[i], now[...])
    fill_right(source, PARTIAL, later)


def scatter(out, side, stages, sums, sems):
    base = 2 * ((lax.axis_index("col") % 2 + side) % 2)
    flat_stages = [s.reshape(CUTS, 2 * WIDTH, LANES) for s in stages]

    def flush(i, cut):
        return pltpu.make_async_copy(
            stages[i].at[cut], out.at[base + i, :, :, pl.ds(cut * LANES, LANES)], sems.at[i, cut]
        )

    def store(i, cut):
        for j in range(2):
            value = sums[i][:, pl.ds((cut * 2 + j) * LANES, LANES)]
            flat_stages[i][cut, pl.ds(j, WIDTH, stride=2), :] = value

    return flush, store


def end(fill, product, flush, store):
    fill(0)
    product(0)
    fill(1)
    product(1)
    for cut in range(CUTS):
        store(0, cut)
    for cut in range(CUTS):
        flush(0, cut).start()
    for cut in range(CUTS):
        store(1, cut)
        flush(1, cut).start()
    for i in range(2):
        for cut in range(CUTS):
            flush(i, cut).wait()


def finish_own(*refs):
    pieces, total, later = refs[:4], refs[4], refs[5]
    out, left, even, odd, sums, other_sums, stage, other_stage, isems, osems = refs[6:]
    held, sums, stages = (even, odd), (sums, other_sums), (stage, other_stage)
    flush, store = scatter(out, 0, stages, sums, osems)
    lefts = fetch_lefts(pieces, left, isems)
    for copy in lefts:
        copy.start()
    for copy in lefts:
        copy.wait()
    source = left.reshape(CUTS, 2 * PARTIAL, LANES)

    def fill(i):
        fill_all(source, i, held[i])

    def product(i):
        sums[i][...] = dot(held[i][...], later[...]) + total[i]

    end(fill, product, flush, store)


def finish_other(*refs):
    early, pieces, now, later = refs[:2], refs[2:6], refs[6], refs[7]
    out, left, even, odd, next_even, next_odd, sums, other_sums, stage, other_stage, isems, osems = refs[9:]
    held, late_held = (even, odd), (next_even, next_odd)
    sums, stages = (sums, other_sums), (stage, other_stage)
    flush, store = scatter(out, 1, stages, sums, osems)
    first = [early[n // 2].at[pl.ds(n % 2 * 2 * HALF, 2 * HALF)] for n in (0, 1, 3, 2)]
    lefts = [fetch_lefts(first, left.at[0], isems.at[0]), fetch_lefts(pieces, left.at[1], isems.at[1])]
    for copy in lefts[0] + lefts[1]:
        copy.start()
    for copy in lefts[0]:
        copy.wait()
    sources = [left.at[h].reshape(CUTS, 2 * PARTIAL, LANES) for h in range(2)]
    fill_all(sources[0], 0, held[0])
    for copy in lefts[1]:
        copy.wait()
    sums[0][...] = dot(held[0][...], now[...])
    fill_all(sources[1], 0, late_held[0])
    sums[0][...] += dot(late_held[0][...], later[...])
    fill_all(sources[0], 1, held[1])
    sums[1][...] = dot(held[1][...], now[...])
    fill_all(sources[1], 1, late_held[1])
    sums[1][...] += dot(late_held[1][...], later[...])
    for i in range(2):
        for cut in range(CUTS):
            store(i, cut)
            flush(i, cut).start()
    for i in range(2):
        for cut in range(CUTS):
            flush(i, cut).wait()


ANY = pl.BlockSpec(memory_space=pl.ANY)
NEAR = pl.BlockSpec(memory_space=pltpu.VMEM)
WIDE = 10 * LANES
HELD = pltpu.VMEM((WIDTH, DEPTH), jnp.bfloat16)
LEFT = pltpu.VMEM((CUTS, PARTIAL, 2, LANES), jnp.float32)
LEFT_SEMS = pltpu.SemaphoreType.DMA((CUTS, 2, GROUP))
PANEL = pltpu.VMEM((DEPTH, WIDE), jnp.bfloat16)
SUMS = pltpu.VMEM((2, WIDTH, WIDE), jnp.float32)
HELDS = pltpu.VMEM((2, WIDTH, DEPTH), jnp.bfloat16)
RIGHT = pltpu.VMEM((CUTS, 2 * PARTIAL, 2, LANES), jnp.float32)
SUM = pltpu.VMEM((WIDTH, WIDE), jnp.float32)
STAGE = pltpu.VMEM((CUTS, WIDTH, 2, LANES), jnp.float32)
LIMIT = 28 * 1024 * 1024
COST = pl.CostEstimate(flops=10**6, bytes_accessed=10**5, transcendentals=0)


def near(value):
    return pltpu.with_memory_space_constraint(value, pltpu.VMEM)


def call(kernel, args, kinds, shapes, scratch, aliases=None):
    nears = [near(arg) if kind is NEAR else arg for arg, kind in zip(args, kinds)]
    outs = [NEAR if isinstance(shape, type(SUMS)) else ANY for shape in shapes]
    return pl.pallas_call(
        kernel,
        out_shape=tuple(shapes),
        in_specs=kinds,
        out_specs=tuple(outs),
        scratch_shapes=scratch,
        input_output_aliases=aliases or {},
        compiler_params=pltpu.CompilerParams(vmem_limit_bytes=LIMIT),
        cost_estimate=COST,
    )(*nears)


def prepare_call(js, mine):
    scratch = [LEFT, pltpu.SemaphoreType.DMA((CUTS, 2, 6)), LEFT_SEMS]
    return call(prepare, [*js, *mine], [ANY] * 10, [RIGHT, HELDS], scratch)


def begin_call(js, right, held):
    scratch = [pltpu.SemaphoreType.DMA((CUTS, 2, 2))]
    args = [*js, right, held]
    return call(begin, args, [ANY] * 2 + [NEAR] * 2, [SUMS, PANEL, PANEL, RIGHT], scratch, {2: 3})[:3]


OUT = jax.ShapeDtypeStruct((4, WIDTH, 2, WIDTH), jnp.float32)
OUT_SEMS = pltpu.SemaphoreType.DMA((2, CUTS))


def own_call(pieces, total, later):
    scratch = [LEFT, HELD, HELD, SUM, SUM, STAGE, STAGE, LEFT_SEMS, OUT_SEMS]
    return call(finish_own, [*pieces, total, later], [ANY] * 4 + [NEAR] * 2, [OUT], scratch)[0]


def other_call(early, pieces, now, later, out):
    scratch = [
        pltpu.VMEM((2, CUTS, PARTIAL, 2, LANES), jnp.float32),
        HELD, HELD, HELD, HELD, SUM, SUM, STAGE, STAGE,
        pltpu.SemaphoreType.DMA((2, CUTS, 2, GROUP)),
        OUT_SEMS,
    ]
    args = [*early, *pieces, now, later, out]
    return call(finish_other, args, [ANY] * 6 + [NEAR] * 2 + [ANY], [OUT], scratch, {8: 0})[0]


def shards(amplitude, coupling):
    amps = jnp.transpose(amplitude, (1, 2, 0, 3)).reshape(HALF, 2, WIDTH)
    ints = coupling.reshape(HALF, 2, WIDTH)
    block = jnp.concatenate([ints, amps], axis=0)

    def way(core):
        return 1 - 2 * core

    def right(x, z, y, low, core):
        return x + way(core), z, y, low, core

    def left(x, z, y, low, core):
        return x - way(core), z, y, low, core

    def up(x, z, y, low, core):
        return x, z, y + way(core), low, core

    def down(x, z, y, low, core):
        return x, z, y - way(core), low, core

    def beyond(x, z, y, low, core):
        return x, z, y, low + 1, core

    def tilt(value, shift):
        return permute(value, lambda x, z, y, low, core: (x, z, y + x + shift, low, core))

    def mirror(value, shift):
        return permute(
            value, lambda x, z, y, low, core: (y - x - shift, low, y, z + shift // 2, core)
        )

    def swap(value):
        return permute(value, lambda x, z, y, low, core: (x, z, y, low, core + 1))

    amps, ints, block = together(amps, ints, block)
    far = permute(block, lambda x, z, y, low, core: (x, z + 1, y, low, core))
    ta = tilt(amps, 0)
    tw = tilt(ints, 2)
    ja = permute(block, right)
    jb = permute(block, left)
    ta, tw = together(ta, tw)
    ma = mirror(ta, 0)
    mw = mirror(tw, 2)

    ma, mw, ja, jb, far = together(ma, mw, ja, jb, far)
    held = jnp.concatenate([ma, mw], axis=0)
    a = permute(held, up)
    b = permute(held, down)
    beside = permute(held, beyond)
    jc = permute(far, right)
    jd = permute(far, left)
    e = permute(a, up)

    ja, jc, jd = together(ja, jc, jd)
    je = permute(ja, right)
    jf = permute(jd, left)
    e, beside = together(e, beside)
    f = permute(e, beyond)
    c = permute(beside, up)
    d = permute(beside, down)

    panel, helds = prepare_call([block, far, ja, jb, jc, jd], [held, beside, a, b])
    own, now, later = begin_call([je, jf], panel, helds)
    held, beside, a, b, e, c, d, f, own = together(held, beside, a, b, e, c, d, f, own)
    early = [swap(jnp.concatenate([held, beside], axis=0)), swap(jnp.concatenate([a, b], axis=0))]
    late = [swap(v) for v in (d, c, e, f)]
    out = own_call([c, d, e, f], own, later)
    return other_call(early, late, now, later, out)


def solution(mesh):
    placed = (P("col", "row", None, None), P("row", None, "col", None))
    return jax.shard_map(
        shards, mesh=mesh, in_specs=placed, out_specs=P("row", None, "col", None), check_vma=False
    )
```

time: 104 us -> 95.7 us (0.920)
  waiting for transfers between devices: 34.2 us -> 24.7 us
  starting transfers between devices: 35.2 us -> 39.1 us
  local copies, waits for them, and re-layouts: 2.56 us -> 0.1 us
    ppermute x24, waiting for transfers between devices: 34.2 us -> 24.7 us  [permute(): return lax.ppermute(value, AXES, pairs)]
    ppermute x24, starting transfers between devices: 35.2 us -> 39.1 us  [permute(): return lax.ppermute(value, AXES, pairs)]
    unnamed x43 -> x1, local copies, waits for them, and re-layouts: 2.5 us -> 0.03 us
    pallas_call x2 -> x4, Pallas kernels: 29.5 us -> 29.1 us  [call(): pl.pallas_call(kernel, out_shape=tuple(shapes), in_specs=kinds, out_specs...]
  transfers between devices with their start and end apart: 24 -> 24, of which waited for: 13 -> 7; matrix products, arithmetic and copies ran while one was open for 2% -> 1% of each run, Pallas kernels for 14% -> 17%
where the time goes in v3:
time: 95.7 us; the launch traced here: 95.5 us
  starting transfers between devices  39.1 us (41%)
  Pallas kernels  29.1 us (30%)
  waiting for transfers between devices  24.7 us (26%)
  other arithmetic  2.17 us (2%)
    ppermute x24, starting transfers between devices, permute(): return lax.ppermute(value, AXES, pairs)  39.1 us
    pallas_call x4, Pallas kernels, call(): pl.pallas_call(kernel, out_shape=tuple(shapes), in_specs=kinds, out_specs...  29.1 us
    ppermute x24, waiting for transfers between devices, permute(): return lax.ppermute(value, AXES, pairs)  24.7 us
  transfers between devices with their start and end apart: 24, of which 7 were waited for; matrix products, arithmetic and copies ran while one was open for 1% of the time, Pallas kernels for 17%

profile of v3, /device:TPU:1, one launch (start us, length us, event | category | flops | bytes accessed | tf_op | source)
XLA Modules:
  0.0 95.5 jit_solution(13994409857167144930)
XLA Ops:
  0.0 1.3 %pad_maximum_fusion.2.refs_0_ = f32[100,2,640]{2,1,0:T(2,128)S(1)} fusion(f32[50,2,640]{2,1,0:T(2,128)} %bitcast.4, f32[50,2,640]{2,1,0:T(2,128)} %bitcast.6), kind=kLoop, calls=%fused_computation.2 | loop fusion | flops 128000 | bytes 1024000 | tf_op jit(solution)/shard_map/concatenate | solution.py:310
  1.3 1.6 %collective-permute-start = (f32[50,2,640]{2,1,0:T(2,128)}, f32[50,2,640]{2,1,0:T(2,128)S(1)}, u32[]{:S(2)}, u32[]{:S(2)}) collective-permute-start(f32[50,2,640]{2,1,0:T(2,128)} %bitcast.5), channel_id=1, source_target_pairs={{0,0},{1,1},{2,2},{3,3},{4,4},{5,5},{6,6},{7,7},{8,8},{9,9},{10,10... | collective-permute-start | bytes 768008 | tf_op jit(solution)/shard_map/ppermute | solution.py:32
  2.9 5.6 %collective-permute-start.1 = (f32[50,2,640]{2,1,0:T(2,128)}, f32[50,2,640]{2,1,0:T(2,128)S(1)}, u32[]{:S(2)}, u32[]{:S(2)}) collective-permute-start(f32[50,2,640]{2,1,0:T(2,128)} %bitcast.7), channel_id=1, source_target_pairs={{0,8},{1,9},{2,10},{3,11},{4,12},{5,13},{6,14},{7,15},{8,0},{9,1},... | collective-permute-start | bytes 768008 | tf_op jit(solution)/shard_map/ppermute | solution.py:32
  8.6 3.7 %collective-permute-start.6 = (f32[100,2,640]{2,1,0:T(2,128)S(1)}, f32[100,2,640]{2,1,0:T(2,128)S(1)}, u32[]{:S(2)}, u32[]{:S(2)}) collective-permute-start(f32[100,2,640]{2,1,0:T(2,128)S(1)} %pad_maximum_fusion.2.refs_0_), channel_id=1, source_target_pairs={{0,16},{1,17},{2,18},{3,19},{4,20},{5,21},{6,22},{7,23},{8,24},{9,... | collective-permute-start | bytes 1536008 | tf_op jit(solution)/shard_map/ppermute | solution.py:32
  12.2 1.4 %collective-permute-start.5 = (f32[100,2,640]{2,1,0:T(2,128)S(1)}, f32[100,2,640]{2,1,0:T(2,128)S(1)}, u32[]{:S(2)}, u32[]{:S(2)}) collective-permute-start(f32[100,2,640]{2,1,0:T(2,128)S(1)} %pad_maximum_fusion.2.refs_0_), channel_id=1, source_target_pairs={{0,96},{1,33},{2,98},{3,35},{4,100},{5,37},{6,102},{7,39},{8,104},... | collective-permute-start | bytes 1536008 | tf_op jit(solution)/shard_map/ppermute | solution.py:32
  13.6 1.3 %collective-permute-start.4 = (f32[100,2,640]{2,1,0:T(2,128)S(1)}, f32[100,2,640]{2,1,0:T(2,128)S(1)}, u32[]{:S(2)}, u32[]{:S(2)}) collective-permute-start(f32[100,2,640]{2,1,0:T(2,128)S(1)} %pad_maximum_fusion.2.refs_0_), channel_id=1, source_target_pairs={{0,32},{1,97},{2,34},{3,99},{4,36},{5,101},{6,38},{7,103},{8,40},{... | collective-permute-start | bytes 1536008 | tf_op jit(solution)/shard_map/ppermute | solution.py:32
  14.9 0.0 collective-permute-done
  14.9 0.0 collective-permute-done.1
  14.9 0.7 collective-permute-start.2
  15.6 4.9 %collective-permute-start.3 = (f32[50,2,640]{2,1,0:T(2,128)S(1)}, f32[50,2,640]{2,1,0:T(2,128)S(1)}, u32[]{:S(2)}, u32[]{:S(2)}) collective-permute-start(f32[50,2,640]{2,1,0:T(2,128)S(1)} %collective-permute-done.1), channel_id=1, source_target_pairs={{0,66},{1,67},{2,82},{3,83},{4,102},{5,103},{6,118},{7,119},{8,10}... | collective-permute-start | bytes 768008 | tf_op jit(solution)/shard_map/ppermute | solution.py:32
  20.5 0.0 collective-permute-done.2
  20.5 11.0 %collective-permute-done.3 = f32[50,2,640]{2,1,0:T(2,128)S(1)} collective-permute-done((f32[50,2,640]{2,1,0:T(2,128)S(1)}, f32[50,2,640]{2,1,0:T(2,128)S(1)}, u32[]{:S(2)}, u32[]{:S(2)}) %collective-permute-start.3) | collective-permute-done | bytes 256032 | tf_op jit(solution)/shard_map/ppermute | solution.py:32
  31.5 0.0 collective-permute-done.6.refs_1_
  31.5 0.0 collective-permute-done.5.refs_3_
  31.5 0.0 collective-permute-done.4.refs_2_
  31.6 0.1 constant_dynamic-update-slice_fusion.refs_6_
  31.7 1.0 %collective-permute-start.7 = (f32[100,2,640]{2,1,0:T(2,128)S(1)}, f32[100,2,640]{2,1,0:T(2,128)S(1)}, u32[]{:S(2)}, u32[]{:S(2)}) collective-permute-start(f32[100,2,640]{2,1,0:T(2,128)S(1)} %constant_dynamic-update-slice_fusion.refs_6_), channel_id=1, source_target_pairs={{0,4},{1,13},{2,6},{3,15},{4,8},{5,1},{6,10},{7,3},{8,12},{9,5},{1... | collective-permute-start | bytes 1536008 | tf_op jit(solution)/shard_map/ppermute | solution.py:32
  32.7 3.5 %collective-permute-start.15 = (f32[100,2,640]{2,1,0:T(2,128)S(1)}, f32[100,2,640]{2,1,0:T(2,128)S(1)}, u32[]{:S(2)}, u32[]{:S(2)}) collective-permute-start(f32[100,2,640]{2,1,0:T(2,128)S(1)} %collective-permute-done.6.refs_1_), channel_id=1, source_target_pairs={{0,96},{1,33},{2,98},{3,35},{4,100},{5,37},{6,102},{7,39},{8,104},... | collective-permute-start | bytes 1536008 | tf_op jit(solution)/shard_map/ppermute | solution.py:32
  36.2 0.0 collective-permute-start.14
  36.2 1.8 %collective-permute-start.9 = (f32[100,2,640]{2,1,0:T(2,128)S(1)}, f32[100,2,640]{2,1,0:T(2,128)S(1)}, u32[]{:S(2)}, u32[]{:S(2)}) collective-permute-start(f32[100,2,640]{2,1,0:T(2,128)S(1)} %constant_dynamic-update-slice_fusion.refs_6_), channel_id=1, source_target_pairs={{0,2},{1,3},{2,0},{3,1},{4,6},{5,7},{6,4},{7,5},{8,10},{9,11},{10,... | collective-permute-start | bytes 1536008 | tf_op jit(solution)/shard_map/ppermute | solution.py:32
  38.0 1.9 %collective-permute-done.7.refs_8_ = f32[100,2,640]{2,1,0:T(2,128)S(1)} collective-permute-done((f32[100,2,640]{2,1,0:T(2,128)S(1)}, f32[100,2,640]{2,1,0:T(2,128)S(1)}, u32[]{:S(2)}, u32[]{:S(2)}) %collective-permute-start.7) | collective-permute-done | bytes 512032 | tf_op jit(solution)/shard_map/ppermute | solution.py:32
  39.9 1.9 %collective-permute-start.8 = (f32[100,2,640]{2,1,0:T(2,128)S(1)}, f32[100,2,640]{2,1,0:T(2,128)S(1)}, u32[]{:S(2)}, u32[]{:S(2)}) collective-permute-start(f32[100,2,640]{2,1,0:T(2,128)S(1)} %collective-permute-done.7.refs_8_), channel_id=1, source_target_pairs={{0,4},{1,13},{2,6},{3,15},{4,8},{5,1},{6,10},{7,3},{8,12},{9,5},{1... | collective-permute-start | bytes 1536008 | tf_op jit(solution)/shard_map/ppermute | solution.py:32
  41.8 0.0 collective-permute-start.10
  41.8 5.3 %collective-permute-done.15.refs_5_ = f32[100,2,640]{2,1,0:T(2,128)S(1)} collective-permute-done((f32[100,2,640]{2,1,0:T(2,128)S(1)}, f32[100,2,640]{2,1,0:T(2,128)S(1)}, u32[]{:S(2)}, u32[]{:S(2)}) %collective-permute-start.15) | collective-permute-done | bytes 512032 | tf_op jit(solution)/shard_map/ppermute | solution.py:32
  47.1 1.3 %collective-permute-done.14.refs_4_ = f32[100,2,640]{2,1,0:T(2,128)S(1)} collective-permute-done((f32[100,2,640]{2,1,0:T(2,128)S(1)}, f32[100,2,640]{2,1,0:T(2,128)S(1)}, u32[]{:S(2)}, u32[]{:S(2)}) %collective-permute-start.14) | collective-permute-done | bytes 512032 | tf_op jit(solution)/shard_map/ppermute | solution.py:32
  48.4 2.2 %collective-permute-start.16 = (f32[100,2,640]{2,1,0:T(2,128)S(1)}, f32[100,2,640]{2,1,0:T(2,128)S(1)}, u32[]{:S(2)}, u32[]{:S(2)}) collective-permute-start(f32[100,2,640]{2,1,0:T(2,128)S(1)} %collective-permute-done.4.refs_2_), channel_id=1, source_target_pairs={{0,32},{1,97},{2,34},{3,99},{4,36},{5,101},{6,38},{7,103},{8,40},{... | collective-permute-start | bytes 1536008 | tf_op jit(solution)/shard_map/ppermute | solution.py:32
  50.5 0.0 collective-permute-start.17
  50.5 0.0 collective-permute-done.9.refs_7_
  50.5 0.0 collective-permute-done.8.refs_2_
  50.5 2.3 %collective-permute-start.13 = (f32[100,2,640]{2,1,0:T(2,128)S(1)}, f32[100,2,640]{2,1,0:T(2,128)S(1)}, u32[]{:S(2)}, u32[]{:S(2)}) collective-permute-start(f32[100,2,640]{2,1,0:T(2,128)S(1)} %collective-permute-done.8.refs_2_), channel_id=1, source_target_pairs={{0,2},{1,3},{2,0},{3,1},{4,6},{5,7},{6,4},{7,5},{8,10},{9,11},{10,... | collective-permute-start | bytes 1536008 | tf_op jit(solution)/shard_map/ppermute | solution.py:32
  52.9 0.0 collective-permute-start.12
  52.9 0.7 collective-permute-done.10.refs_9_
  53.5 2.0 %collective-permute-start.11 = (f32[100,2,640]{2,1,0:T(2,128)S(1)}, f32[100,2,640]{2,1,0:T(2,128)S(1)}, u32[]{:S(2)}, u32[]{:S(2)}) collective-permute-start(f32[100,2,640]{2,1,0:T(2,128)S(1)} %collective-permute-done.9.refs_7_), channel_id=1, source_target_pairs={{0,4},{1,13},{2,6},{3,15},{4,8},{5,1},{6,10},{7,3},{8,12},{9,5},{1... | collective-permute-start | bytes 1536008 | tf_op jit(solution)/shard_map/ppermute | solution.py:32
  55.5 3.7 %shard_map.28 = (f32[5,800,2,128]{3,2,1,0:T(2,128)S(1)}, bf16[2,640,1280]{2,1,0:T(8,128)(2,1)S(1)}) custom-call(f32[100,2,640]{2,1,0:T(2,128)S(1)} %pad_maximum_fusion.2.refs_0_, f32[100,2,640]{2,1,0:T(2,128)S(1)} %collective-permute-done.6.refs_1_, f32[100,2,640]{2,1,0:T(2,128)S(1)} %collective-permute-done.4.refs_2_, ...), custom_call_target="tpu_custom_call" | custom-call | flops 1000000 | bytes 100000 | tf_op jit(solution)/shard_map/pallas_call | solution.py:264
  59.2 1.2 %collective-permute-done.16.je = f32[100,2,640]{2,1,0:T(2,128)S(1)} collective-permute-done((f32[100,2,640]{2,1,0:T(2,128)S(1)}, f32[100,2,640]{2,1,0:T(2,128)S(1)}, u32[]{:S(2)}, u32[]{:S(2)}) %collective-permute-start.16) | collective-permute-done | bytes 512032 | tf_op jit(solution)/shard_map/ppermute | solution.py:32
  60.4 3.4 %collective-permute-done.17.jf = f32[100,2,640]{2,1,0:T(2,128)S(1)} collective-permute-done((f32[100,2,640]{2,1,0:T(2,128)S(1)}, f32[100,2,640]{2,1,0:T(2,128)S(1)}, u32[]{:S(2)}, u32[]{:S(2)}) %collective-permute-start.17) | collective-permute-done | bytes 512032 | tf_op jit(solution)/shard_map/ppermute | solution.py:32
  63.7 5.8 %shard_map.29 = (f32[2,640,1280]{2,1,0:T(8,128)S(1)}, bf16[1280,1280]{1,0:T(8,128)(2,1)S(1)}, bf16[1280,1280]{1,0:T(8,128)(2,1)S(1)}, f32[5,800,2,128]{3,2,1,0:T(2,128)S(1)}) custom-call(f32[100,2,640]{2,1,0:T(2,128)S(1)} %collective-permute-done.16.je, f32[100,2,640]{2,1,0:T(2,128)S(1)} %collective-permute-done.17.jf, ...), custom_call_target="tpu_custom_call", output_to_operand_aliasing={{3}: (2, {})} | custom-call | flops 1000000 | bytes 100000 | tf_op jit(solution)/shard_map/pallas_call | solution.py:264
  69.5 0.0 collective-permute-done.13.refs_3_
  69.5 0.0 collective-permute-done.12.refs_1_
  69.5 0.0 collective-permute-done.11.refs_0_
  69.5 3.9 %collective-permute-start.20 = (f32[100,2,640]{2,1,0:T(2,128)S(1)}, f32[100,2,640]{2,1,0:T(2,128)S(1)}, u32[]{:S(2)}, u32[]{:S(2)}) collective-permute-start(f32[100,2,640]{2,1,0:T(2,128)S(1)} %collective-permute-done.12.refs_1_), channel_id=1, source_target_pairs={{0,1},{1,0},{2,3},{3,2},{4,5},{5,4},{6,7},{7,6},{8,9},{9,8},{10,11... | collective-permute-start | bytes 1536008 | tf_op jit(solution)/shard_map/ppermute | solution.py:32
  73.5 0.4 pad_maximum_fusion.1
  73.9 0.1 collective-permute-start.19
  74.0 0.4 pad_maximum_fusion
  74.5 0.6 collective-permute-start.18
  75.0 0.1 collective-permute-start.21
  75.1 0.4 collective-permute-start.22
  75.5 0.0 collective-permute-done.20.refs_2_
  75.5 0.1 collective-permute-start.23
  75.6 7.0 %shard_map.30.refs_8_ = f32[4,640,2,640]{3,2,1,0:T(2,128)} custom-call(f32[100,2,640]{2,1,0:T(2,128)S(1)} %collective-permute-done.11.refs_0_, f32[100,2,640]{2,1,0:T(2,128)S(1)} %collective-permute-done.12.refs_1_, f32[100,2,640]{2,1,0:T(2,128)S(1)} %collective-permute-done.8.refs_2_, f32[100,2,640]{2,1,0:T(2,128)S(1)} %collective-permute-done.13.refs_3_, ...), custom_call_target="tpu_custom_call" | custom-call | flops 1000000 | bytes 100000 | tf_op jit(solution)/shard_map/pallas_call | solution.py:264
  82.6 0.0 collective-permute-done.21.refs_3_
  82.7 0.0 collective-permute-done.22.refs_4_
  82.7 0.0 collective-permute-done.23.refs_5_
  82.7 0.0 collective-permute-done.19.refs_1_
  82.7 0.0 collective-permute-done.18.refs_0_
  82.7 12.6 %shard_map.31 = f32[4,640,2,640]{3,2,1,0:T(2,128)} custom-call(f32[200,2,640]{2,1,0:T(2,128)S(1)} %collective-permute-done.18.refs_0_, f32[200,2,640]{2,1,0:T(2,128)S(1)} %collective-permute-done.19.refs_1_, f32[100,2,640]{2,1,0:T(2,128)S(1)} %collective-permute-done.20.refs_2_, ...), custom_call_target="tpu_custom_call", output_to_operand_aliasing={{}: (8, {})} | custom-call | flops 1000000 | bytes 100000 | tf_op jit(solution)/shard_map/pallas_call | solution.py:264
  (1 shorter events, 0.0 us)
Async XLA Ops:
  1.3 13.6 %collective-permute-start = (f32[50,2,640]{2,1,0:T(2,128)}, f32[50,2,640]{2,1,0:T(2,128)S(1)}, u32[]{:S(2)}, u32[]{:S(2)}) collective-permute-start(f32[50,2,640]{2,1,0:T(2,128)} %bitcast.5), channel_id=1, source_target_pairs={{0,0},{1,1},{2,2},{3,3},{4,4},{5,5},{6,6},{7,7},{8,8},{9,9},{10,10... | collective-permute-start | bytes 768008 | tf_op jit(solution)/shard_map/ppermute | solution.py:32
  2.9 12.0 %collective-permute-start.1 = (f32[50,2,640]{2,1,0:T(2,128)}, f32[50,2,640]{2,1,0:T(2,128)S(1)}, u32[]{:S(2)}, u32[]{:S(2)}) collective-permute-start(f32[50,2,640]{2,1,0:T(2,128)} %bitcast.7), channel_id=1, source_target_pairs={{0,8},{1,9},{2,10},{3,11},{4,12},{5,13},{6,14},{7,15},{8,0},{9,1},... | collective-permute-start | bytes 768008 | tf_op jit(solution)/shard_map/ppermute | solution.py:32
  8.6 23.0 %collective-permute-start.6 = (f32[100,2,640]{2,1,0:T(2,128)S(1)}, f32[100,2,640]{2,1,0:T(2,128)S(1)}, u32[]{:S(2)}, u32[]{:S(2)}) collective-permute-start(f32[100,2,640]{2,1,0:T(2,128)S(1)} %pad_maximum_fusion.2.refs_0_), channel_id=1, source_target_pairs={{0,16},{1,17},{2,18},{3,19},{4,20},{5,21},{6,22},{7,23},{8,24},{9,... | collective-permute-start | bytes 1536008 | tf_op jit(solution)/shard_map/ppermute | solution.py:32
  12.2 19.3 %collective-permute-start.5 = (f32[100,2,640]{2,1,0:T(2,128)S(1)}, f32[100,2,640]{2,1,0:T(2,128)S(1)}, u32[]{:S(2)}, u32[]{:S(2)}) collective-permute-start(f32[100,2,640]{2,1,0:T(2,128)S(1)} %pad_maximum_fusion.2.refs_0_), channel_id=1, source_target_pairs={{0,96},{1,33},{2,98},{3,35},{4,100},{5,37},{6,102},{7,39},{8,104},... | collective-permute-start | bytes 1536008 | tf_op jit(solution)/shard_map/ppermute | solution.py:32
  13.6 17.9 %collective-permute-start.4 = (f32[100,2,640]{2,1,0:T(2,128)S(1)}, f32[100,2,640]{2,1,0:T(2,128)S(1)}, u32[]{:S(2)}, u32[]{:S(2)}) collective-permute-start(f32[100,2,640]{2,1,0:T(2,128)S(1)} %pad_maximum_fusion.2.refs_0_), channel_id=1, source_target_pairs={{0,32},{1,97},{2,34},{3,99},{4,36},{5,101},{6,38},{7,103},{8,40},{... | collective-permute-start | bytes 1536008 | tf_op jit(solution)/shard_map/ppermute | solution.py:32
  14.9 5.6 %collective-permute-start.2 = (f32[50,2,640]{2,1,0:T(2,128)S(1)}, f32[50,2,640]{2,1,0:T(2,128)S(1)}, u32[]{:S(2)}, u32[]{:S(2)}) collective-permute-start(f32[50,2,640]{2,1,0:T(2,128)S(1)} %collective-permute-done), channel_id=1, source_target_pairs={{0,0},{1,1},{2,16},{3,17},{4,36},{5,37},{6,52},{7,53},{8,72},{9,73... | collective-permute-start | bytes 768008 | tf_op jit(solution)/shard_map/ppermute | solution.py:32
  15.6 15.9 %collective-permute-start.3 = (f32[50,2,640]{2,1,0:T(2,128)S(1)}, f32[50,2,640]{2,1,0:T(2,128)S(1)}, u32[]{:S(2)}, u32[]{:S(2)}) collective-permute-start(f32[50,2,640]{2,1,0:T(2,128)S(1)} %collective-permute-done.1), channel_id=1, source_target_pairs={{0,66},{1,67},{2,82},{3,83},{4,102},{5,103},{6,118},{7,119},{8,10}... | collective-permute-start | bytes 768008 | tf_op jit(solution)/shard_map/ppermute | solution.py:32
  31.7 8.3 %collective-permute-start.7 = (f32[100,2,640]{2,1,0:T(2,128)S(1)}, f32[100,2,640]{2,1,0:T(2,128)S(1)}, u32[]{:S(2)}, u32[]{:S(2)}) collective-permute-start(f32[100,2,640]{2,1,0:T(2,128)S(1)} %constant_dynamic-update-slice_fusion.refs_6_), channel_id=1, source_target_pairs={{0,4},{1,13},{2,6},{3,15},{4,8},{5,1},{6,10},{7,3},{8,12},{9,5},{1... | collective-permute-start | bytes 1536008 | tf_op jit(solution)/shard_map/ppermute | solution.py:32
  32.7 14.4 %collective-permute-start.15 = (f32[100,2,640]{2,1,0:T(2,128)S(1)}, f32[100,2,640]{2,1,0:T(2,128)S(1)}, u32[]{:S(2)}, u32[]{:S(2)}) collective-permute-start(f32[100,2,640]{2,1,0:T(2,128)S(1)} %collective-permute-done.6.refs_1_), channel_id=1, source_target_pairs={{0,96},{1,33},{2,98},{3,35},{4,100},{5,37},{6,102},{7,39},{8,104},... | collective-permute-start | bytes 1536008 | tf_op jit(solution)/shard_map/ppermute | solution.py:32
  36.2 12.2 %collective-permute-start.14 = (f32[100,2,640]{2,1,0:T(2,128)S(1)}, f32[100,2,640]{2,1,0:T(2,128)S(1)}, u32[]{:S(2)}, u32[]{:S(2)}) collective-permute-start(f32[100,2,640]{2,1,0:T(2,128)S(1)} %collective-permute-done.6.refs_1_), channel_id=1, source_target_pairs={{0,32},{1,97},{2,34},{3,99},{4,36},{5,101},{6,38},{7,103},{8,40},{... | collective-permute-start | bytes 1536008 | tf_op jit(solution)/shard_map/ppermute | solution.py:32
  36.2 14.3 %collective-permute-start.9 = (f32[100,2,640]{2,1,0:T(2,128)S(1)}, f32[100,2,640]{2,1,0:T(2,128)S(1)}, u32[]{:S(2)}, u32[]{:S(2)}) collective-permute-start(f32[100,2,640]{2,1,0:T(2,128)S(1)} %constant_dynamic-update-slice_fusion.refs_6_), channel_id=1, source_target_pairs={{0,2},{1,3},{2,0},{3,1},{4,6},{5,7},{6,4},{7,5},{8,10},{9,11},{10,... | collective-permute-start | bytes 1536008 | tf_op jit(solution)/shard_map/ppermute | solution.py:32
  39.9 10.6 %collective-permute-start.8 = (f32[100,2,640]{2,1,0:T(2,128)S(1)}, f32[100,2,640]{2,1,0:T(2,128)S(1)}, u32[]{:S(2)}, u32[]{:S(2)}) collective-permute-start(f32[100,2,640]{2,1,0:T(2,128)S(1)} %collective-permute-done.7.refs_8_), channel_id=1, source_target_pairs={{0,4},{1,13},{2,6},{3,15},{4,8},{5,1},{6,10},{7,3},{8,12},{9,5},{1... | collective-permute-start | bytes 1536008 | tf_op jit(solution)/shard_map/ppermute | solution.py:32
  41.8 11.7 %collective-permute-start.10 = (f32[100,2,640]{2,1,0:T(2,128)S(1)}, f32[100,2,640]{2,1,0:T(2,128)S(1)}, u32[]{:S(2)}, u32[]{:S(2)}) collective-permute-start(f32[100,2,640]{2,1,0:T(2,128)S(1)} %constant_dynamic-update-slice_fusion.refs_6_), channel_id=1, source_target_pairs={{0,12},{1,5},{2,14},{3,7},{4,0},{5,9},{6,2},{7,11},{8,4},{9,13},{1... | collective-permute-start | bytes 1536008 | tf_op jit(solution)/shard_map/ppermute | solution.py:32
  48.4 12.0 %collective-permute-start.16 = (f32[100,2,640]{2,1,0:T(2,128)S(1)}, f32[100,2,640]{2,1,0:T(2,128)S(1)}, u32[]{:S(2)}, u32[]{:S(2)}) collective-permute-start(f32[100,2,640]{2,1,0:T(2,128)S(1)} %collective-permute-done.4.refs_2_), channel_id=1, source_target_pairs={{0,32},{1,97},{2,34},{3,99},{4,36},{5,101},{6,38},{7,103},{8,40},{... | collective-permute-start | bytes 1536008 | tf_op jit(solution)/shard_map/ppermute | solution.py:32
  50.5 13.2 %collective-permute-start.17 = (f32[100,2,640]{2,1,0:T(2,128)S(1)}, f32[100,2,640]{2,1,0:T(2,128)S(1)}, u32[]{:S(2)}, u32[]{:S(2)}) collective-permute-start(f32[100,2,640]{2,1,0:T(2,128)S(1)} %collective-permute-done.15.refs_5_), channel_id=1, source_target_pairs={{0,96},{1,33},{2,98},{3,35},{4,100},{5,37},{6,102},{7,39},{8,104},... | collective-permute-start | bytes 1536008 | tf_op jit(solution)/shard_map/ppermute | solution.py:32
  50.5 19.0 %collective-permute-start.13 = (f32[100,2,640]{2,1,0:T(2,128)S(1)}, f32[100,2,640]{2,1,0:T(2,128)S(1)}, u32[]{:S(2)}, u32[]{:S(2)}) collective-permute-start(f32[100,2,640]{2,1,0:T(2,128)S(1)} %collective-permute-done.8.refs_2_), channel_id=1, source_target_pairs={{0,2},{1,3},{2,0},{3,1},{4,6},{5,7},{6,4},{7,5},{8,10},{9,11},{10,... | collective-permute-start | bytes 1536008 | tf_op jit(solution)/shard_map/ppermute | solution.py:32
  52.9 16.7 %collective-permute-start.12 = (f32[100,2,640]{2,1,0:T(2,128)S(1)}, f32[100,2,640]{2,1,0:T(2,128)S(1)}, u32[]{:S(2)}, u32[]{:S(2)}) collective-permute-start(f32[100,2,640]{2,1,0:T(2,128)S(1)} %collective-permute-done.9.refs_7_), channel_id=1, source_target_pairs={{0,12},{1,5},{2,14},{3,7},{4,0},{5,9},{6,2},{7,11},{8,4},{9,13},{1... | collective-permute-start | bytes 1536008 | tf_op jit(solution)/shard_map/ppermute | solution.py:32
  53.5 16.0 %collective-permute-start.11 = (f32[100,2,640]{2,1,0:T(2,128)S(1)}, f32[100,2,640]{2,1,0:T(2,128)S(1)}, u32[]{:S(2)}, u32[]{:S(2)}) collective-permute-start(f32[100,2,640]{2,1,0:T(2,128)S(1)} %collective-permute-done.9.refs_7_), channel_id=1, source_target_pairs={{0,4},{1,13},{2,6},{3,15},{4,8},{5,1},{6,10},{7,3},{8,12},{9,5},{1... | collective-permute-start | bytes 1536008 | tf_op jit(solution)/shard_map/ppermute | solution.py:32
  69.5 6.0 %collective-permute-start.20 = (f32[100,2,640]{2,1,0:T(2,128)S(1)}, f32[100,2,640]{2,1,0:T(2,128)S(1)}, u32[]{:S(2)}, u32[]{:S(2)}) collective-permute-start(f32[100,2,640]{2,1,0:T(2,128)S(1)} %collective-permute-done.12.refs_1_), channel_id=1, source_target_pairs={{0,1},{1,0},{2,3},{3,2},{4,5},{5,4},{6,7},{7,6},{8,9},{9,8},{10,11... | collective-permute-start | bytes 1536008 | tf_op jit(solution)/shard_map/ppermute | solution.py:32
  73.9 8.8 %collective-permute-start.19 = (f32[200,2,640]{2,1,0:T(2,128)S(1)}, f32[200,2,640]{2,1,0:T(2,128)S(1)}, u32[]{:S(2)}, u32[]{:S(2)}) collective-permute-start(f32[200,2,640]{2,1,0:T(2,128)S(1)} %pad_maximum_fusion.1), channel_id=1, source_target_pairs={{0,1},{1,0},{2,3},{3,2},{4,5},{5,4},{6,7},{7,6},{8,9},{9,8},{10,11... | collective-permute-start | bytes 3072008 | tf_op jit(solution)/shard_map/ppermute | solution.py:32
  74.5 8.2 %collective-permute-start.18 = (f32[200,2,640]{2,1,0:T(2,128)S(1)}, f32[200,2,640]{2,1,0:T(2,128)S(1)}, u32[]{:S(2)}, u32[]{:S(2)}) collective-permute-start(f32[200,2,640]{2,1,0:T(2,128)S(1)} %pad_maximum_fusion), channel_id=1, source_target_pairs={{0,1},{1,0},{2,3},{3,2},{4,5},{5,4},{6,7},{7,6},{8,9},{9,8},{10,11... | collective-permute-start | bytes 3072008 | tf_op jit(solution)/shard_map/ppermute | solution.py:32
  75.0 7.6 %collective-permute-start.21 = (f32[100,2,640]{2,1,0:T(2,128)S(1)}, f32[100,2,640]{2,1,0:T(2,128)S(1)}, u32[]{:S(2)}, u32[]{:S(2)}) collective-permute-start(f32[100,2,640]{2,1,0:T(2,128)S(1)} %collective-permute-done.11.refs_0_), channel_id=1, source_target_pairs={{0,1},{1,0},{2,3},{3,2},{4,5},{5,4},{6,7},{7,6},{8,9},{9,8},{10,11... | collective-permute-start | bytes 1536008 | tf_op jit(solution)/shard_map/ppermute | solution.py:32
  75.1 7.5 %collective-permute-start.22 = (f32[100,2,640]{2,1,0:T(2,128)S(1)}, f32[100,2,640]{2,1,0:T(2,128)S(1)}, u32[]{:S(2)}, u32[]{:S(2)}) collective-permute-start(f32[100,2,640]{2,1,0:T(2,128)S(1)} %collective-permute-done.8.refs_2_), channel_id=1, source_target_pairs={{0,1},{1,0},{2,3},{3,2},{4,5},{5,4},{6,7},{7,6},{8,9},{9,8},{10,11... | collective-permute-start | bytes 1536008 | tf_op jit(solution)/shard_map/ppermute | solution.py:32
  75.5 7.1 %collective-permute-start.23 = (f32[100,2,640]{2,1,0:T(2,128)S(1)}, f32[100,2,640]{2,1,0:T(2,128)S(1)}, u32[]{:S(2)}, u32[]{:S(2)}) collective-permute-start(f32[100,2,640]{2,1,0:T(2,128)S(1)} %collective-permute-done.13.refs_3_), channel_id=1, source_target_pairs={{0,1},{1,0},{2,3},{3,2},{4,5},{5,4},{6,7},{7,6},{8,9},{9,8},{10,11... | collective-permute-start | bytes 1536008 | tf_op jit(solution)/shard_map/ppermute | solution.py:32

commit v4 on v3

--- a/solution.py
+++ b/solution.py
@@ -112,9 +112,9 @@
     for half in range(2):
         for m, (ref, n) in enumerate(zip(refs, chosen)):
             a, b = places(z, x, way)[n]
-            delta = (a - (y - x + 2 * half) + 16) % 4
+            delta = (a - (x - y + 2 * half) + 16) % 4
             other = (b + low + half) % 2
-            side = jnp.where(delta == (4 - way) % 4, 2, 3) + 2 * other
+            side = jnp.where(delta == (4 + way) % 4, 2, 3) + 2 * other
             n = jnp.where(delta == 0, other, jnp.where(delta == 2, 6 + other, side))
             at = (n // GROUP) * PARTIAL + half * GROUP * HALF + (n % GROUP) * HALF
             for cut in range(CUTS):
@@ -328,11 +328,11 @@
         return x, z, y, low + 1, core
 
     def tilt(value, shift):
-        return permute(value, lambda x, z, y, low, core: (x, z, y + x + shift, low, core))
+        return permute(value, lambda x, z, y, low, core: (x, low, y - x + shift, z + shift // 2, core))
 
     def mirror(value, shift):
         return permute(
-            value, lambda x, z, y, low, core: (y - x - shift, low, y, z + shift // 2, core)
+            value, lambda x, z, y, low, core: (y + x - shift, z, y, low, core)
         )
 
     def swap(value):

time: 95.7 us -> 93.1 us (0.973)
  starting transfers between devices: 39.1 us -> 35.9 us
    ppermute x24, starting transfers between devices: 39.1 us -> 35.9 us  [permute(): return lax.ppermute(value, AXES, pairs)]
  transfers between devices with their start and end apart: 24 -> 24, of which waited for: 7 -> 8; matrix products, arithmetic and copies ran while one was open for 1% -> 1% of each run, Pallas kernels for 17% -> 18%
where the time goes in v4:
time: 93.1 us; the launch traced here: 92.9 us
  starting transfers between devices  35.9 us (39%)
  Pallas kernels  29.1 us (31%)
  waiting for transfers between devices  25.3 us (27%)
  other arithmetic  2.17 us (2%)
    ppermute x24, starting transfers between devices, permute(): return lax.ppermute(value, AXES, pairs)  35.9 us
    pallas_call x4, Pallas kernels, call(): pl.pallas_call(kernel, out_shape=tuple(shapes), in_specs=kinds, out_specs...  29.1 us
    ppermute x24, waiting for transfers between devices, permute(): return lax.ppermute(value, AXES, pairs)  25.3 us
  transfers between devices with their start and end apart: 24, of which 8 were waited for; matrix products, arithmetic and copies ran while one was open for 1% of the time, Pallas kernels for 18%

profile of v4, /device:TPU:1, one launch (start us, length us, event | category | flops | bytes accessed | tf_op | source)
XLA Modules:
  0.0 92.9 jit_solution(16536371250667053)
XLA Ops:
  0.0 1.3 %pad_maximum_fusion.2.refs_0_ = f32[100,2,640]{2,1,0:T(2,128)S(1)} fusion(f32[50,2,640]{2,1,0:T(2,128)} %bitcast.4, f32[50,2,640]{2,1,0:T(2,128)} %bitcast.6), kind=kLoop, calls=%fused_computation.2 | loop fusion | flops 128000 | bytes 1024000 | tf_op jit(solution)/shard_map/concatenate | solution.py:310
  1.3 1.6 %collective-permute-start = (f32[50,2,640]{2,1,0:T(2,128)}, f32[50,2,640]{2,1,0:T(2,128)S(1)}, u32[]{:S(2)}, u32[]{:S(2)}) collective-permute-start(f32[50,2,640]{2,1,0:T(2,128)} %bitcast.5), channel_id=1, source_target_pairs={{0,0},{1,1},{2,16},{3,17},{4,4},{5,5},{6,20},{7,21},{8,8},{9,9},{1... | collective-permute-start | bytes 768008 | tf_op jit(solution)/shard_map/ppermute | solution.py:32
  2.9 7.1 %collective-permute-start.1 = (f32[50,2,640]{2,1,0:T(2,128)}, f32[50,2,640]{2,1,0:T(2,128)S(1)}, u32[]{:S(2)}, u32[]{:S(2)}) collective-permute-start(f32[50,2,640]{2,1,0:T(2,128)} %bitcast.7), channel_id=1, source_target_pairs={{0,10},{1,11},{2,26},{3,27},{4,14},{5,15},{6,30},{7,31},{8,2},{9,3... | collective-permute-start | bytes 768008 | tf_op jit(solution)/shard_map/ppermute | solution.py:32
  10.0 0.0 collective-permute-start.6
  10.0 1.3 %collective-permute-start.5 = (f32[100,2,640]{2,1,0:T(2,128)S(1)}, f32[100,2,640]{2,1,0:T(2,128)S(1)}, u32[]{:S(2)}, u32[]{:S(2)}) collective-permute-start(f32[100,2,640]{2,1,0:T(2,128)S(1)} %pad_maximum_fusion.2.refs_0_), channel_id=1, source_target_pairs={{0,96},{1,33},{2,98},{3,35},{4,100},{5,37},{6,102},{7,39},{8,104},... | collective-permute-start | bytes 1536008 | tf_op jit(solution)/shard_map/ppermute | solution.py:32
  11.3 1.4 %collective-permute-start.4 = (f32[100,2,640]{2,1,0:T(2,128)S(1)}, f32[100,2,640]{2,1,0:T(2,128)S(1)}, u32[]{:S(2)}, u32[]{:S(2)}) collective-permute-start(f32[100,2,640]{2,1,0:T(2,128)S(1)} %pad_maximum_fusion.2.refs_0_), channel_id=1, source_target_pairs={{0,32},{1,97},{2,34},{3,99},{4,36},{5,101},{6,38},{7,103},{8,40},{... | collective-permute-start | bytes 1536008 | tf_op jit(solution)/shard_map/ppermute | solution.py:32
  12.7 0.0 collective-permute-done
  12.7 3.7 %collective-permute-done.1 = f32[50,2,640]{2,1,0:T(2,128)S(1)} collective-permute-done((f32[50,2,640]{2,1,0:T(2,128)}, f32[50,2,640]{2,1,0:T(2,128)S(1)}, u32[]{:S(2)}, u32[]{:S(2)}) %collective-permute-start.1) | collective-permute-done | bytes 256032 | tf_op jit(solution)/shard_map/ppermute | solution.py:32
  16.4 0.7 collective-permute-start.2
  17.0 4.1 %collective-permute-start.3 = (f32[50,2,640]{2,1,0:T(2,128)S(1)}, f32[50,2,640]{2,1,0:T(2,128)S(1)}, u32[]{:S(2)}, u32[]{:S(2)}) collective-permute-start(f32[50,2,640]{2,1,0:T(2,128)S(1)} %collective-permute-done.1), channel_id=1, source_target_pairs={{0,64},{1,65},{2,66},{3,67},{4,100},{5,101},{6,102},{7,103},{8,8},... | collective-permute-start | bytes 768008 | tf_op jit(solution)/shard_map/ppermute | solution.py:32
  21.2 0.0 collective-permute-done.2
  21.2 7.5 %collective-permute-done.3 = f32[50,2,640]{2,1,0:T(2,128)S(1)} collective-permute-done((f32[50,2,640]{2,1,0:T(2,128)S(1)}, f32[50,2,640]{2,1,0:T(2,128)S(1)}, u32[]{:S(2)}, u32[]{:S(2)}) %collective-permute-start.3) | collective-permute-done | bytes 256032 | tf_op jit(solution)/shard_map/ppermute | solution.py:32
  28.7 0.0 collective-permute-done.6.refs_1_
  28.7 0.0 collective-permute-done.5.refs_3_
  28.7 0.0 collective-permute-done.4.refs_2_
  28.7 0.1 constant_dynamic-update-slice_fusion.refs_6_
  28.8 3.8 %collective-permute-start.7 = (f32[100,2,640]{2,1,0:T(2,128)S(1)}, f32[100,2,640]{2,1,0:T(2,128)S(1)}, u32[]{:S(2)}, u32[]{:S(2)}) collective-permute-start(f32[100,2,640]{2,1,0:T(2,128)S(1)} %constant_dynamic-update-slice_fusion.refs_6_), channel_id=1, source_target_pairs={{0,4},{1,13},{2,6},{3,15},{4,8},{5,1},{6,10},{7,3},{8,12},{9,5},{1... | collective-permute-start | bytes 1536008 | tf_op jit(solution)/shard_map/ppermute | solution.py:32
  32.6 0.0 collective-permute-start.15
  32.6 2.7 %collective-permute-start.14 = (f32[100,2,640]{2,1,0:T(2,128)S(1)}, f32[100,2,640]{2,1,0:T(2,128)S(1)}, u32[]{:S(2)}, u32[]{:S(2)}) collective-permute-start(f32[100,2,640]{2,1,0:T(2,128)S(1)} %collective-permute-done.6.refs_1_), channel_id=1, source_target_pairs={{0,32},{1,97},{2,34},{3,99},{4,36},{5,101},{6,38},{7,103},{8,40},{... | collective-permute-start | bytes 1536008 | tf_op jit(solution)/shard_map/ppermute | solution.py:32
  35.3 1.5 %collective-permute-start.9 = (f32[100,2,640]{2,1,0:T(2,128)S(1)}, f32[100,2,640]{2,1,0:T(2,128)S(1)}, u32[]{:S(2)}, u32[]{:S(2)}) collective-permute-start(f32[100,2,640]{2,1,0:T(2,128)S(1)} %constant_dynamic-update-slice_fusion.refs_6_), channel_id=1, source_target_pairs={{0,2},{1,3},{2,0},{3,1},{4,6},{5,7},{6,4},{7,5},{8,10},{9,11},{10,... | collective-permute-start | bytes 1536008 | tf_op jit(solution)/shard_map/ppermute | solution.py:32
  36.8 1.8 %collective-permute-done.7.refs_8_ = f32[100,2,640]{2,1,0:T(2,128)S(1)} collective-permute-done((f32[100,2,640]{2,1,0:T(2,128)S(1)}, f32[100,2,640]{2,1,0:T(2,128)S(1)}, u32[]{:S(2)}, u32[]{:S(2)}) %collective-permute-start.7) | collective-permute-done | bytes 512032 | tf_op jit(solution)/shard_map/ppermute | solution.py:32
  38.6 3.4 %collective-permute-start.8 = (f32[100,2,640]{2,1,0:T(2,128)S(1)}, f32[100,2,640]{2,1,0:T(2,128)S(1)}, u32[]{:S(2)}, u32[]{:S(2)}) collective-permute-start(f32[100,2,640]{2,1,0:T(2,128)S(1)} %collective-permute-done.7.refs_8_), channel_id=1, source_target_pairs={{0,4},{1,13},{2,6},{3,15},{4,8},{5,1},{6,10},{7,3},{8,12},{9,5},{1... | collective-permute-start | bytes 1536008 | tf_op jit(solution)/shard_map/ppermute | solution.py:32
  42.0 0.0 collective-permute-start.10
  42.0 2.9 %collective-permute-done.15.refs_5_ = f32[100,2,640]{2,1,0:T(2,128)S(1)} collective-permute-done((f32[100,2,640]{2,1,0:T(2,128)S(1)}, f32[100,2,640]{2,1,0:T(2,128)S(1)}, u32[]{:S(2)}, u32[]{:S(2)}) %collective-permute-start.15) | collective-permute-done | bytes 512032 | tf_op jit(solution)/shard_map/ppermute | solution.py:32
  45.0 1.3 %collective-permute-done.14.refs_4_ = f32[100,2,640]{2,1,0:T(2,128)S(1)} collective-permute-done((f32[100,2,640]{2,1,0:T(2,128)S(1)}, f32[100,2,640]{2,1,0:T(2,128)S(1)}, u32[]{:S(2)}, u32[]{:S(2)}) %collective-permute-start.14) | collective-permute-done | bytes 512032 | tf_op jit(solution)/shard_map/ppermute | solution.py:32
  46.3 3.4 %collective-permute-start.16 = (f32[100,2,640]{2,1,0:T(2,128)S(1)}, f32[100,2,640]{2,1,0:T(2,128)S(1)}, u32[]{:S(2)}, u32[]{:S(2)}) collective-permute-start(f32[100,2,640]{2,1,0:T(2,128)S(1)} %collective-permute-done.4.refs_2_), channel_id=1, source_target_pairs={{0,32},{1,97},{2,34},{3,99},{4,36},{5,101},{6,38},{7,103},{8,40},{... | collective-permute-start | bytes 1536008 | tf_op jit(solution)/shard_map/ppermute | solution.py:32
  49.7 0.0 collective-permute-start.17
  49.7 0.0 collective-permute-done.9.refs_7_
  49.7 0.6 collective-permute-done.8.refs_2_
  50.3 1.5 %collective-permute-start.13 = (f32[100,2,640]{2,1,0:T(2,128)S(1)}, f32[100,2,640]{2,1,0:T(2,128)S(1)}, u32[]{:S(2)}, u32[]{:S(2)}) collective-permute-start(f32[100,2,640]{2,1,0:T(2,128)S(1)} %collective-permute-done.8.refs_2_), channel_id=1, source_target_pairs={{0,2},{1,3},{2,0},{3,1},{4,6},{5,7},{6,4},{7,5},{8,10},{9,11},{10,... | collective-permute-start | bytes 1536008 | tf_op jit(solution)/shard_map/ppermute | solution.py:32
  51.8 0.0 collective-permute-start.12
  51.8 4.9 %collective-permute-done.10.refs_9_ = f32[100,2,640]{2,1,0:T(2,128)S(1)} collective-permute-done((f32[100,2,640]{2,1,0:T(2,128)S(1)}, f32[100,2,640]{2,1,0:T(2,128)S(1)}, u32[]{:S(2)}, u32[]{:S(2)}) %collective-permute-start.10) | collective-permute-done | bytes 512032 | tf_op jit(solution)/shard_map/ppermute | solution.py:32
  56.7 0.0 collective-permute-start.11
  56.7 3.7 %shard_map.28 = (f32[5,800,2,128]{3,2,1,0:T(2,128)S(1)}, bf16[2,640,1280]{2,1,0:T(8,128)(2,1)S(1)}) custom-call(f32[100,2,640]{2,1,0:T(2,128)S(1)} %pad_maximum_fusion.2.refs_0_, f32[100,2,640]{2,1,0:T(2,128)S(1)} %collective-permute-done.6.refs_1_, f32[100,2,640]{2,1,0:T(2,128)S(1)} %collective-permute-done.4.refs_2_, ...), custom_call_target="tpu_custom_call" | custom-call | flops 1000000 | bytes 100000 | tf_op jit(solution)/shard_map/pallas_call | solution.py:264
  60.4 0.0 collective-permute-done.16.je
  60.4 2.6 %collective-permute-done.17.jf = f32[100,2,640]{2,1,0:T(2,128)S(1)} collective-permute-done((f32[100,2,640]{2,1,0:T(2,128)S(1)}, f32[100,2,640]{2,1,0:T(2,128)S(1)}, u32[]{:S(2)}, u32[]{:S(2)}) %collective-permute-start.17) | collective-permute-done | bytes 512032 | tf_op jit(solution)/shard_map/ppermute | solution.py:32
  63.0 5.7 %shard_map.29 = (f32[2,640,1280]{2,1,0:T(8,128)S(1)}, bf16[1280,1280]{1,0:T(8,128)(2,1)S(1)}, bf16[1280,1280]{1,0:T(8,128)(2,1)S(1)}, f32[5,800,2,128]{3,2,1,0:T(2,128)S(1)}) custom-call(f32[100,2,640]{2,1,0:T(2,128)S(1)} %collective-permute-done.16.je, f32[100,2,640]{2,1,0:T(2,128)S(1)} %collective-permute-done.17.jf, ...), custom_call_target="tpu_custom_call", output_to_operand_aliasing={{3}: (2, {})} | custom-call | flops 1000000 | bytes 100000 | tf_op jit(solution)/shard_map/pallas_call | solution.py:264
  68.7 0.0 collective-permute-done.13.refs_3_
  68.7 0.0 collective-permute-done.12.refs_1_
  68.7 0.0 collective-permute-done.11.refs_0_
  68.7 2.1 %collective-permute-start.20 = (f32[100,2,640]{2,1,0:T(2,128)S(1)}, f32[100,2,640]{2,1,0:T(2,128)S(1)}, u32[]{:S(2)}, u32[]{:S(2)}) collective-permute-start(f32[100,2,640]{2,1,0:T(2,128)S(1)} %collective-permute-done.12.refs_1_), channel_id=1, source_target_pairs={{0,1},{1,0},{2,3},{3,2},{4,5},{5,4},{6,7},{7,6},{8,9},{9,8},{10,11... | collective-permute-start | bytes 1536008 | tf_op jit(solution)/shard_map/ppermute | solution.py:32
  70.9 0.4 pad_maximum_fusion.1
  71.3 0.1 collective-permute-start.19
  71.4 0.4 pad_maximum_fusion
  71.9 0.6 collective-permute-start.18
  72.4 0.1 collective-permute-start.21
  72.5 0.4 collective-permute-start.22
  72.9 0.0 collective-permute-done.20.refs_2_
  72.9 0.1 collective-permute-start.23
  73.0 7.0 %shard_map.30.refs_8_ = f32[4,640,2,640]{3,2,1,0:T(2,128)} custom-call(f32[100,2,640]{2,1,0:T(2,128)S(1)} %collective-permute-done.11.refs_0_, f32[100,2,640]{2,1,0:T(2,128)S(1)} %collective-permute-done.12.refs_1_, f32[100,2,640]{2,1,0:T(2,128)S(1)} %collective-permute-done.8.refs_2_, f32[100,2,640]{2,1,0:T(2,128)S(1)} %collective-permute-done.13.refs_3_, ...), custom_call_target="tpu_custom_call" | custom-call | flops 1000000 | bytes 100000 | tf_op jit(solution)/shard_map/pallas_call | solution.py:264
  80.0 0.0 collective-permute-done.21.refs_3_
  80.1 0.0 collective-permute-done.22.refs_4_
  80.1 0.0 collective-permute-done.23.refs_5_
  80.1 0.0 collective-permute-done.19.refs_1_
  80.1 0.0 collective-permute-done.18.refs_0_
  80.1 12.6 %shard_map.31 = f32[4,640,2,640]{3,2,1,0:T(2,128)} custom-call(f32[200,2,640]{2,1,0:T(2,128)S(1)} %collective-permute-done.18.refs_0_, f32[200,2,640]{2,1,0:T(2,128)S(1)} %collective-permute-done.19.refs_1_, f32[100,2,640]{2,1,0:T(2,128)S(1)} %collective-permute-done.20.refs_2_, ...), custom_call_target="tpu_custom_call", output_to_operand_aliasing={{}: (8, {})} | custom-call | flops 1000000 | bytes 100000 | tf_op jit(solution)/shard_map/pallas_call | solution.py:264
  (1 shorter events, 0.0 us)
Async XLA Ops:
  1.3 11.4 %collective-permute-start = (f32[50,2,640]{2,1,0:T(2,128)}, f32[50,2,640]{2,1,0:T(2,128)S(1)}, u32[]{:S(2)}, u32[]{:S(2)}) collective-permute-start(f32[50,2,640]{2,1,0:T(2,128)} %bitcast.5), channel_id=1, source_target_pairs={{0,0},{1,1},{2,16},{3,17},{4,4},{5,5},{6,20},{7,21},{8,8},{9,9},{1... | collective-permute-start | bytes 768008 | tf_op jit(solution)/shard_map/ppermute | solution.py:32
  2.9 13.5 %collective-permute-start.1 = (f32[50,2,640]{2,1,0:T(2,128)}, f32[50,2,640]{2,1,0:T(2,128)S(1)}, u32[]{:S(2)}, u32[]{:S(2)}) collective-permute-start(f32[50,2,640]{2,1,0:T(2,128)} %bitcast.7), channel_id=1, source_target_pairs={{0,10},{1,11},{2,26},{3,27},{4,14},{5,15},{6,30},{7,31},{8,2},{9,3... | collective-permute-start | bytes 768008 | tf_op jit(solution)/shard_map/ppermute | solution.py:32
  10.0 18.7 %collective-permute-start.6 = (f32[100,2,640]{2,1,0:T(2,128)S(1)}, f32[100,2,640]{2,1,0:T(2,128)S(1)}, u32[]{:S(2)}, u32[]{:S(2)}) collective-permute-start(f32[100,2,640]{2,1,0:T(2,128)S(1)} %pad_maximum_fusion.2.refs_0_), channel_id=1, source_target_pairs={{0,16},{1,17},{2,18},{3,19},{4,20},{5,21},{6,22},{7,23},{8,24},{9,... | collective-permute-start | bytes 1536008 | tf_op jit(solution)/shard_map/ppermute | solution.py:32
  10.0 18.7 %collective-permute-start.5 = (f32[100,2,640]{2,1,0:T(2,128)S(1)}, f32[100,2,640]{2,1,0:T(2,128)S(1)}, u32[]{:S(2)}, u32[]{:S(2)}) collective-permute-start(f32[100,2,640]{2,1,0:T(2,128)S(1)} %pad_maximum_fusion.2.refs_0_), channel_id=1, source_target_pairs={{0,96},{1,33},{2,98},{3,35},{4,100},{5,37},{6,102},{7,39},{8,104},... | collective-permute-start | bytes 1536008 | tf_op jit(solution)/shard_map/ppermute | solution.py:32
  11.3 17.4 %collective-permute-start.4 = (f32[100,2,640]{2,1,0:T(2,128)S(1)}, f32[100,2,640]{2,1,0:T(2,128)S(1)}, u32[]{:S(2)}, u32[]{:S(2)}) collective-permute-start(f32[100,2,640]{2,1,0:T(2,128)S(1)} %pad_maximum_fusion.2.refs_0_), channel_id=1, source_target_pairs={{0,32},{1,97},{2,34},{3,99},{4,36},{5,101},{6,38},{7,103},{8,40},{... | collective-permute-start | bytes 1536008 | tf_op jit(solution)/shard_map/ppermute | solution.py:32
  16.4 4.8 %collective-permute-start.2 = (f32[50,2,640]{2,1,0:T(2,128)S(1)}, f32[50,2,640]{2,1,0:T(2,128)S(1)}, u32[]{:S(2)}, u32[]{:S(2)}) collective-permute-start(f32[50,2,640]{2,1,0:T(2,128)S(1)} %collective-permute-done), channel_id=1, source_target_pairs={{0,0},{1,1},{2,2},{3,3},{4,36},{5,37},{6,38},{7,39},{8,72},{9,73},... | collective-permute-start | bytes 768008 | tf_op jit(solution)/shard_map/ppermute | solution.py:32
  17.0 11.7 %collective-permute-start.3 = (f32[50,2,640]{2,1,0:T(2,128)S(1)}, f32[50,2,640]{2,1,0:T(2,128)S(1)}, u32[]{:S(2)}, u32[]{:S(2)}) collective-permute-start(f32[50,2,640]{2,1,0:T(2,128)S(1)} %collective-permute-done.1), channel_id=1, source_target_pairs={{0,64},{1,65},{2,66},{3,67},{4,100},{5,101},{6,102},{7,103},{8,8},... | collective-permute-start | bytes 768008 | tf_op jit(solution)/shard_map/ppermute | solution.py:32
  28.8 9.8 %collective-permute-start.7 = (f32[100,2,640]{2,1,0:T(2,128)S(1)}, f32[100,2,640]{2,1,0:T(2,128)S(1)}, u32[]{:S(2)}, u32[]{:S(2)}) collective-permute-start(f32[100,2,640]{2,1,0:T(2,128)S(1)} %constant_dynamic-update-slice_fusion.refs_6_), channel_id=1, source_target_pairs={{0,4},{1,13},{2,6},{3,15},{4,8},{5,1},{6,10},{7,3},{8,12},{9,5},{1... | collective-permute-start | bytes 1536008 | tf_op jit(solution)/shard_map/ppermute | solution.py:32
  32.6 12.4 %collective-permute-start.15 = (f32[100,2,640]{2,1,0:T(2,128)S(1)}, f32[100,2,640]{2,1,0:T(2,128)S(1)}, u32[]{:S(2)}, u32[]{:S(2)}) collective-permute-start(f32[100,2,640]{2,1,0:T(2,128)S(1)} %collective-permute-done.6.refs_1_), channel_id=1, source_target_pairs={{0,96},{1,33},{2,98},{3,35},{4,100},{5,37},{6,102},{7,39},{8,104},... | collective-permute-start | bytes 1536008 | tf_op jit(solution)/shard_map/ppermute | solution.py:32
  32.6 13.7 %collective-permute-start.14 = (f32[100,2,640]{2,1,0:T(2,128)S(1)}, f32[100,2,640]{2,1,0:T(2,128)S(1)}, u32[]{:S(2)}, u32[]{:S(2)}) collective-permute-start(f32[100,2,640]{2,1,0:T(2,128)S(1)} %collective-permute-done.6.refs_1_), channel_id=1, source_target_pairs={{0,32},{1,97},{2,34},{3,99},{4,36},{5,101},{6,38},{7,103},{8,40},{... | collective-permute-start | bytes 1536008 | tf_op jit(solution)/shard_map/ppermute | solution.py:32
  35.3 14.4 %collective-permute-start.9 = (f32[100,2,640]{2,1,0:T(2,128)S(1)}, f32[100,2,640]{2,1,0:T(2,128)S(1)}, u32[]{:S(2)}, u32[]{:S(2)}) collective-permute-start(f32[100,2,640]{2,1,0:T(2,128)S(1)} %constant_dynamic-update-slice_fusion.refs_6_), channel_id=1, source_target_pairs={{0,2},{1,3},{2,0},{3,1},{4,6},{5,7},{6,4},{7,5},{8,10},{9,11},{10,... | collective-permute-start | bytes 1536008 | tf_op jit(solution)/shard_map/ppermute | solution.py:32
  38.6 11.7 %collective-permute-start.8 = (f32[100,2,640]{2,1,0:T(2,128)S(1)}, f32[100,2,640]{2,1,0:T(2,128)S(1)}, u32[]{:S(2)}, u32[]{:S(2)}) collective-permute-start(f32[100,2,640]{2,1,0:T(2,128)S(1)} %collective-permute-done.7.refs_8_), channel_id=1, source_target_pairs={{0,4},{1,13},{2,6},{3,15},{4,8},{5,1},{6,10},{7,3},{8,12},{9,5},{1... | collective-permute-start | bytes 1536008 | tf_op jit(solution)/shard_map/ppermute | solution.py:32
  42.0 14.7 %collective-permute-start.10 = (f32[100,2,640]{2,1,0:T(2,128)S(1)}, f32[100,2,640]{2,1,0:T(2,128)S(1)}, u32[]{:S(2)}, u32[]{:S(2)}) collective-permute-start(f32[100,2,640]{2,1,0:T(2,128)S(1)} %constant_dynamic-update-slice_fusion.refs_6_), channel_id=1, source_target_pairs={{0,12},{1,5},{2,14},{3,7},{4,0},{5,9},{6,2},{7,11},{8,4},{9,13},{1... | collective-permute-start | bytes 1536008 | tf_op jit(solution)/shard_map/ppermute | solution.py:32
  46.3 14.1 %collective-permute-start.16 = (f32[100,2,640]{2,1,0:T(2,128)S(1)}, f32[100,2,640]{2,1,0:T(2,128)S(1)}, u32[]{:S(2)}, u32[]{:S(2)}) collective-permute-start(f32[100,2,640]{2,1,0:T(2,128)S(1)} %collective-permute-done.4.refs_2_), channel_id=1, source_target_pairs={{0,32},{1,97},{2,34},{3,99},{4,36},{5,101},{6,38},{7,103},{8,40},{... | collective-permute-start | bytes 1536008 | tf_op jit(solution)/shard_map/ppermute | solution.py:32
  49.7 13.3 %collective-permute-start.17 = (f32[100,2,640]{2,1,0:T(2,128)S(1)}, f32[100,2,640]{2,1,0:T(2,128)S(1)}, u32[]{:S(2)}, u32[]{:S(2)}) collective-permute-start(f32[100,2,640]{2,1,0:T(2,128)S(1)} %collective-permute-done.15.refs_5_), channel_id=1, source_target_pairs={{0,96},{1,33},{2,98},{3,35},{4,100},{5,37},{6,102},{7,39},{8,104},... | collective-permute-start | bytes 1536008 | tf_op jit(solution)/shard_map/ppermute | solution.py:32
  50.3 18.4 %collective-permute-start.13 = (f32[100,2,640]{2,1,0:T(2,128)S(1)}, f32[100,2,640]{2,1,0:T(2,128)S(1)}, u32[]{:S(2)}, u32[]{:S(2)}) collective-permute-start(f32[100,2,640]{2,1,0:T(2,128)S(1)} %collective-permute-done.8.refs_2_), channel_id=1, source_target_pairs={{0,2},{1,3},{2,0},{3,1},{4,6},{5,7},{6,4},{7,5},{8,10},{9,11},{10,... | collective-permute-start | bytes 1536008 | tf_op jit(solution)/shard_map/ppermute | solution.py:32
  51.8 16.9 %collective-permute-start.12 = (f32[100,2,640]{2,1,0:T(2,128)S(1)}, f32[100,2,640]{2,1,0:T(2,128)S(1)}, u32[]{:S(2)}, u32[]{:S(2)}) collective-permute-start(f32[100,2,640]{2,1,0:T(2,128)S(1)} %collective-permute-done.9.refs_7_), channel_id=1, source_target_pairs={{0,12},{1,5},{2,14},{3,7},{4,0},{5,9},{6,2},{7,11},{8,4},{9,13},{1... | collective-permute-start | bytes 1536008 | tf_op jit(solution)/shard_map/ppermute | solution.py:32
  56.7 12.0 %collective-permute-start.11 = (f32[100,2,640]{2,1,0:T(2,128)S(1)}, f32[100,2,640]{2,1,0:T(2,128)S(1)}, u32[]{:S(2)}, u32[]{:S(2)}) collective-permute-start(f32[100,2,640]{2,1,0:T(2,128)S(1)} %collective-permute-done.9.refs_7_), channel_id=1, source_target_pairs={{0,4},{1,13},{2,6},{3,15},{4,8},{5,1},{6,10},{7,3},{8,12},{9,5},{1... | collective-permute-start | bytes 1536008 | tf_op jit(solution)/shard_map/ppermute | solution.py:32
  68.7 4.2 %collective-permute-start.20 = (f32[100,2,640]{2,1,0:T(2,128)S(1)}, f32[100,2,640]{2,1,0:T(2,128)S(1)}, u32[]{:S(2)}, u32[]{:S(2)}) collective-permute-start(f32[100,2,640]{2,1,0:T(2,128)S(1)} %collective-permute-done.12.refs_1_), channel_id=1, source_target_pairs={{0,1},{1,0},{2,3},{3,2},{4,5},{5,4},{6,7},{7,6},{8,9},{9,8},{10,11... | collective-permute-start | bytes 1536008 | tf_op jit(solution)/shard_map/ppermute | solution.py:32
  71.3 8.8 %collective-permute-start.19 = (f32[200,2,640]{2,1,0:T(2,128)S(1)}, f32[200,2,640]{2,1,0:T(2,128)S(1)}, u32[]{:S(2)}, u32[]{:S(2)}) collective-permute-start(f32[200,2,640]{2,1,0:T(2,128)S(1)} %pad_maximum_fusion.1), channel_id=1, source_target_pairs={{0,1},{1,0},{2,3},{3,2},{4,5},{5,4},{6,7},{7,6},{8,9},{9,8},{10,11... | collective-permute-start | bytes 3072008 | tf_op jit(solution)/shard_map/ppermute | solution.py:32
  71.9 8.2 %collective-permute-start.18 = (f32[200,2,640]{2,1,0:T(2,128)S(1)}, f32[200,2,640]{2,1,0:T(2,128)S(1)}, u32[]{:S(2)}, u32[]{:S(2)}) collective-permute-start(f32[200,2,640]{2,1,0:T(2,128)S(1)} %pad_maximum_fusion), channel_id=1, source_target_pairs={{0,1},{1,0},{2,3},{3,2},{4,5},{5,4},{6,7},{7,6},{8,9},{9,8},{10,11... | collective-permute-start | bytes 3072008 | tf_op jit(solution)/shard_map/ppermute | solution.py:32
  72.4 7.6 %collective-permute-start.21 = (f32[100,2,640]{2,1,0:T(2,128)S(1)}, f32[100,2,640]{2,1,0:T(2,128)S(1)}, u32[]{:S(2)}, u32[]{:S(2)}) collective-permute-start(f32[100,2,640]{2,1,0:T(2,128)S(1)} %collective-permute-done.11.refs_0_), channel_id=1, source_target_pairs={{0,1},{1,0},{2,3},{3,2},{4,5},{5,4},{6,7},{7,6},{8,9},{9,8},{10,11... | collective-permute-start | bytes 1536008 | tf_op jit(solution)/shard_map/ppermute | solution.py:32
  72.5 7.5 %collective-permute-start.22 = (f32[100,2,640]{2,1,0:T(2,128)S(1)}, f32[100,2,640]{2,1,0:T(2,128)S(1)}, u32[]{:S(2)}, u32[]{:S(2)}) collective-permute-start(f32[100,2,640]{2,1,0:T(2,128)S(1)} %collective-permute-done.8.refs_2_), channel_id=1, source_target_pairs={{0,1},{1,0},{2,3},{3,2},{4,5},{5,4},{6,7},{7,6},{8,9},{9,8},{10,11... | collective-permute-start | bytes 1536008 | tf_op jit(solution)/shard_map/ppermute | solution.py:32
  72.9 7.1 %collective-permute-start.23 = (f32[100,2,640]{2,1,0:T(2,128)S(1)}, f32[100,2,640]{2,1,0:T(2,128)S(1)}, u32[]{:S(2)}, u32[]{:S(2)}) collective-permute-start(f32[100,2,640]{2,1,0:T(2,128)S(1)} %collective-permute-done.13.refs_3_), channel_id=1, source_target_pairs={{0,1},{1,0},{2,3},{3,2},{4,5},{5,4},{6,7},{7,6},{8,9},{9,8},{10,11... | collective-permute-start | bytes 1536008 | tf_op jit(solution)/shard_map/ppermute | solution.py:32

commit v5 on v4

--- a/solution.py
+++ b/solution.py
@@ -357,15 +357,15 @@
     jd = permute(far, left)
     e = permute(a, up)
 
-    ja, jc, jd = together(ja, jc, jd)
+    ja, jc, jd, beside, b = together(ja, jc, jd, beside, b)
     je = permute(ja, right)
     jf = permute(jd, left)
-    e, beside = together(e, beside)
+    panel, helds = prepare_call([block, far, ja, jb, jc, jd], [held, beside, a, b])
+    e, beside, panel, helds = together(e, beside, panel, helds)
     f = permute(e, beyond)
     c = permute(beside, up)
     d = permute(beside, down)
 
-    panel, helds = prepare_call([block, far, ja, jb, jc, jd], [held, beside, a, b])
     own, now, later = begin_call([je, jf], panel, helds)
     held, beside, a, b, e, c, d, f, own = together(held, beside, a, b, e, c, d, f, own)
     early = [swap(jnp.concatenate([held, beside], axis=0)), swap(jnp.concatenate([a, b], axis=0))]

time: 93.1 us -> 93 us (level)
  transfers between devices with their start and end apart: 24 -> 24, of which waited for: 8 -> 6; matrix products, arithmetic and copies ran while one was open for 1% -> 1% of each run, Pallas kernels for 18% -> 18%
where the time goes in v5:
time: 93 us; the launch traced here: 92.8 us
  starting transfers between devices  36.4 us (39%)
  Pallas kernels  29.1 us (31%)
  waiting for transfers between devices  24.7 us (27%)
  other arithmetic  2.17 us (2%)
    ppermute x24, starting transfers between devices, permute(): return lax.ppermute(value, AXES, pairs)  36.4 us
    pallas_call x4, Pallas kernels, call(): pl.pallas_call(kernel, out_shape=tuple(shapes), in_specs=kinds, out_specs...  29.1 us
    ppermute x24, waiting for transfers between devices, permute(): return lax.ppermute(value, AXES, pairs)  24.7 us
  transfers between devices with their start and end apart: 24, of which 6 were waited for; matrix products, arithmetic and copies ran while one was open for 1% of the time, Pallas kernels for 18%

profile of v5, /device:TPU:1, one launch (start us, length us, event | category | flops | bytes accessed | tf_op | source)
XLA Modules:
  0.0 92.8 jit_solution(13721860532023729953)
XLA Ops:
  0.0 1.3 %pad_maximum_fusion.2.refs_0_ = f32[100,2,640]{2,1,0:T(2,128)S(1)} fusion(f32[50,2,640]{2,1,0:T(2,128)} %bitcast.4, f32[50,2,640]{2,1,0:T(2,128)} %bitcast.6), kind=kLoop, calls=%fused_computation.2 | loop fusion | flops 128000 | bytes 1024000 | tf_op jit(solution)/shard_map/concatenate | solution.py:310
  1.3 1.6 %collective-permute-start = (f32[50,2,640]{2,1,0:T(2,128)}, f32[50,2,640]{2,1,0:T(2,128)S(1)}, u32[]{:S(2)}, u32[]{:S(2)}) collective-permute-start(f32[50,2,640]{2,1,0:T(2,128)} %bitcast.5), channel_id=1, source_target_pairs={{0,0},{1,1},{2,16},{3,17},{4,4},{5,5},{6,20},{7,21},{8,8},{9,9},{1... | collective-permute-start | bytes 768008 | tf_op jit(solution)/shard_map/ppermute | solution.py:32
  2.9 7.1 %collective-permute-start.1 = (f32[50,2,640]{2,1,0:T(2,128)}, f32[50,2,640]{2,1,0:T(2,128)S(1)}, u32[]{:S(2)}, u32[]{:S(2)}) collective-permute-start(f32[50,2,640]{2,1,0:T(2,128)} %bitcast.7), channel_id=1, source_target_pairs={{0,10},{1,11},{2,26},{3,27},{4,14},{5,15},{6,30},{7,31},{8,2},{9,3... | collective-permute-start | bytes 768008 | tf_op jit(solution)/shard_map/ppermute | solution.py:32
  10.0 0.0 collective-permute-start.6
  10.0 1.3 %collective-permute-start.5 = (f32[100,2,640]{2,1,0:T(2,128)S(1)}, f32[100,2,640]{2,1,0:T(2,128)S(1)}, u32[]{:S(2)}, u32[]{:S(2)}) collective-permute-start(f32[100,2,640]{2,1,0:T(2,128)S(1)} %pad_maximum_fusion.2.refs_0_), channel_id=1, source_target_pairs={{0,96},{1,33},{2,98},{3,35},{4,100},{5,37},{6,102},{7,39},{8,104},... | collective-permute-start | bytes 1536008 | tf_op jit(solution)/shard_map/ppermute | solution.py:32
  11.3 1.4 %collective-permute-start.4 = (f32[100,2,640]{2,1,0:T(2,128)S(1)}, f32[100,2,640]{2,1,0:T(2,128)S(1)}, u32[]{:S(2)}, u32[]{:S(2)}) collective-permute-start(f32[100,2,640]{2,1,0:T(2,128)S(1)} %pad_maximum_fusion.2.refs_0_), channel_id=1, source_target_pairs={{0,32},{1,97},{2,34},{3,99},{4,36},{5,101},{6,38},{7,103},{8,40},{... | collective-permute-start | bytes 1536008 | tf_op jit(solution)/shard_map/ppermute | solution.py:32
  12.7 0.0 collective-permute-done
  12.7 3.7 %collective-permute-done.1 = f32[50,2,640]{2,1,0:T(2,128)S(1)} collective-permute-done((f32[50,2,640]{2,1,0:T(2,128)}, f32[50,2,640]{2,1,0:T(2,128)S(1)}, u32[]{:S(2)}, u32[]{:S(2)}) %collective-permute-start.1) | collective-permute-done | bytes 256032 | tf_op jit(solution)/shard_map/ppermute | solution.py:32
  16.4 0.7 collective-permute-start.2
  17.0 4.1 %collective-permute-start.3 = (f32[50,2,640]{2,1,0:T(2,128)S(1)}, f32[50,2,640]{2,1,0:T(2,128)S(1)}, u32[]{:S(2)}, u32[]{:S(2)}) collective-permute-start(f32[50,2,640]{2,1,0:T(2,128)S(1)} %collective-permute-done.1), channel_id=1, source_target_pairs={{0,64},{1,65},{2,66},{3,67},{4,100},{5,101},{6,102},{7,103},{8,8},... | collective-permute-start | bytes 768008 | tf_op jit(solution)/shard_map/ppermute | solution.py:32
  21.2 0.0 collective-permute-done.2
  21.2 7.5 %collective-permute-done.3 = f32[50,2,640]{2,1,0:T(2,128)S(1)} collective-permute-done((f32[50,2,640]{2,1,0:T(2,128)S(1)}, f32[50,2,640]{2,1,0:T(2,128)S(1)}, u32[]{:S(2)}, u32[]{:S(2)}) %collective-permute-start.3) | collective-permute-done | bytes 256032 | tf_op jit(solution)/shard_map/ppermute | solution.py:32
  28.7 0.0 collective-permute-done.6.refs_1_
  28.7 0.0 collective-permute-done.5.refs_3_
  28.7 0.0 collective-permute-done.4.refs_2_
  28.7 0.1 constant_dynamic-update-slice_fusion.refs_6_
  28.8 3.8 %collective-permute-start.7 = (f32[100,2,640]{2,1,0:T(2,128)S(1)}, f32[100,2,640]{2,1,0:T(2,128)S(1)}, u32[]{:S(2)}, u32[]{:S(2)}) collective-permute-start(f32[100,2,640]{2,1,0:T(2,128)S(1)} %constant_dynamic-update-slice_fusion.refs_6_), channel_id=1, source_target_pairs={{0,4},{1,13},{2,6},{3,15},{4,8},{5,1},{6,10},{7,3},{8,12},{9,5},{1... | collective-permute-start | bytes 1536008 | tf_op jit(solution)/shard_map/ppermute | solution.py:32
  32.6 0.0 collective-permute-start.12
  32.6 1.5 %collective-permute-start.11 = (f32[100,2,640]{2,1,0:T(2,128)S(1)}, f32[100,2,640]{2,1,0:T(2,128)S(1)}, u32[]{:S(2)}, u32[]{:S(2)}) collective-permute-start(f32[100,2,640]{2,1,0:T(2,128)S(1)} %constant_dynamic-update-slice_fusion.refs_6_), channel_id=1, source_target_pairs={{0,2},{1,3},{2,0},{3,1},{4,6},{5,7},{6,4},{7,5},{8,10},{9,11},{10,... | collective-permute-start | bytes 1536008 | tf_op jit(solution)/shard_map/ppermute | solution.py:32
  34.1 0.0 collective-permute-start.10
  34.1 2.7 %collective-permute-start.9 = (f32[100,2,640]{2,1,0:T(2,128)S(1)}, f32[100,2,640]{2,1,0:T(2,128)S(1)}, u32[]{:S(2)}, u32[]{:S(2)}) collective-permute-start(f32[100,2,640]{2,1,0:T(2,128)S(1)} %collective-permute-done.6.refs_1_), channel_id=1, source_target_pairs={{0,32},{1,97},{2,34},{3,99},{4,36},{5,101},{6,38},{7,103},{8,40},{... | collective-permute-start | bytes 1536008 | tf_op jit(solution)/shard_map/ppermute | solution.py:32
  36.8 4.9 %collective-permute-done.7.refs_8_ = f32[100,2,640]{2,1,0:T(2,128)S(1)} collective-permute-done((f32[100,2,640]{2,1,0:T(2,128)S(1)}, f32[100,2,640]{2,1,0:T(2,128)S(1)}, u32[]{:S(2)}, u32[]{:S(2)}) %collective-permute-start.7) | collective-permute-done | bytes 512032 | tf_op jit(solution)/shard_map/ppermute | solution.py:32
  41.7 3.4 %collective-permute-start.8 = (f32[100,2,640]{2,1,0:T(2,128)S(1)}, f32[100,2,640]{2,1,0:T(2,128)S(1)}, u32[]{:S(2)}, u32[]{:S(2)}) collective-permute-start(f32[100,2,640]{2,1,0:T(2,128)S(1)} %collective-permute-done.7.refs_8_), channel_id=1, source_target_pairs={{0,4},{1,13},{2,6},{3,15},{4,8},{5,1},{6,10},{7,3},{8,12},{9,5},{1... | collective-permute-start | bytes 1536008 | tf_op jit(solution)/shard_map/ppermute | solution.py:32
  45.1 1.7 %collective-permute-done.12.refs_9_ = f32[100,2,640]{2,1,0:T(2,128)S(1)} collective-permute-done((f32[100,2,640]{2,1,0:T(2,128)S(1)}, f32[100,2,640]{2,1,0:T(2,128)S(1)}, u32[]{:S(2)}, u32[]{:S(2)}) %collective-permute-start.12) | collective-permute-done | bytes 512032 | tf_op jit(solution)/shard_map/ppermute | solution.py:32
  46.8 0.0 collective-permute-done.11.refs_7_
  46.9 0.0 collective-permute-done.10.refs_5_
  46.9 0.0 collective-permute-done.9.refs_4_
  46.9 2.7 %collective-permute-start.16 = (f32[100,2,640]{2,1,0:T(2,128)S(1)}, f32[100,2,640]{2,1,0:T(2,128)S(1)}, u32[]{:S(2)}, u32[]{:S(2)}) collective-permute-start(f32[100,2,640]{2,1,0:T(2,128)S(1)} %collective-permute-done.4.refs_2_), channel_id=1, source_target_pairs={{0,32},{1,97},{2,34},{3,99},{4,36},{5,101},{6,38},{7,103},{8,40},{... | collective-permute-start | bytes 1536008 | tf_op jit(solution)/shard_map/ppermute | solution.py:32
  49.6 0.0 collective-permute-start.17
  49.6 3.7 %shard_map.28 = (f32[5,800,2,128]{3,2,1,0:T(2,128)S(1)}, bf16[2,640,1280]{2,1,0:T(8,128)(2,1)S(1)}) custom-call(f32[100,2,640]{2,1,0:T(2,128)S(1)} %pad_maximum_fusion.2.refs_0_, f32[100,2,640]{2,1,0:T(2,128)S(1)} %collective-permute-done.6.refs_1_, f32[100,2,640]{2,1,0:T(2,128)S(1)} %collective-permute-done.4.refs_2_, ...), custom_call_target="tpu_custom_call" | custom-call | flops 1000000 | bytes 100000 | tf_op jit(solution)/shard_map/pallas_call | solution.py:264
  53.3 0.0 collective-permute-done.8.refs_2_
  53.3 0.4 collective-permute-start.15
  53.6 0.0 collective-permute-start.14
  53.7 3.7 %collective-permute-start.13 = (f32[100,2,640]{2,1,0:T(2,128)S(1)}, f32[100,2,640]{2,1,0:T(2,128)S(1)}, u32[]{:S(2)}, u32[]{:S(2)}) collective-permute-start(f32[100,2,640]{2,1,0:T(2,128)S(1)} %collective-permute-done.11.refs_7_), channel_id=1, source_target_pairs={{0,4},{1,13},{2,6},{3,15},{4,8},{5,1},{6,10},{7,3},{8,12},{9,5},{1... | collective-permute-start | bytes 1536008 | tf_op jit(solution)/shard_map/ppermute | solution.py:32
  57.3 0.5 collective-permute-done.16.je
  57.8 6.4 %collective-permute-done.17.jf = f32[100,2,640]{2,1,0:T(2,128)S(1)} collective-permute-done((f32[100,2,640]{2,1,0:T(2,128)S(1)}, f32[100,2,640]{2,1,0:T(2,128)S(1)}, u32[]{:S(2)}, u32[]{:S(2)}) %collective-permute-start.17) | collective-permute-done | bytes 512032 | tf_op jit(solution)/shard_map/ppermute | solution.py:32
  64.2 5.7 %shard_map.29 = (f32[2,640,1280]{2,1,0:T(8,128)S(1)}, bf16[1280,1280]{1,0:T(8,128)(2,1)S(1)}, bf16[1280,1280]{1,0:T(8,128)(2,1)S(1)}, f32[5,800,2,128]{3,2,1,0:T(2,128)S(1)}) custom-call(f32[100,2,640]{2,1,0:T(2,128)S(1)} %collective-permute-done.16.je, f32[100,2,640]{2,1,0:T(2,128)S(1)} %collective-permute-done.17.jf, ...), custom_call_target="tpu_custom_call", output_to_operand_aliasing={{3}: (2, {})} | custom-call | flops 1000000 | bytes 100000 | tf_op jit(solution)/shard_map/pallas_call | solution.py:264
  70.0 0.0 collective-permute-done.15.refs_3_
  70.0 0.0 collective-permute-done.14.refs_1_
  70.0 0.0 collective-permute-done.13.refs_0_
  70.0 0.8 collective-permute-start.20
  70.7 0.4 pad_maximum_fusion.1
  71.2 0.1 collective-permute-start.19
  71.3 0.4 pad_maximum_fusion
  71.7 0.6 collective-permute-start.18
  72.3 0.1 collective-permute-start.21
  72.4 0.4 collective-permute-start.22
  72.8 0.0 collective-permute-done.20.refs_2_
  72.8 0.1 collective-permute-start.23
  72.9 7.0 %shard_map.30.refs_8_ = f32[4,640,2,640]{3,2,1,0:T(2,128)} custom-call(f32[100,2,640]{2,1,0:T(2,128)S(1)} %collective-permute-done.13.refs_0_, f32[100,2,640]{2,1,0:T(2,128)S(1)} %collective-permute-done.14.refs_1_, f32[100,2,640]{2,1,0:T(2,128)S(1)} %collective-permute-done.8.refs_2_, f32[100,2,640]{2,1,0:T(2,128)S(1)} %collective-permute-done.15.refs_3_, ...), custom_call_target="tpu_custom_call" | custom-call | flops 1000000 | bytes 100000 | tf_op jit(solution)/shard_map/pallas_call | solution.py:264
  79.9 0.0 collective-permute-done.21.refs_3_
  79.9 0.0 collective-permute-done.22.refs_4_
  79.9 0.0 collective-permute-done.23.refs_5_
  80.0 0.0 collective-permute-done.19.refs_1_
  80.0 0.0 collective-permute-done.18.refs_0_
  80.0 12.6 %shard_map.31 = f32[4,640,2,640]{3,2,1,0:T(2,128)} custom-call(f32[200,2,640]{2,1,0:T(2,128)S(1)} %collective-permute-done.18.refs_0_, f32[200,2,640]{2,1,0:T(2,128)S(1)} %collective-permute-done.19.refs_1_, f32[100,2,640]{2,1,0:T(2,128)S(1)} %collective-permute-done.20.refs_2_, ...), custom_call_target="tpu_custom_call", output_to_operand_aliasing={{}: (8, {})} | custom-call | flops 1000000 | bytes 100000 | tf_op jit(solution)/shard_map/pallas_call | solution.py:264
  (1 shorter events, 0.0 us)
Async XLA Ops:
  1.3 11.4 %collective-permute-start = (f32[50,2,640]{2,1,0:T(2,128)}, f32[50,2,640]{2,1,0:T(2,128)S(1)}, u32[]{:S(2)}, u32[]{:S(2)}) collective-permute-start(f32[50,2,640]{2,1,0:T(2,128)} %bitcast.5), channel_id=1, source_target_pairs={{0,0},{1,1},{2,16},{3,17},{4,4},{5,5},{6,20},{7,21},{8,8},{9,9},{1... | collective-permute-start | bytes 768008 | tf_op jit(solution)/shard_map/ppermute | solution.py:32
  2.9 13.5 %collective-permute-start.1 = (f32[50,2,640]{2,1,0:T(2,128)}, f32[50,2,640]{2,1,0:T(2,128)S(1)}, u32[]{:S(2)}, u32[]{:S(2)}) collective-permute-start(f32[50,2,640]{2,1,0:T(2,128)} %bitcast.7), channel_id=1, source_target_pairs={{0,10},{1,11},{2,26},{3,27},{4,14},{5,15},{6,30},{7,31},{8,2},{9,3... | collective-permute-start | bytes 768008 | tf_op jit(solution)/shard_map/ppermute | solution.py:32
  10.0 18.7 %collective-permute-start.6 = (f32[100,2,640]{2,1,0:T(2,128)S(1)}, f32[100,2,640]{2,1,0:T(2,128)S(1)}, u32[]{:S(2)}, u32[]{:S(2)}) collective-permute-start(f32[100,2,640]{2,1,0:T(2,128)S(1)} %pad_maximum_fusion.2.refs_0_), channel_id=1, source_target_pairs={{0,16},{1,17},{2,18},{3,19},{4,20},{5,21},{6,22},{7,23},{8,24},{9,... | collective-permute-start | bytes 1536008 | tf_op jit(solution)/shard_map/ppermute | solution.py:32
  10.0 18.7 %collective-permute-start.5 = (f32[100,2,640]{2,1,0:T(2,128)S(1)}, f32[100,2,640]{2,1,0:T(2,128)S(1)}, u32[]{:S(2)}, u32[]{:S(2)}) collective-permute-start(f32[100,2,640]{2,1,0:T(2,128)S(1)} %pad_maximum_fusion.2.refs_0_), channel_id=1, source_target_pairs={{0,96},{1,33},{2,98},{3,35},{4,100},{5,37},{6,102},{7,39},{8,104},... | collective-permute-start | bytes 1536008 | tf_op jit(solution)/shard_map/ppermute | solution.py:32
  11.3 17.4 %collective-permute-start.4 = (f32[100,2,640]{2,1,0:T(2,128)S(1)}, f32[100,2,640]{2,1,0:T(2,128)S(1)}, u32[]{:S(2)}, u32[]{:S(2)}) collective-permute-start(f32[100,2,640]{2,1,0:T(2,128)S(1)} %pad_maximum_fusion.2.refs_0_), channel_id=1, source_target_pairs={{0,32},{1,97},{2,34},{3,99},{4,36},{5,101},{6,38},{7,103},{8,40},{... | collective-permute-start | bytes 1536008 | tf_op jit(solution)/shard_map/ppermute | solution.py:32
  16.4 4.8 %collective-permute-start.2 = (f32[50,2,640]{2,1,0:T(2,128)S(1)}, f32[50,2,640]{2,1,0:T(2,128)S(1)}, u32[]{:S(2)}, u32[]{:S(2)}) collective-permute-start(f32[50,2,640]{2,1,0:T(2,128)S(1)} %collective-permute-done), channel_id=1, source_target_pairs={{0,0},{1,1},{2,2},{3,3},{4,36},{5,37},{6,38},{7,39},{8,72},{9,73},... | collective-permute-start | bytes 768008 | tf_op jit(solution)/shard_map/ppermute | solution.py:32
  17.0 11.7 %collective-permute-start.3 = (f32[50,2,640]{2,1,0:T(2,128)S(1)}, f32[50,2,640]{2,1,0:T(2,128)S(1)}, u32[]{:S(2)}, u32[]{:S(2)}) collective-permute-start(f32[50,2,640]{2,1,0:T(2,128)S(1)} %collective-permute-done.1), channel_id=1, source_target_pairs={{0,64},{1,65},{2,66},{3,67},{4,100},{5,101},{6,102},{7,103},{8,8},... | collective-permute-start | bytes 768008 | tf_op jit(solution)/shard_map/ppermute | solution.py:32
  28.8 12.9 %collective-permute-start.7 = (f32[100,2,640]{2,1,0:T(2,128)S(1)}, f32[100,2,640]{2,1,0:T(2,128)S(1)}, u32[]{:S(2)}, u32[]{:S(2)}) collective-permute-start(f32[100,2,640]{2,1,0:T(2,128)S(1)} %constant_dynamic-update-slice_fusion.refs_6_), channel_id=1, source_target_pairs={{0,4},{1,13},{2,6},{3,15},{4,8},{5,1},{6,10},{7,3},{8,12},{9,5},{1... | collective-permute-start | bytes 1536008 | tf_op jit(solution)/shard_map/ppermute | solution.py:32
  32.6 14.2 %collective-permute-start.12 = (f32[100,2,640]{2,1,0:T(2,128)S(1)}, f32[100,2,640]{2,1,0:T(2,128)S(1)}, u32[]{:S(2)}, u32[]{:S(2)}) collective-permute-start(f32[100,2,640]{2,1,0:T(2,128)S(1)} %constant_dynamic-update-slice_fusion.refs_6_), channel_id=1, source_target_pairs={{0,12},{1,5},{2,14},{3,7},{4,0},{5,9},{6,2},{7,11},{8,4},{9,13},{1... | collective-permute-start | bytes 1536008 | tf_op jit(solution)/shard_map/ppermute | solution.py:32
  32.6 14.2 %collective-permute-start.11 = (f32[100,2,640]{2,1,0:T(2,128)S(1)}, f32[100,2,640]{2,1,0:T(2,128)S(1)}, u32[]{:S(2)}, u32[]{:S(2)}) collective-permute-start(f32[100,2,640]{2,1,0:T(2,128)S(1)} %constant_dynamic-update-slice_fusion.refs_6_), channel_id=1, source_target_pairs={{0,2},{1,3},{2,0},{3,1},{4,6},{5,7},{6,4},{7,5},{8,10},{9,11},{10,... | collective-permute-start | bytes 1536008 | tf_op jit(solution)/shard_map/ppermute | solution.py:32
  34.1 12.7 %collective-permute-start.10 = (f32[100,2,640]{2,1,0:T(2,128)S(1)}, f32[100,2,640]{2,1,0:T(2,128)S(1)}, u32[]{:S(2)}, u32[]{:S(2)}) collective-permute-start(f32[100,2,640]{2,1,0:T(2,128)S(1)} %collective-permute-done.6.refs_1_), channel_id=1, source_target_pairs={{0,96},{1,33},{2,98},{3,35},{4,100},{5,37},{6,102},{7,39},{8,104},... | collective-permute-start | bytes 1536008 | tf_op jit(solution)/shard_map/ppermute | solution.py:32
  34.1 12.7 %collective-permute-start.9 = (f32[100,2,640]{2,1,0:T(2,128)S(1)}, f32[100,2,640]{2,1,0:T(2,128)S(1)}, u32[]{:S(2)}, u32[]{:S(2)}) collective-permute-start(f32[100,2,640]{2,1,0:T(2,128)S(1)} %collective-permute-done.6.refs_1_), channel_id=1, source_target_pairs={{0,32},{1,97},{2,34},{3,99},{4,36},{5,101},{6,38},{7,103},{8,40},{... | collective-permute-start | bytes 1536008 | tf_op jit(solution)/shard_map/ppermute | solution.py:32
  41.7 11.6 %collective-permute-start.8 = (f32[100,2,640]{2,1,0:T(2,128)S(1)}, f32[100,2,640]{2,1,0:T(2,128)S(1)}, u32[]{:S(2)}, u32[]{:S(2)}) collective-permute-start(f32[100,2,640]{2,1,0:T(2,128)S(1)} %collective-permute-done.7.refs_8_), channel_id=1, source_target_pairs={{0,4},{1,13},{2,6},{3,15},{4,8},{5,1},{6,10},{7,3},{8,12},{9,5},{1... | collective-permute-start | bytes 1536008 | tf_op jit(solution)/shard_map/ppermute | solution.py:32
  46.9 10.9 %collective-permute-start.16 = (f32[100,2,640]{2,1,0:T(2,128)S(1)}, f32[100,2,640]{2,1,0:T(2,128)S(1)}, u32[]{:S(2)}, u32[]{:S(2)}) collective-permute-start(f32[100,2,640]{2,1,0:T(2,128)S(1)} %collective-permute-done.4.refs_2_), channel_id=1, source_target_pairs={{0,32},{1,97},{2,34},{3,99},{4,36},{5,101},{6,38},{7,103},{8,40},{... | collective-permute-start | bytes 1536008 | tf_op jit(solution)/shard_map/ppermute | solution.py:32
  49.6 14.6 %collective-permute-start.17 = (f32[100,2,640]{2,1,0:T(2,128)S(1)}, f32[100,2,640]{2,1,0:T(2,128)S(1)}, u32[]{:S(2)}, u32[]{:S(2)}) collective-permute-start(f32[100,2,640]{2,1,0:T(2,128)S(1)} %collective-permute-done.10.refs_5_), channel_id=1, source_target_pairs={{0,96},{1,33},{2,98},{3,35},{4,100},{5,37},{6,102},{7,39},{8,104},... | collective-permute-start | bytes 1536008 | tf_op jit(solution)/shard_map/ppermute | solution.py:32
  53.3 16.7 %collective-permute-start.15 = (f32[100,2,640]{2,1,0:T(2,128)S(1)}, f32[100,2,640]{2,1,0:T(2,128)S(1)}, u32[]{:S(2)}, u32[]{:S(2)}) collective-permute-start(f32[100,2,640]{2,1,0:T(2,128)S(1)} %collective-permute-done.8.refs_2_), channel_id=1, source_target_pairs={{0,2},{1,3},{2,0},{3,1},{4,6},{5,7},{6,4},{7,5},{8,10},{9,11},{10,... | collective-permute-start | bytes 1536008 | tf_op jit(solution)/shard_map/ppermute | solution.py:32
  53.6 16.3 %collective-permute-start.14 = (f32[100,2,640]{2,1,0:T(2,128)S(1)}, f32[100,2,640]{2,1,0:T(2,128)S(1)}, u32[]{:S(2)}, u32[]{:S(2)}) collective-permute-start(f32[100,2,640]{2,1,0:T(2,128)S(1)} %collective-permute-done.11.refs_7_), channel_id=1, source_target_pairs={{0,12},{1,5},{2,14},{3,7},{4,0},{5,9},{6,2},{7,11},{8,4},{9,13},{1... | collective-permute-start | bytes 1536008 | tf_op jit(solution)/shard_map/ppermute | solution.py:32
  53.7 16.3 %collective-permute-start.13 = (f32[100,2,640]{2,1,0:T(2,128)S(1)}, f32[100,2,640]{2,1,0:T(2,128)S(1)}, u32[]{:S(2)}, u32[]{:S(2)}) collective-permute-start(f32[100,2,640]{2,1,0:T(2,128)S(1)} %collective-permute-done.11.refs_7_), channel_id=1, source_target_pairs={{0,4},{1,13},{2,6},{3,15},{4,8},{5,1},{6,10},{7,3},{8,12},{9,5},{1... | collective-permute-start | bytes 1536008 | tf_op jit(solution)/shard_map/ppermute | solution.py:32
  70.0 2.8 %collective-permute-start.20 = (f32[100,2,640]{2,1,0:T(2,128)S(1)}, f32[100,2,640]{2,1,0:T(2,128)S(1)}, u32[]{:S(2)}, u32[]{:S(2)}) collective-permute-start(f32[100,2,640]{2,1,0:T(2,128)S(1)} %collective-permute-done.14.refs_1_), channel_id=1, source_target_pairs={{0,1},{1,0},{2,3},{3,2},{4,5},{5,4},{6,7},{7,6},{8,9},{9,8},{10,11... | collective-permute-start | bytes 1536008 | tf_op jit(solution)/shard_map/ppermute | solution.py:32
  71.2 8.8 %collective-permute-start.19 = (f32[200,2,640]{2,1,0:T(2,128)S(1)}, f32[200,2,640]{2,1,0:T(2,128)S(1)}, u32[]{:S(2)}, u32[]{:S(2)}) collective-permute-start(f32[200,2,640]{2,1,0:T(2,128)S(1)} %pad_maximum_fusion.1), channel_id=1, source_target_pairs={{0,1},{1,0},{2,3},{3,2},{4,5},{5,4},{6,7},{7,6},{8,9},{9,8},{10,11... | collective-permute-start | bytes 3072008 | tf_op jit(solution)/shard_map/ppermute | solution.py:32
  71.7 8.2 %collective-permute-start.18 = (f32[200,2,640]{2,1,0:T(2,128)S(1)}, f32[200,2,640]{2,1,0:T(2,128)S(1)}, u32[]{:S(2)}, u32[]{:S(2)}) collective-permute-start(f32[200,2,640]{2,1,0:T(2,128)S(1)} %pad_maximum_fusion), channel_id=1, source_target_pairs={{0,1},{1,0},{2,3},{3,2},{4,5},{5,4},{6,7},{7,6},{8,9},{9,8},{10,11... | collective-permute-start | bytes 3072008 | tf_op jit(solution)/shard_map/ppermute | solution.py:32
  72.3 7.6 %collective-permute-start.21 = (f32[100,2,640]{2,1,0:T(2,128)S(1)}, f32[100,2,640]{2,1,0:T(2,128)S(1)}, u32[]{:S(2)}, u32[]{:S(2)}) collective-permute-start(f32[100,2,640]{2,1,0:T(2,128)S(1)} %collective-permute-done.13.refs_0_), channel_id=1, source_target_pairs={{0,1},{1,0},{2,3},{3,2},{4,5},{5,4},{6,7},{7,6},{8,9},{9,8},{10,11... | collective-permute-start | bytes 1536008 | tf_op jit(solution)/shard_map/ppermute | solution.py:32
  72.4 7.5 %collective-permute-start.22 = (f32[100,2,640]{2,1,0:T(2,128)S(1)}, f32[100,2,640]{2,1,0:T(2,128)S(1)}, u32[]{:S(2)}, u32[]{:S(2)}) collective-permute-start(f32[100,2,640]{2,1,0:T(2,128)S(1)} %collective-permute-done.8.refs_2_), channel_id=1, source_target_pairs={{0,1},{1,0},{2,3},{3,2},{4,5},{5,4},{6,7},{7,6},{8,9},{9,8},{10,11... | collective-permute-start | bytes 1536008 | tf_op jit(solution)/shard_map/ppermute | solution.py:32
  72.8 7.1 %collective-permute-start.23 = (f32[100,2,640]{2,1,0:T(2,128)S(1)}, f32[100,2,640]{2,1,0:T(2,128)S(1)}, u32[]{:S(2)}, u32[]{:S(2)}) collective-permute-start(f32[100,2,640]{2,1,0:T(2,128)S(1)} %collective-permute-done.15.refs_3_), channel_id=1, source_target_pairs={{0,1},{1,0},{2,3},{3,2},{4,5},{5,4},{6,7},{7,6},{8,9},{9,8},{10,11... | collective-permute-start | bytes 1536008 | tf_op jit(solution)/shard_map/ppermute | solution.py:32
